TPU v7x, 32 devices: a whole 2x2x4 slice. The times are simulated.
32 devices in a mesh: rep: 4 (over z), fsdp: 8 (over y, x, core).
Axes of the slice: x: 2, y: 2, z: 4, core: 2. Of those that a mesh axis runs over, the one named last changes fastest.
Arguments:
- tokens: bfloat16 [256, 256, 512], P(('rep', 'fsdp')), may hold values from -11 to 11
- cotangent: bfloat16 [256, 256, 512], P(('rep', 'fsdp')), may hold values from -6 to 6
- slot_items: int32 [256], P(('rep', 'fsdp')), may hold values from 0 to 4
- filter_gain: bfloat16 [512], P('fsdp'), may hold values from 0.5 to 1.5
- filter_shift: bfloat16 [512], P('fsdp'), may hold values from -4 to 4
- inner_weight: bfloat16 [512, 128], P('fsdp'), may hold values from -0.5 to 0.5
- inner_bias: bfloat16 [1024], P('fsdp'), may hold values from -4 to 4
- outer_weight: bfloat16 [512, 128], P('fsdp'), may hold values from -0.75 to 0.75
- outer_bias: bfloat16 [1024], P('fsdp'), may hold values from -4 to 4
- feed_gain: bfloat16 [512], P('fsdp'), may hold values from 0.5 to 1.5
- feed_shift: bfloat16 [512], P('fsdp'), may hold values from -4 to 4
- expand_weight: bfloat16 [512, 2048], P('fsdp'), may hold values from -0.25 to 0.25
- expand_bias: bfloat16 [2048], P('fsdp'), may hold values from -4 to 4
- contract_weight: bfloat16 [2048, 512], P('fsdp'), may hold values from -0.25 to 0.25
- contract_bias: bfloat16 [512], P('fsdp'), may hold values from -4 to 4
Outputs:
- block_output: bfloat16 [256, 256, 512], P(('rep', 'fsdp'))
- input_grad: float32 [256, 256, 512], P(('rep', 'fsdp'))
- filter_gain_grad: float32 [512], P('fsdp')
- filter_shift_grad: float32 [512], P('fsdp')
- inner_weight_grad: float32 [512, 128], P('fsdp')
- inner_bias_grad: float32 [1024], P('fsdp')
- outer_weight_grad: float32 [512, 128], P('fsdp')
- outer_bias_grad: float32 [1024], P('fsdp')
- feed_gain_grad: float32 [512], P('fsdp')
- feed_shift_grad: float32 [512], P('fsdp')
- expand_weight_grad: float32 [512, 2048], P('fsdp')
- expand_bias_grad: float32 [2048], P('fsdp')
- contract_weight_grad: float32 [2048, 512], P('fsdp')
- contract_bias_grad: float32 [512], P('fsdp')
- statistics: float32 [5], replicated
Inputs may be any that keep to these rules, and one draw needn't show every extreme that they name: `slot_items`: 0: the slot holds one item of 16 x 16 patches; 1 to 4: it holds that many items of (8) x (8) patches in its first quadrants, and the rest is padding.
All inputs are finite; a program needn't handle non-finite values.
Results may differ from a plain program's by a relative error of at most 0.014.
The roundings to bfloat16 on the way count: a program that leaves them out, or rounds other values in their place, can miss the bound.
Values may be sent and summed in bfloat16 or wider, within the bound.
A program may use at most 192 MiB of HBM per device.

v0:
```python
import math

import jax
import jax.numpy as jnp
from jax import lax
from jax.sharding import PartitionSpec as P

BS = 64
NB = 8
SIDE = 16


EPSILON = 1e-05
SHRINK = 0.25
HIGHEST = lax.Precision.HIGHEST


def norm_rows(values, scale_gain, offset_shift):
    centre = values - jnp.mean(values, axis=-1, keepdims=True)
    spread = jnp.mean(centre * centre, axis=-1, keepdims=True)
    return centre * lax.rsqrt(spread + EPSILON) * scale_gain + offset_shift


def valid_rows(slot_kinds):
    position = jnp.arange(SIDE * SIDE)
    half_side = SIDE // 2
    quadrant = position // SIDE // half_side * 2 + position % SIDE // half_side
    chosen = (slot_kinds[:, None] == 0) | (quadrant[None, :] < slot_kinds[:, None])
    return jnp.where(chosen, 1.0, 0.0).astype(jnp.float32)


def patch_table(slot_kinds):
    half_side = SIDE // 2
    position = jnp.arange(SIDE * SIDE)
    grid_row = position // SIDE
    grid_col = position % SIDE
    whole_phase = (
        grid_row[:, None] * grid_row[None, :] + grid_col[:, None] * grid_col[None, :]
    ) % SIDE
    whole_angle = 2.0 * math.pi / SIDE * whole_phase.astype(jnp.float32)
    local_row = grid_row % half_side
    local_col = grid_col % half_side
    part_phase = (
        local_row[:, None] * local_row[None, :] + local_col[:, None] * local_col[None, :]
    ) % half_side
    part_angle = 2.0 * math.pi / half_side * part_phase.astype(jnp.float32)
    quadrant = grid_row // half_side * 2 + grid_col // half_side
    same_block = quadrant[:, None] == quadrant[None, :]
    part_cosine = jnp.where(same_block, jnp.cos(part_angle), 0.0) / half_side
    part_sine = jnp.where(same_block, jnp.sin(part_angle), 0.0) / half_side
    whole_table = jnp.concatenate([jnp.cos(whole_angle), -jnp.sin(whole_angle)], axis=0) / SIDE
    part_table = jnp.concatenate([part_cosine, -part_sine], axis=0)
    whole_slot = (slot_kinds == 0)[:, None, None]
    return jnp.where(whole_slot, whole_table[None], part_table[None])


def forward_transform(field, table):
    both = jnp.einsum("sap,spd->sad", table, field, precision=HIGHEST)
    patches = field.shape[1]
    return (both[:, :patches], both[:, patches:])


def inverse_transform(real_part, imag_part, table):
    joined = jnp.concatenate([real_part, imag_part], axis=1)
    return jnp.einsum("spa,spd->sad", table, joined, precision=HIGHEST)


def split_weight(weight):
    blocks = weight.reshape(NB, BS, 2, BS)
    return (blocks[:, :, 0, :], blocks[:, :, 1, :])


def split_offset(offset):
    blocks = offset.astype(jnp.float32).reshape(NB, 2, BS)
    return (blocks[:, 0, :], blocks[:, 1, :])


def block_product(left, right):
    return jnp.einsum("nkc,kco->nko", left, right, preferred_element_type=jnp.float32)


def block_mix(real_in, imag_in, weight_real, weight_imag):
    out_real = block_product(real_in, weight_real) - block_product(imag_in, weight_imag)
    out_imag = block_product(real_in, weight_imag) + block_product(imag_in, weight_real)
    return (out_real, out_imag)


def block_mix_back(real_in, imag_in, real_grad, imag_grad, weight_real, weight_imag):

    def input_side(grad_part, weight_part):
        return jnp.einsum(
            "nko,kco->nkc", grad_part, weight_part, preferred_element_type=jnp.float32
        )

    def weight_side(input_part, grad_part):
        return jnp.einsum("nkc,nko->kco", input_part, grad_part, preferred_element_type=jnp.float32)

    in_real = input_side(real_grad, weight_real) + input_side(imag_grad, weight_imag)
    in_imag = input_side(imag_grad, weight_real) - input_side(real_grad, weight_imag)
    grad_real = weight_side(real_in, real_grad) + weight_side(imag_in, imag_grad)
    grad_imag = weight_side(real_in, imag_grad) - weight_side(imag_in, real_grad)
    return (in_real, in_imag, grad_real, grad_imag)


def gelu_pair(real_part, imag_part):
    return (jax.nn.gelu(real_part, approximate=False), jax.nn.gelu(imag_part, approximate=False))


def shrink_pair(real_part, imag_part):
    return (
        real_part - SHRINK * jnp.tanh(real_part / SHRINK),
        imag_part - SHRINK * jnp.tanh(imag_part / SHRINK),
    )


def gelu_exact(values):
    return jax.nn.gelu(values, approximate=False)


def column_sums(values):
    return jnp.sum(values.astype(jnp.float32), axis=0)


def pair_offsets(real_grad, imag_grad):
    return jnp.stack([column_sums(real_grad), column_sums(imag_grad)], axis=1).reshape(2 * NB * BS)


def body(
    tokens,
    cotangent,
    slot_items,
    filter_gain,
    filter_shift,
    inner_weight,
    inner_bias,
    outer_weight,
    outer_bias,
    feed_gain,
    feed_shift,
    expand_weight,
    expand_bias,
    contract_weight,
    contract_bias,
):
    gathered = (
        lax.all_gather(filter_gain, "fsdp", axis=0, tiled=True),
        lax.all_gather(filter_shift, "fsdp", axis=0, tiled=True),
        lax.all_gather(inner_weight, "fsdp", axis=0, tiled=True),
        lax.all_gather(inner_bias, "fsdp", axis=0, tiled=True),
        lax.all_gather(outer_weight, "fsdp", axis=0, tiled=True),
        lax.all_gather(outer_bias, "fsdp", axis=0, tiled=True),
        lax.all_gather(feed_gain, "fsdp", axis=0, tiled=True),
        lax.all_gather(feed_shift, "fsdp", axis=0, tiled=True),
        lax.all_gather(expand_weight, "fsdp", axis=0, tiled=True),
        lax.all_gather(expand_bias, "fsdp", axis=0, tiled=True),
        lax.all_gather(contract_weight, "fsdp", axis=0, tiled=True),
        lax.all_gather(contract_bias, "fsdp", axis=0, tiled=True),
    )
    (
        gain_one,
        shift_one,
        inner_full,
        inner_off,
        outer_full,
        outer_off,
        gain_two,
        shift_two,
        expand_full,
        expand_off,
        contract_full,
        contract_off,
    ) = gathered
    width = NB * BS
    slot_total = tokens.shape[0]
    block_shape = (slot_total * SIDE * SIDE, NB, BS)
    flat_shape = (slot_total * SIDE * SIDE, width)
    tokens_in = tokens.astype(jnp.float32)
    normed, first_norm_back = jax.vjp(
        norm_rows, tokens_in, gain_one.astype(jnp.float32), shift_one.astype(jnp.float32)
    )
    table = patch_table(slot_items)
    spec_real, spec_imag = forward_transform(normed, table)
    spec_real_low = spec_real.reshape(block_shape).astype(jnp.bfloat16)
    spec_imag_low = spec_imag.reshape(block_shape).astype(jnp.bfloat16)
    inner_wr, inner_wi = split_weight(inner_full)
    inner_br, inner_bi = split_offset(inner_off)
    pre_real, pre_imag = block_mix(spec_real_low, spec_imag_low, inner_wr, inner_wi)
    (act_real, act_imag), inner_gelu_back = jax.vjp(
        gelu_pair, pre_real + inner_br, pre_imag + inner_bi
    )
    act_real_low = act_real.astype(jnp.bfloat16)
    act_imag_low = act_imag.astype(jnp.bfloat16)
    outer_wr, outer_wi = split_weight(outer_full)
    outer_br, outer_bi = split_offset(outer_off)
    post_real, post_imag = block_mix(act_real_low, act_imag_low, outer_wr, outer_wi)
    (shrunk_real, shrunk_imag), shrink_back = jax.vjp(
        shrink_pair, post_real + outer_br, post_imag + outer_bi
    )
    mixer_out = inverse_transform(
        shrunk_real.reshape(tokens_in.shape), shrunk_imag.reshape(tokens_in.shape), table
    )
    middle = tokens_in + mixer_out
    feed_norm, second_norm_back = jax.vjp(
        norm_rows, middle, gain_two.astype(jnp.float32), shift_two.astype(jnp.float32)
    )
    feed_low = feed_norm.reshape(flat_shape).astype(jnp.bfloat16)
    hidden_pre = jnp.dot(
        feed_low, expand_full, preferred_element_type=jnp.float32
    ) + expand_off.astype(jnp.float32)
    hidden_act, hidden_gelu_back = jax.vjp(gelu_exact, hidden_pre)
    hidden_low = hidden_act.astype(jnp.bfloat16)
    branch = jnp.dot(
        hidden_low, contract_full, preferred_element_type=jnp.float32
    ) + contract_off.astype(jnp.float32)
    branch = branch.reshape(tokens_in.shape)
    result = middle + branch
    inner_back_w, outer_back_w, expand_back_w, contract_back_w = (
        lax.all_gather(inner_weight, "fsdp", axis=0, tiled=True),
        lax.all_gather(outer_weight, "fsdp", axis=0, tiled=True),
        lax.all_gather(expand_weight, "fsdp", axis=0, tiled=True),
        lax.all_gather(contract_weight, "fsdp", axis=0, tiled=True),
    )
    mask = valid_rows(slot_items)
    masked_grad = cotangent.astype(jnp.float32) * mask[:, :, None]
    masked_flat = masked_grad.reshape(flat_shape)
    masked_low = masked_flat.astype(jnp.bfloat16)
    contract_weight_grad = lax.dot_general(
        hidden_low, masked_low, (((0,), (0,)), ((), ())), preferred_element_type=jnp.float32
    )
    contract_bias_grad = column_sums(masked_low)
    act_grad = lax.dot_general(
        masked_low, contract_back_w, (((1,), (1,)), ((), ())), preferred_element_type=jnp.float32
    )
    (hidden_grad,) = hidden_gelu_back(act_grad)
    hidden_grad_low = hidden_grad.astype(jnp.bfloat16)
    expand_weight_grad = lax.dot_general(
        feed_low, hidden_grad_low, (((0,), (0,)), ((), ())), preferred_element_type=jnp.float32
    )
    expand_bias_grad = column_sums(hidden_grad_low)
    feed_grad = lax.dot_general(
        hidden_grad_low, expand_back_w, (((1,), (1,)), ((), ())), preferred_element_type=jnp.float32
    )
    norm_two_grad, feed_gain_grad, feed_shift_grad = second_norm_back(
        feed_grad.reshape(tokens_in.shape)
    )
    middle_grad = masked_grad + norm_two_grad
    shrunk_grad_real, shrunk_grad_imag = forward_transform(middle_grad, table)
    outer_grad_real, outer_grad_imag = shrink_back(
        (shrunk_grad_real.reshape(block_shape), shrunk_grad_imag.reshape(block_shape))
    )
    outer_grad_real_low = outer_grad_real.astype(jnp.bfloat16)
    outer_grad_imag_low = outer_grad_imag.astype(jnp.bfloat16)
    outer_back_wr, outer_back_wi = split_weight(outer_back_w)
    act_grad_real, act_grad_imag, outer_dwr, outer_dwi = block_mix_back(
        act_real_low,
        act_imag_low,
        outer_grad_real_low,
        outer_grad_imag_low,
        outer_back_wr,
        outer_back_wi,
    )
    outer_weight_grad = jnp.stack([outer_dwr, outer_dwi], axis=2).reshape(width, 2 * BS)
    outer_bias_grad = pair_offsets(outer_grad_real_low, outer_grad_imag_low)
    inner_grad_real, inner_grad_imag = inner_gelu_back((act_grad_real, act_grad_imag))
    inner_grad_real_low = inner_grad_real.astype(jnp.bfloat16)
    inner_grad_imag_low = inner_grad_imag.astype(jnp.bfloat16)
    inner_back_wr, inner_back_wi = split_weight(inner_back_w)
    spec_grad_real, spec_grad_imag, inner_dwr, inner_dwi = block_mix_back(
        spec_real_low,
        spec_imag_low,
        inner_grad_real_low,
        inner_grad_imag_low,
        inner_back_wr,
        inner_back_wi,
    )
    inner_weight_grad = jnp.stack([inner_dwr, inner_dwi], axis=2).reshape(width, 2 * BS)
    inner_bias_grad = pair_offsets(inner_grad_real_low, inner_grad_imag_low)
    normed_grad = inverse_transform(
        spec_grad_real.reshape(tokens_in.shape), spec_grad_imag.reshape(tokens_in.shape), table
    )
    norm_one_grad, filter_gain_grad, filter_shift_grad = first_norm_back(normed_grad)
    input_grad = middle_grad + norm_one_grad
    (
        own_fg,
        own_fs,
        own_iw,
        own_ib,
        own_ow,
        own_ob,
        own_gg,
        own_gs,
        own_ew,
        own_eb,
        own_cw,
        own_cb,
    ) = (
        lax.psum_scatter(filter_gain_grad, "fsdp", scatter_dimension=0, tiled=True),
        lax.psum_scatter(filter_shift_grad, "fsdp", scatter_dimension=0, tiled=True),
        lax.psum_scatter(inner_weight_grad, "fsdp", scatter_dimension=0, tiled=True),
        lax.psum_scatter(inner_bias_grad, "fsdp", scatter_dimension=0, tiled=True),
        lax.psum_scatter(outer_weight_grad, "fsdp", scatter_dimension=0, tiled=True),
        lax.psum_scatter(outer_bias_grad, "fsdp", scatter_dimension=0, tiled=True),
        lax.psum_scatter(feed_gain_grad, "fsdp", scatter_dimension=0, tiled=True),
        lax.psum_scatter(feed_shift_grad, "fsdp", scatter_dimension=0, tiled=True),
        lax.psum_scatter(expand_weight_grad, "fsdp", scatter_dimension=0, tiled=True),
        lax.psum_scatter(expand_bias_grad, "fsdp", scatter_dimension=0, tiled=True),
        lax.psum_scatter(contract_weight_grad, "fsdp", scatter_dimension=0, tiled=True),
        lax.psum_scatter(contract_bias_grad, "fsdp", scatter_dimension=0, tiled=True),
    )
    shares = (
        lax.psum(own_fg.astype(jnp.bfloat16), "rep").astype(jnp.float32),
        lax.psum(own_fs.astype(jnp.bfloat16), "rep").astype(jnp.float32),
        lax.psum(own_iw.astype(jnp.bfloat16), "rep").astype(jnp.float32),
        lax.psum(own_ib.astype(jnp.bfloat16), "rep").astype(jnp.float32),
        lax.psum(own_ow.astype(jnp.bfloat16), "rep").astype(jnp.float32),
        lax.psum(own_ob.astype(jnp.bfloat16), "rep").astype(jnp.float32),
        lax.psum(own_gg.astype(jnp.bfloat16), "rep").astype(jnp.float32),
        lax.psum(own_gs.astype(jnp.bfloat16), "rep").astype(jnp.float32),
        lax.psum(own_ew.astype(jnp.bfloat16), "rep").astype(jnp.float32),
        lax.psum(own_eb.astype(jnp.bfloat16), "rep").astype(jnp.float32),
        lax.psum(own_cw.astype(jnp.bfloat16), "rep").astype(jnp.float32),
        lax.psum(own_cb.astype(jnp.bfloat16), "rep").astype(jnp.float32),
    )
    weighted = mask[:, :, None]

    def square_sum(values):
        return jnp.sum(values * values * weighted)

    local_sums = jnp.stack(
        [
            square_sum(tokens_in),
            square_sum(mixer_out),
            square_sum(middle),
            square_sum(branch),
            square_sum(result),
        ]
    )
    local_patches = jnp.sum(mask) * width
    total_sums, total_patches = lax.psum((local_sums, local_patches), ("rep", "fsdp"))
    statistics = jnp.sqrt(total_sums / total_patches)
    return (
        result.astype(jnp.bfloat16),
        input_grad,
        shares[0],
        shares[1],
        shares[2],
        shares[3],
        shares[4],
        shares[5],
        shares[6],
        shares[7],
        shares[8],
        shares[9],
        shares[10],
        shares[11],
        statistics,
    )


def solution(mesh):
    return jax.shard_map(
        body,
        mesh=mesh,
        in_specs=(
            P(("rep", "fsdp"), None, None),
            P(("rep", "fsdp"), None, None),
            P(("rep", "fsdp")),
            P("fsdp"),
            P("fsdp"),
            P("fsdp", None),
            P("fsdp"),
            P("fsdp", None),
            P("fsdp"),
            P("fsdp"),
            P("fsdp"),
            P("fsdp", None),
            P("fsdp"),
            P("fsdp", None),
            P("fsdp"),
        ),
        out_specs=(
            P(("rep", "fsdp"), None, None),
            P(("rep", "fsdp"), None, None),
            P("fsdp"),
            P("fsdp"),
            P("fsdp", None),
            P("fsdp"),
            P("fsdp", None),
            P("fsdp"),
            P("fsdp"),
            P("fsdp"),
            P("fsdp", None),
            P("fsdp"),
            P("fsdp", None),
            P("fsdp"),
            P(),
        ),
        check_vma=False,
    )
```

profile of v0, /device:TPU:0, one launch (start us, length us, event | category | flops | bytes accessed | tf_op | source)
XLA Modules:
  0.0 624.1 jit_solution(4934278995789588007)
XLA Ops:
  16.4 16.2 %all-reduce.15 = (bf16[512]{0:T(512)(128)(2,1)S(1)}, bf16[512]{0:T(512)(128)(2,1)S(1)}, bf16[512]{0:T(512)(128)(2,1)}, bf16[512]{0:T(512)(128)(2,1)}, bf16[512]{0:T(512)(128)(2,1)}) all-reduce(bf16[512]{0:T(512)(128)(2,1)S(1)} %dynamic-update-slice.1, bf16[512]{0:T(512)(128)(2,1)S(1)} %dynamic-update-slice, ...), channel_id=1, replica_groups=mesh['rep'=4,'fsdp'=8] {'fsdp'}, use_global_device_ids=true, to_apply=%add.1 | all-reduce | flops 2560 | bytes 10240
  40.9 9.3 %fusion.80 = bf16[8,512,512]{2,1,0:T(8,128)(2,1)S(1)} fusion(bf16[8,256,512]{2,1,0:T(8,128)(2,1)S(1)} %copy-done.4, f32[512]{0:T(512)S(1)} %convert_element_type.183, f32[512]{0:T(512)S(1)} %convert_element_type.182, f32[8,256]{1,0:T(8,128)S(1)} %fusion.142, f32[8,256]{1,0:T(8,128)S(1)} %get-tuple-element.145, f32[512,256]{0,1:T(8,128)S(1)} %pad_maximum_fusion, ...), kind=kOutput, calls=%fused_computation.144 | convolution fusion | flops 6450839552 | bytes 7360520 | tf_op jit(solution)/shard_map/sap,spd->sad/dot_general | solution.py:58
  57.8 8.6 %all_gather.42 = bf16[512,128]{1,0:T(8,128)(2,1)S(1)} all-gather(bf16[64,128]{1,0:T(8,128)(2,1)S(1)} %copy-done.65), channel_id=1, replica_groups=mesh['rep'=4,'fsdp'=8] {'fsdp'}, dimensions={0}, use_global_device_ids=true | all-gather | bytes 147456 | tf_op jit(solution)/shard_map/all_gather | solution.py:148
  78.5 8.8 %all-gather = bf16[8,1,128]{2,1,0:T(2,128)(2,1)S(1)} all-gather(bf16[1,1,128]{2,1,0:T(2,128)(2,1)} %bitcast.375), channel_id=1, replica_groups=mesh['rep'=4,'fsdp'=8] {'fsdp'}, dimensions={0}, use_global_device_ids=true | all-gather | bytes 2304 | tf_op jit(solution)/shard_map/all_gather | solution.py:149
  87.3 7.9 %all-gather.1 = bf16[8,1,128]{2,1,0:T(2,128)(2,1)S(1)} all-gather(bf16[1,1,128]{2,1,0:T(2,128)(2,1)} %bitcast.376), channel_id=1, replica_groups=mesh['rep'=4,'fsdp'=8] {'fsdp'}, dimensions={0}, use_global_device_ids=true | all-gather | bytes 2304 | tf_op jit(solution)/shard_map/all_gather | solution.py:151
  96.5 10.1 %all_gather.44 = bf16[512,128]{1,0:T(8,128)(2,1)} all-gather(bf16[64,128]{1,0:T(8,128)(2,1)} %param.22), channel_id=1, replica_groups=mesh['rep'=4,'fsdp'=8] {'fsdp'}, dimensions={0}, use_global_device_ids=true | all-gather | bytes 147456 | tf_op jit(solution)/shard_map/all_gather | solution.py:150
  117.9 13.2 %fusion.54 = (bf16[2048,8,64]{0,2,1:T(8,128)(2,1)S(1)}, f32[2048,8,64]{0,2,1:T(8,128)}, f32[8,2048,64]{1,2,0:T(8,128)}) fusion(f32[8,64]{1,0:T(8,128)} %bitcast.374, f32[8,2048,64]{1,2,0:T(8,128)} %fusion.139, bf16[2048,8,64]{0,2,1:T(8,128)(2,1)} %convert_element_type.185, bf16[8,64,1,64]{1,3,0,2:T(8,128)(2,1)S(1)} %copy-done.39), kind=kOutput, calls=%fused_computation.91 | convolution fusion | flops 204472320 | bytes 16844800 | tf_op jit(solution)/shard_map/nkc,kco->nko/dot_general | solution.py:79
  136.2 11.1 %fusion.52 = (bf16[2048,8,64]{0,2,1:T(8,128)(2,1)S(1)}, f32[2048,8,64]{0,2,1:T(8,128)}, f32[8,2048,64]{1,2,0:T(8,128)}) fusion(f32[8,64]{1,0:T(8,128)S(1)} %bitcast.373, f32[8,2048,64]{1,2,0:T(8,128)S(1)} %copy-done.32, bf16[2048,8,64]{0,2,1:T(8,128)(2,1)S(1)} %copy-done.23, bf16[8,64,1,64]{1,3,0,2:T(8,128)(2,1)S(1)} %copy.145), kind=kOutput, calls=%fused_computation.84 | convolution fusion | flops 204472320 | bytes 16844800 | tf_op jit(solution)/shard_map/nkc,kco->nko/dot_general | solution.py:79
  175.1 11.4 %fusion.153 = (f32[8,256]{1,0:T(8,128)S(1)}, f32[8,256,512]{2,1,0:T(8,128)S(1)}, f32[8,256,512]{2,1,0:T(8,128)}) fusion(bf16[8,256,512]{2,1,0:T(8,128)(2,1)S(1)} %copy-done.5, f32[8,256,512]{2,1,0:T(8,128)} %copy.104, f32[8,256,512]{2,1,0:T(8,128)} %copy.103, f32[512,256]{0,1:T(8,128)S(1)} %pad_maximum_fusion, f32[512,256]{0,1:T(8,128)S(1)} %maximum_multiply_fusion, ...), kind=kOutput, calls=%fused_computation.273 | convolution fusion | flops 6448740352 | bytes 19931144 | tf_op jit(solution)/shard_map/spa,spd->sad/dot_general | solution.py:65
  189.6 8.7 %all-gather.2 = bf16[8,1,256]{2,1,0:T(2,128)(2,1)S(1)} all-gather(bf16[1,1,256]{2,1,0:T(2,128)(2,1)S(1)} %reshape.488), channel_id=1, replica_groups=mesh['rep'=4,'fsdp'=8] {'fsdp'}, dimensions={0}, use_global_device_ids=true | all-gather | bytes 4608 | tf_op jit(solution)/shard_map/all_gather | solution.py:155
  207.8 42.2 %multiply_convert_fusion = (bf16[2048,2048]{1,0:T(8,128)(2,1)}, f32[2048,2048]{1,0:T(8,128)}, f32[2048,2048]{1,0:T(8,128)}) fusion(f32[2048]{0:T(1024)S(1)} %bitcast.369, bf16[2048,512]{1,0:T(8,128)(2,1)} %bitcast.361, bf16[512,2048]{1,0:T(8,128)(2,1)} %all-gather.6.cloned.1.call-done), kind=kOutput, calls=%fused_computation.4 | convolution fusion | flops 4571791360 | bytes 46145536 | tf_op jit(solution)/shard_map/dot_general | solution.py:207
  250.0 19.6 %convert_reduce_fusion = (f32[2048]{0:T(1024)S(1)}, bf16[2048,2048]{1,0:T(8,128)(2,1)}) fusion(f32[2048,2048]{1,0:T(8,128)} %get-tuple-element.91, bf16[2048,512]{1,0:T(8,128)(2,1)S(1)} %bitcast.359, bf16[2048,512]{1,0:T(8,128)(2,1)} %all-gather.8.cloned.1.call-done, f32[2048,2048]{1,0:T(8,128)} %get-tuple-element.127, f32[2048]{0:T(1024)S(1)} %bitcast.370), kind=kOutput, calls=%fused_computation.2 | convolution fusion | flops 4366268416 | bytes 46153728 | tf_op jit(solution)/shard_map/dot_general | solution.py:231
  269.6 10.6 %fusion.168 = f32[512,2048]{1,0:T(8,128)} fusion(bf16[2048,512]{1,0:T(8,128)(2,1)} %bitcast.362, bf16[2048,2048]{1,0:T(8,128)(2,1)} %get-tuple-element.136), kind=kOutput, calls=%fused_computation.286 | convolution fusion | flops 4294967296 | bytes 14680064 | tf_op jit(solution)/shard_map/dot_general | solution.py:236
  289.0 8.6 %multiply_reduce_fusion.1 = (f32[]{:T(128)}, f32[2048,512]{1,0:T(8,128)S(1)}) fusion(f32[2048]{0:T(1024)S(1)} %copy-done.71, f32[512]{0:T(512)S(1)} %copy-done.73, bf16[2048,2048]{1,0:T(8,128)(2,1)} %get-tuple-element.90, bf16[2048,512]{1,0:T(8,128)(2,1)S(1)} %copy-done.78), kind=kOutput, calls=%fused_computation.93 | convolution fusion | flops 4299161600 | bytes 14690308 | tf_op jit(solution)/shard_map/dot_general | solution.py:212
  308.1 11.5 %fusion.8 = f32[8,512,512]{2,1,0:T(8,128)S(1)} fusion(f32[8,256,512]{2,1,0:T(8,128)} %get-tuple-element.100, bf16[8,256,512]{2,1,0:T(8,128)(2,1)S(1)} %copy-done.22, f32[8,256]{1,0:T(8,128)S(1)} %negate_multiply_fusion.4, f32[8,256]{1,0:T(8,128)S(1)} %copy-done.46, f32[512,256]{0,1:T(8,128)S(1)} %copy-done.28, f32[512,256]{0,1:T(8,128)S(1)} %copy-done.30, ...), kind=kOutput, calls=%fused_computation.20 | convolution fusion | flops 6447693824 | bytes 15745032 | tf_op jit(solution)/shard_map/sap,spd->sad/dot_general | solution.py:58
  368.2 8.3 %convert_reduce_fusion.6 = (f32[8,64]{1,0:T(8,128)S(1)}, bf16[2048,8,64]{0,2,1:T(8,128)(2,1)S(1)}) fusion(f32[2048,8,64]{0,2,1:T(8,128)} %get-tuple-element.97, f32[8,2048,64]{1,2,0:T(8,128)} %get-tuple-element.120, f32[8,2048,64]{1,2,0:T(8,128)} %fusion.125, bf16[2048,8,64]{0,2,1:T(8,128)(2,1)} %copy-done.12, bf16[8,64,1,64]{1,3,0,2:T(8,128)(2,1)S(1)} %copy-done.43), kind=kOutput, calls=%fused_computation.101 | convolution fusion | flops 152043008 | bytes 16844800 | tf_op jit(solution)/shard_map/nko,kco->nkc/dot_general | solution.py:91
  405.3 13.6 %fusion.150 = (f32[512]{0:T(512)S(1)}, f32[8,256]{1,0:T(8,128)S(1)}, f32[]{:T(128)}, f32[]{:T(128)}, f32[8,256,512]{2,1,0:T(8,128)}) fusion(f32[512]{0:T(512)S(1)} %copy-done.62, f32[8,256]{1,0:T(8,128)S(1)} %copy-done.50, bf16[8,256,512]{2,1,0:T(8,128)(2,1)S(1)} %copy-done.6, f32[8,256]{1,0:T(8,128)S(1)} %copy-done.46, ...), kind=kOutput, calls=%fused_computation.272 | convolution fusion | flops 6458177024 | bytes 19951632 | tf_op jit(solution)/shard_map/spa,spd->sad/dot_general | solution.py:65
  422.8 39.4 %all-reduce.13 = (f32[5]{0:T(128)S(1)}, f32[]{:T(128)}) all-reduce(f32[5]{0:T(128)S(1)} %stack.71, f32[]{:T(128)S(6)} %mul.502), channel_id=1, replica_groups=mesh['rep'=4,'fsdp'=8] {'rep','fsdp'}, use_global_device_ids=true, to_apply=%region_47.48 | all-reduce | flops 6 | bytes 48 | tf_op jit(solution)/shard_map/psum | solution.py:339
  466.0 23.4 %all-reduce.14 = (bf16[512]{0:T(512)(128)(2,1)S(1)}, bf16[512]{0:T(512)(128)(2,1)S(1)}, bf16[1024]{0:T(1024)(128)(2,1)S(1)}, bf16[1024]{0:T(1024)(128)(2,1)S(1)}...) all-reduce(f32[512]{0:T(512)S(1)} %get-tuple-element.45, ...), channel_id=2, replica_groups=mesh['rep'=4,'fsdp'=8] {'fsdp'}, use_global_device_ids=true, to_apply=%region_9.10.clone | all-reduce | flops 6656 | bytes 39936
  511.0 7.2 %add_add_fusion.2 = f32[8,256,512]{2,1,0:T(8,128)} fusion(f32[8,256,512]{2,1,0:T(8,128)} %get-tuple-element.100, bf16[8,256,512]{2,1,0:T(8,128)(2,1)} %param.16, f32[8,256]{1,0:T(8,128)S(1)} %negate_multiply_fusion.3, f32[8,256]{1,0:T(8,128)S(1)} %negate_multiply_fusion.4, f32[8,256]{1,0:T(8,128)S(1)} %copy-done.46, ...), kind=kLoop, calls=%fused_computation.102 | loop fusion | flops 13631488 | bytes 16828416 | tf_op jit(solution)/shard_map/add | solution.py:282
  518.2 15.9 %reduce-scatter.15.cloned.1.call-done = f32[64,128]{1,0:T(8,128)} async-done(((f32[512,128]{1,0:T(8,128)}), f32[64,128]{1,0:T(8,128)}) %reduce-scatter.15.cloned.1.call-update) | async-done | bytes 32784
  535.0 36.5 %reduce-scatter.13.cloned.1.call-done = f32[64,128]{1,0:T(8,128)} async-done(((f32[512,128]{1,0:T(8,128)}), f32[64,128]{1,0:T(8,128)}) %reduce-scatter.13.cloned.1.call-update) | async-done | bytes 32784
  572.4 20.8 %all-reduce.16 = (bf16[64,128]{0,1:T(8,128)(2,1)S(1)}, bf16[64,128]{0,1:T(8,128)(2,1)S(1)}, bf16[64]{0:T(256)(128)(2,1)S(1)}, bf16[64]{0:T(256)(128)(2,1)S(1)}, ...) all-reduce(bf16[64,128]{0,1:T(8,128)(2,1)S(1)} %copy.133, ...), channel_id=1, replica_groups=mesh['rep'=4,'fsdp'=8] {'rep'}, use_global_device_ids=true, to_apply=%region_15.16 | all-reduce | flops 17216 | bytes 68864 | tf_op jit(solution)/shard_map/psum | solution.py:313
  598.8 14.4 %all-reduce.20.cloned.1.call-done = (bf16[64,2048]{1,0:T(8,128)(2,1)}, bf16[256,512]{1,0:T(8,128)(2,1)}) async-done(((bf16[64,2048]{1,0:T(8,128)(2,1)}, bf16[256,512]{1,0:T(8,128)(2,1)}), (bf16[64,2048]{1,0:T(8,128)(2,1)}, bf16[256,512]{1,0:T(8,128)(2,1)})) %all-reduce.20.cloned.1.call-update) | async-done | bytes 524304 | tf_op jit(solution)/shard_map/psum | solution.py:319
  (328 shorter events, 227.9 us)
Async XLA Ops:
  7.2 33.7 %copy-start.4 = (bf16[8,256,512]{2,1,0:T(8,128)(2,1)S(1)}, bf16[8,256,512]{2,1,0:T(8,128)(2,1)}, u32[]{:S(2)}) copy-start(bf16[8,256,512]{2,1,0:T(8,128)(2,1)} %param.15) | copy-start | bytes 6291460
  7.2 200.6 %all-gather.6.cloned.1.call-start = ((), (), s32[]{:S(2)}) async-start(), calls=%async_computation.4 | async-start | bytes 2359296 | tf_op jit(solution)/shard_map/all_gather | solution.py:154
  7.9 242.1 %all-gather.8.cloned.1.call-start = ((), (), s32[]{:S(2)}) async-start(), calls=%async_computation.5 | async-start | bytes 2359296 | tf_op jit(solution)/shard_map/all_gather | solution.py:156
  8.7 498.7 %reduce-scatter.9.cloned.1.call-start = ((), (), s32[]{:S(2)}) async-start(), calls=%async_computation.6 | async-start | bytes 4718592 | tf_op jit(solution)/shard_map/reduce_scatter | solution.py:305
  8.8 41.4 %copy-start.63 = (s32[256]{0:T(256)}, s32[256]{0:T(256)S(1)}, u32[]{:S(2)}) copy-start(s32[256]{0:T(256)S(1)} %fusion.147) | copy-start | bytes 3076
  9.4 40.8 %copy-start.67 = (pred[8]{0:T(512)(128)(4,1)}, pred[8]{0:T(512)(128)(4,1)S(1)}, u32[]{:S(2)}) copy-start(pred[8]{0:T(512)(128)(4,1)S(1)} %broadcast_compare_fusion.4) | copy-start | bytes 28
  35.9 164.4 %copy-start.45 = (f32[8,256]{1,0:T(8,128)}, f32[8,256]{1,0:T(8,128)S(1)}, u32[]{:S(2)}) copy-start(f32[8,256]{1,0:T(8,128)S(1)} %get-tuple-element.115) | copy-start | bytes 24580
  39.6 135.5 %copy-start.27 = (f32[512,256]{0,1:T(8,128)}, f32[512,256]{0,1:T(8,128)S(1)}, u32[]{:S(2)}) copy-start(f32[512,256]{0,1:T(8,128)S(1)} %pad_maximum_fusion) | copy-start | bytes 1572868
  40.8 134.3 %copy-start.29 = (f32[512,256]{0,1:T(8,128)}, f32[512,256]{0,1:T(8,128)S(1)}, u32[]{:S(2)}) copy-start(f32[512,256]{0,1:T(8,128)S(1)} %maximum_multiply_fusion) | copy-start | bytes 1572868
  57.8 54.9 %copy-start.2 = (bf16[2048,8,64]{0,2,1:T(8,128)(2,1)}, bf16[2048,8,64]{0,2,1:T(8,128)(2,1)S(1)}, u32[]{:S(2)}) copy-start(bf16[2048,8,64]{0,2,1:T(8,128)(2,1)S(1)} %convert_element_type.184) | copy-start | bytes 6291460
  68.9 65.8 %copy-start.35 = (bf16[8,64,1,64]{1,3,0,2:T(8,128)(2,1)}, bf16[8,64,1,64]{1,3,0,2:T(8,128)(2,1)S(1)}, u32[]{:S(2)}) copy-start(bf16[8,64,1,64]{1,3,0,2:T(8,128)(2,1)S(1)} %copy.145) | copy-start | bytes 196612
  110.0 50.2 %copy-start.33 = (bf16[8,64,1,64]{1,3,0,2:T(8,128)(2,1)}, bf16[8,64,1,64]{1,3,0,2:T(8,128)(2,1)S(1)}, u32[]{:S(2)}) copy-start(bf16[8,64,1,64]{1,3,0,2:T(8,128)(2,1)S(1)} %copy.144) | copy-start | bytes 196612
  189.5 17.7 %copy-start.57 = (f32[8,256]{1,0:T(8,128)}, f32[8,256]{1,0:T(8,128)S(1)}, u32[]{:S(2)}) copy-start(f32[8,256]{1,0:T(8,128)S(1)} %multiply_reduce_fusion.6) | copy-start | bytes 24580
  189.5 17.7 %copy-start.51 = (f32[8,256]{1,0:T(8,128)}, f32[8,256]{1,0:T(8,128)S(1)}, u32[]{:S(2)}) copy-start(f32[8,256]{1,0:T(8,128)S(1)} %fusion.143) | copy-start | bytes 24580
  207.8 42.2 %copy-start.37 = (bf16[8,256,512]{2,1,0:T(8,128)(2,1)S(1)}, bf16[8,256,512]{2,1,0:T(8,128)(2,1)}, u32[]{:S(2)}) copy-start(bf16[8,256,512]{2,1,0:T(8,128)(2,1)} %get-tuple-element.85) | copy-start | bytes 6291460
  280.2 228.9 %reduce-scatter.11.cloned.1.call-start = ((), (), s32[]{:S(2)}) async-start(), calls=%async_computation.7 | async-start | bytes 4718592 | tf_op jit(solution)/shard_map/reduce_scatter | solution.py:307
  350.7 25.8 %copy-start.10 = (bf16[2048,8,64]{0,2,1:T(8,128)(2,1)}, bf16[2048,8,64]{0,2,1:T(8,128)(2,1)S(1)}, u32[]{:S(2)}) copy-start(bf16[2048,8,64]{0,2,1:T(8,128)(2,1)S(1)} %get-tuple-element.87) | copy-start | bytes 6291460
  367.3 166.8 %reduce-scatter.15.cloned.1.call-start = ((), (), s32[]{:S(2)}) async-start(), calls=%async_computation.9 | async-start | bytes 294912
  405.2 57.1 %copy-start.56 = (f32[8,256]{1,0:T(8,128)S(1)}, f32[8,256]{1,0:T(8,128)}, u32[]{:S(2)}) copy-start(f32[8,256]{1,0:T(8,128)} %copy-done.55) | copy-start | bytes 24580
  405.3 57.1 %copy-start.54 = (f32[8,256]{1,0:T(8,128)S(1)}, f32[8,256]{1,0:T(8,128)}, u32[]{:S(2)}) copy-start(f32[8,256]{1,0:T(8,128)} %copy-done.53) | copy-start | bytes 24580
  418.8 47.1 %copy-start.70 = (f32[512]{0:T(512)S(1)}, f32[512]{0:T(512)}, u32[]{:S(2)}) copy-start(f32[512]{0:T(512)} %get-tuple-element.84) | copy-start | bytes 6148
  466.0 27.1 %copy-start.13 = (bf16[2048,8,64]{0,2,1:T(8,128)(2,1)S(1)}, bf16[2048,8,64]{0,2,1:T(8,128)(2,1)}, u32[]{:S(2)}) copy-start(bf16[2048,8,64]{0,2,1:T(8,128)(2,1)} %copy-done.12) | copy-start | bytes 6291460
  501.1 70.4 %reduce-scatter.13.cloned.1.call-start = ((), (), s32[]{:S(2)}) async-start(), calls=%async_computation.8 | async-start | bytes 294912
  506.1 107.0 %all-reduce.20.cloned.1.call-start = ((), (), s32[]{:S(2)}) async-start(), calls=%async_computation.10 | async-start | bytes 1048576 | tf_op jit(solution)/shard_map/psum | solution.py:319
  (67 other events, 436.3 us)
Sparse Core Ops, SparseCore 0:
  9.9 30.7 all-gather.5
  42.6 28.2 all-gather.7
  280.3 51.4 reduce-scatter.8
  367.5 51.4 reduce-scatter.10
  501.2 32.8 reduce-scatter.14
  537.9 33.5 reduce-scatter.12
  573.9 39.2 all-reduce.19
where the time goes:
time: 634 us; the launch traced here: 624 us
  matrix products  214 us (34%)
  blocking collectives  144 us (23%)
  local copies, waits for them, and re-layouts  120 us (19%)
  waiting for transfers between devices  68.3 us (11%)
  other arithmetic  58.6 us (9%)
  between operations  19.1 us (3%)
    unnamed x9, waiting for transfers between devices  53.9 us
    unnamed x206, local copies, waits for them, and re-layouts  46.4 us
    dot_general x1, matrix products, body(): jnp.dot(feed_low, expand_full, preferred_element_type=jnp.float32)  42.2 us
    dot_general x8, matrix products, block_product(): jnp.einsum('nkc,kco->nko', left, right, preferred_element_type=jnp.float32)  42 us
    unnamed x2, blocking collectives  39.6 us
    psum x1, blocking collectives, body(): lax.psum((local_sums, local_patches), ('rep', 'fsdp'))  39.4 us
    dot_general x2, matrix products, inverse_transform(): return jnp.einsum('spa,spd->sad', table, joined, precision=HIGHEST)  25 us
    slice x6, local copies, waits for them, and re-layouts, forward_transform(): return (both[:, :patches], both[:, patches:])  24.7 us
  transfers between devices with their start and end apart: 7, of which 3 were waited for; matrix products, arithmetic and copies ran while one was open for 55% of the time, Pallas kernels for 0%

commit v1 on v0

v1 whole, which is shorter than its diff:
```python
import functools
import math

import jax
import jax.numpy as jnp
import numpy as np
from jax import lax
from jax.experimental import pallas as pl
from jax.experimental.pallas import tpu as pltpu
from jax.sharding import PartitionSpec as P

BS = 64
NB = 8
SIDE = 16
PATCHES = SIDE * SIDE
WIDTH = NB * BS
HALF = PATCHES // 2
PAIRS = NB // 2
EPSILON = 1e-05
SHRINK = 0.25
F32 = jnp.float32
BF16 = jnp.bfloat16
NT = (((1,), (1,)), ((), ()))
TN = (((0,), (0,)), ((), ()))
TABLE_SCALE = 1.132805


def frequency_order(side):
    pairs, selfs = [], []
    for a in range(side):
        for b in range(side):
            other = ((-a) % side, (-b) % side)
            if other == (a, b):
                selfs.append((a, b))
            elif (a, b) < other:
                pairs.append((a, b))
    return pairs, selfs


def spectrum_table(side):
    tiles = SIDE // side
    pairs, selfs = frequency_order(side)
    row = np.arange(PATCHES) // SIDE
    col = np.arange(PATCHES) % SIDE
    top, bottom = [], []
    for kind in ("pair", "self"):
        for qr in range(tiles):
            for qc in range(tiles):
                inside = (row // side == qr) & (col // side == qc)
                listed = pairs if kind == "pair" else selfs
                for at, (a, b) in enumerate(listed):
                    angle = 2.0 * math.pi / side * ((a * row + b * col) % side)
                    if kind == "pair":
                        top.append(np.where(inside, np.cos(angle), 0.0) / side)
                        bottom.append(np.where(inside, -np.sin(angle), 0.0) / side)
    extra = []
    for at in range(len(selfs)):
        for qr in range(tiles):
            for qc in range(tiles):
                inside = (row // side == qr) & (col // side == qc)
                a, b = selfs[at]
                angle = 2.0 * math.pi / side * ((a * row + b * col) % side)
                extra.append(np.where(inside, np.cos(angle), 0.0) / side)
    half = len(extra) // 2
    return np.array(top + extra[:half] + bottom + extra[half:]), len(top), tiles * tiles


WHOLE_TABLE, WHOLE_PAIRS, WHOLE_ZEROS = spectrum_table(SIDE)
PART_TABLE, PART_PAIRS, PART_ZEROS = spectrum_table(SIDE // 2)
TABLES = np.concatenate([WHOLE_TABLE * TABLE_SCALE, PART_TABLE], axis=0)


def dot(a, b, dims=(((1,), (0,)), ((), ()))):
    return lax.dot_general(a, b, dims, preferred_element_type=F32)


def sum8(values):
    return jnp.sum(values.reshape(-1, 8, values.shape[-1]), axis=0)


def gelu_and_slope(v):
    phi = 0.5 * lax.erf(v * 0.7071067811865476) + 0.5
    bell = jnp.exp2(v * v * (-0.5 / math.log(2.0))) * (1.0 / math.sqrt(2.0 * math.pi))
    return v * phi, phi + v * bell


def row_stats(values):
    centre = values - jnp.mean(values, axis=-1, keepdims=True)
    scale = lax.rsqrt(jnp.mean(centre * centre, axis=-1, keepdims=True) + EPSILON)
    return centre * scale, scale


def slot_facts(kind):
    whole = kind == 0
    pairs = jnp.where(whole, WHOLE_PAIRS, PART_PAIRS)
    zeros = jnp.where(whole, WHOLE_ZEROS, PART_ZEROS)
    scale = jnp.where(whole, 1.0 / TABLE_SCALE, 1.0).astype(F32)
    return whole, pairs, zeros, scale


def table_of(R, kind):
    at = pl.multiple_of(jnp.minimum(kind, 1) * PATCHES, PATCHES)
    return R.table[pl.ds(at, PATCHES), :]


def spread(halves, pairs):
    top, bottom = halves[:HALF], halves[HALF:]
    is_pair = lax.broadcasted_iota(jnp.int32, top.shape, 0) < pairs
    imag = jnp.where(is_pair, bottom, 0.0)
    return top, imag, jnp.where(is_pair, top, bottom), -imag


def fold(block, pairs):
    ra, ia = block[:HALF, :128], block[:HALF, 128:]
    rb, ib = block[HALF:, :128], block[HALF:, 128:]
    is_pair = lax.broadcasted_iota(jnp.int32, ra.shape, 0) < pairs
    return ra + jnp.where(is_pair, rb, 0.0), jnp.where(is_pair, ia - ib, rb)


def complex_pairs(weight_ref, out_ref):
    low = lax.broadcasted_iota(jnp.int32, (BS, 128), 1) < BS
    for j in range(PAIRS):
        first = weight_ref[pl.ds(128 * j, BS), :].astype(F32)
        second = weight_ref[pl.ds(128 * j + BS, BS), :].astype(F32)
        real = jnp.concatenate([jnp.where(low, first, 0.0), jnp.where(low, 0.0, pltpu.roll(second, BS, 1))], axis=0)
        imag = jnp.concatenate([jnp.where(low, pltpu.roll(first, BS, 1), 0.0), jnp.where(low, 0.0, second)], axis=0)
        out_ref[pl.ds(256 * j, 256), :] = jnp.concatenate(
            [jnp.concatenate([real, imag], axis=1), jnp.concatenate([-imag, real], axis=1)], axis=0
        ).astype(BF16)


def pair_gradient(product):
    real = product[:128, :128] + product[128:, 128:]
    imag = product[:128, 128:] - product[128:, :128]
    low = lax.broadcasted_iota(jnp.int32, (BS, 128), 1) < BS
    first = jnp.where(low, real[:BS], pltpu.roll(imag[:BS], BS, 1))
    second = jnp.where(low, pltpu.roll(real[BS:], BS, 1), imag[BS:])
    return jnp.concatenate([first, second], axis=0)


def masked_squares(values, kind):
    squares = values * values
    parts = jnp.sum(squares.reshape(2, 8, 2, 8, squares.shape[-1]), axis=1)
    total = parts[0, 0]
    for q in range(1, 4):
        valid = jnp.where((kind == 0) | (q < kind), 1.0, 0.0).astype(F32)
        total = total + valid * parts[q // 2, q % 2]
    return total


def masked(values, kind):
    position = lax.broadcasted_iota(jnp.int32, values.shape, 0)
    quadrant = (position >> 7) * 2 + ((position >> 3) & 1)
    return jnp.where((kind == 0) | (quadrant < kind), values, 0.0)


def mixer_forward(R, slot):
    kind = R.items[slot]
    whole, pairs, zeros, scale = slot_facts(kind)
    rows = pl.ds(pl.multiple_of(slot * PATCHES, PATCHES), PATCHES)
    table = table_of(R, kind)
    x = R.tok[rows, :].astype(F32)
    xhat, _ = row_stats(x)
    R.stats[pl.ds(0, 8), :] += masked_squares(x, kind)
    spec = dot(table, xhat.astype(BF16)) * (R.vec[0:1, :] * scale)
    top = lax.broadcasted_iota(jnp.int32, (HALF, WIDTH), 0)
    at_zero = (top >= pairs) & (top < pairs + zeros)
    shift = R.vec[1:2, :] * jnp.where(whole, float(SIDE), float(SIDE // 2)).astype(F32)
    spec = jnp.concatenate([spec[:HALF] + jnp.where(at_zero, shift, 0.0), spec[HALF:]], axis=0)
    ra, ia, rb, ib = [part.astype(BF16) for part in spread(spec, pairs)]
    tops, bottoms = [], []
    for j in range(PAIRS):
        lanes = slice(256 * j, 256 * j + 256)
        cols = slice(128 * j, 128 * j + 128)
        low = jnp.concatenate(
            [
                jnp.concatenate([ra[:, cols], ia[:, cols]], axis=1),
                jnp.concatenate([rb[:, cols], ib[:, cols]], axis=1),
            ],
            axis=0,
        )
        R.spec[rows, lanes] = low
        pre = dot(low, R.win[pl.ds(256 * j, 256), :]) + jnp.concatenate([R.vec[2:3, cols], R.vec[3:4, cols]], axis=1)
        act, slope = gelu_and_slope(pre)
        act = act.astype(BF16)
        R.act[rows, lanes] = act
        R.slope[rows, lanes] = slope.astype(BF16)
        post = dot(act, R.wout[pl.ds(256 * j, 256), :]) + jnp.concatenate(
            [R.vec[4:5, cols], R.vec[5:6, cols]], axis=1
        )
        bent = jnp.tanh(post * (1.0 / SHRINK))
        R.bent[rows, lanes] = (bent * bent).astype(BF16)
        u, v = fold(post - SHRINK * bent, pairs)
        tops.append(u.astype(BF16))
        bottoms.append(v.astype(BF16))
    folded = jnp.concatenate([jnp.concatenate(tops, axis=1), jnp.concatenate(bottoms, axis=1)], axis=0)
    mixer_out = dot(table, folded, TN) * scale
    R.stats[pl.ds(8, 8), :] += masked_squares(mixer_out, kind)
    middle = x + mixer_out
    R.stats[pl.ds(16, 8), :] += masked_squares(middle, kind)
    R.mid[rows, :] = middle
    yhat, _ = row_stats(middle)
    R.feed[rows, :] = (yhat * R.vec[6:7, :] + R.vec[7:8, :]).astype(BF16)
    grad = masked(R.cot[rows, :].astype(F32), kind)
    R.sums[pl.ds(16, 8), :] += sum8(grad)
    R.msk[rows, :] = grad.astype(BF16)


def mlp_chunk(R, rows, cols, first):
    feed, grad = R.feed[rows, :], R.msk[rows, :]
    hidden, slope = gelu_and_slope(dot(feed, R.we[:, cols]) + R.be[0:1, cols])
    hidden = hidden.astype(BF16)
    R.hidden[rows, cols] = hidden
    back = (dot(grad, R.wc[cols, :], NT) * slope).astype(BF16)
    R.hgrad[rows, :] = back
    R.dbe[:, cols] += sum8(back.astype(F32))
    branch = dot(hidden, R.wc[cols, :])
    fgrad = dot(back, R.we[:, cols], NT)
    if first:
        R.br[rows, :] = branch
        R.fg[rows, :] = fgrad
    else:
        R.br[rows, :] += branch
        R.fg[rows, :] += fgrad


def mixer_backward_first(R, slot):
    kind = R.items[slot]
    whole, pairs, zeros, scale = slot_facts(kind)
    rows = pl.ds(pl.multiple_of(slot * PATCHES, PATCHES), PATCHES)
    table = table_of(R, kind)
    branch = R.br[rows, :] + R.vec[8:9, :]
    middle = R.mid[rows, :]
    result = middle + branch
    R.stats[pl.ds(24, 8), :] += masked_squares(branch, kind)
    R.stats[pl.ds(32, 8), :] += masked_squares(result, kind)
    R.out[rows, :] = result.astype(BF16)
    feed_grad = R.fg[rows, :]
    yhat, yscale = row_stats(middle)
    R.sums[pl.ds(0, 8), :] += sum8(feed_grad * yhat)
    R.sums[pl.ds(8, 8), :] += sum8(feed_grad)
    scaled = feed_grad * R.vec[6:7, :]
    inner = scaled - jnp.mean(scaled, axis=-1, keepdims=True) - yhat * jnp.mean(scaled * yhat, axis=-1, keepdims=True)
    mgrad = R.msk[rows, :].astype(F32) + inner * yscale
    R.mgrad[rows, :] = mgrad
    parts = spread(dot(table, mgrad.astype(BF16)) * scale, pairs)
    for j in range(PAIRS):
        lanes = slice(256 * j, 256 * j + 256)
        cols = slice(128 * j, 128 * j + 128)
        ra, ia, rb, ib = [part[:, cols] for part in parts]
        grad = jnp.concatenate([jnp.concatenate([ra, ia], axis=1), jnp.concatenate([rb, ib], axis=1)], axis=0)
        grad = (grad * R.bent[rows, lanes].astype(F32)).astype(BF16)
        R.ograd[rows, lanes] = grad
        R.dbias[pl.ds(0, 8), lanes] += sum8(grad.astype(F32))
        grad = dot(grad, R.wout[pl.ds(256 * j, 256), :], NT) * R.slope[rows, lanes].astype(F32)
        grad = grad.astype(BF16)
        R.igrad[rows, lanes] = grad
        R.dbias[pl.ds(8, 8), lanes] += sum8(grad.astype(F32))


def mixer_weight_gradients(R, put_inner, put_outer):
    for j in range(PAIRS):
        lanes = slice(256 * j, 256 * j + 256)
        put_outer(j, pair_gradient(dot(R.act[:, lanes], R.ograd[:, lanes], TN)))
        put_inner(j, pair_gradient(dot(R.spec[:, lanes], R.igrad[:, lanes], TN)))


def mixer_backward_second(R, slot, put):
    kind = R.items[slot]
    whole, pairs, zeros, scale = slot_facts(kind)
    rows = pl.ds(pl.multiple_of(slot * PATCHES, PATCHES), PATCHES)
    table = table_of(R, kind)
    tops, bottoms = [], []
    for j in range(PAIRS):
        lanes = slice(256 * j, 256 * j + 256)
        u, v = fold(dot(R.igrad[rows, lanes], R.win[pl.ds(256 * j, 256), :], NT), pairs)
        tops.append(u.astype(BF16))
        bottoms.append(v.astype(BF16))
    folded = jnp.concatenate([jnp.concatenate(tops, axis=1), jnp.concatenate(bottoms, axis=1)], axis=0)
    ngrad = dot(table, folded, TN) * scale
    xhat, xscale = row_stats(R.tok[rows, :].astype(F32))
    R.sums[pl.ds(24, 8), :] += sum8(ngrad * xhat)
    R.sums[pl.ds(32, 8), :] += sum8(ngrad)
    scaled = ngrad * R.vec[0:1, :]
    inner = scaled - jnp.mean(scaled, axis=-1, keepdims=True) - xhat * jnp.mean(scaled * xhat, axis=-1, keepdims=True)
    put(slot, rows, R.mgrad[rows, :] + inner * xscale)
class Refs:
    pass


VMEM = pl.BlockSpec(memory_space=pltpu.VMEM)
SMEM = pl.BlockSpec(memory_space=pltpu.SMEM)
ROOM = 62 * 2**20
CHUNK = 512


def named(names, refs):
    R = Refs()
    for name, ref in zip(names, refs):
        setattr(R, name, ref)
    return R


def plain_call(body, ins, outs, scratch, name):
    names = list(ins) + list(outs) + list(scratch)

    def kernel(*refs):
        body(named(names, refs))

    values = pl.pallas_call(
        kernel,
        out_shape=[jax.ShapeDtypeStruct(*spec) for spec in outs.values()],
        in_specs=[SMEM if key == "items" else VMEM for key in ins],
        out_specs=[VMEM for _ in outs],
        scratch_shapes=[pltpu.VMEM(*spec) for spec in scratch.values()],
        compiler_params=pltpu.CompilerParams(vmem_limit_bytes=ROOM),
        name=name,
    )(*ins.values())
    return dict(zip(outs, values))


def forward_body(R):
    complex_pairs(R.inner, R.win)
    complex_pairs(R.outer, R.wout)
    R.stats[...] = jnp.zeros_like(R.stats)
    R.sums[...] = jnp.zeros_like(R.sums)

    @pl.loop(0, R.tok.shape[0] // PATCHES)
    def _(slot):
        mixer_forward(R, slot)


def mlp_body(R):
    rows_all = R.feed.shape[0]
    hidden_all = R.we.shape[1]
    R.dbe[...] = jnp.zeros_like(R.dbe)
    for at in range(0, hidden_all, CHUNK):
        cols = slice(at, at + CHUNK)

        @pl.loop(0, rows_all // CHUNK)
        def _(i):
            mlp_chunk(R, pl.ds(pl.multiple_of(i * CHUNK, CHUNK), CHUNK), cols, at == 0)

        R.dwe[:, cols] = dot(R.feed[...], R.hgrad[...], TN).astype(BF16)

    @pl.loop(0, hidden_all // CHUNK)
    def _(i):
        cols = pl.ds(pl.multiple_of(i * CHUNK, CHUNK), CHUNK)
        R.dwc[:, cols] = dot(R.msk[...], R.hidden[:, cols], TN).astype(BF16)


def backward_body(R):
    R.stats[...] = jnp.zeros_like(R.stats)
    R.sums[...] = jnp.zeros_like(R.sums)
    R.dbias[...] = jnp.zeros_like(R.dbias)
    slots = R.tok.shape[0] // PATCHES

    @pl.loop(0, slots)
    def _(slot):
        mixer_backward_first(R, slot)

    def put_inner(j, value):
        R.dinner[pl.ds(128 * j, 128), :] = value

    def put_outer(j, value):
        R.douter[pl.ds(128 * j, 128), :] = value

    mixer_weight_gradients(R, put_inner, put_outer)

    def put(slot, rows, value):
        R.igrad_out[rows, :] = value

    @pl.loop(0, slots)
    def _(slot):
        mixer_backward_second(R, slot, put)


def pair_order(vector):
    parts = vector.reshape(NB, 2, BS)
    return parts[:, 0].reshape(1, WIDTH), parts[:, 1].reshape(1, WIDTH)


def body_by_collectives(
    tokens, cotangent, slot_items, filter_gain, filter_shift, inner_weight, inner_bias, outer_weight, outer_bias,
    feed_gain, feed_shift, expand_weight, expand_bias, contract_weight, contract_bias,
):
    def gather(x):
        return lax.all_gather(x, "fsdp", axis=0, tiled=True)

    vectors = (filter_gain, filter_shift, inner_bias, outer_bias, feed_gain, feed_shift, contract_bias, expand_bias)
    sizes = [v.shape[0] for v in vectors]
    packed = lax.all_gather(jnp.concatenate(vectors), "fsdp", axis=0)
    ends = np.cumsum([0] + sizes)
    g1, s1, bi, bo, g2, s2, bc, be = [packed[:, a:b].reshape(-1).astype(F32) for a, b in zip(ends, ends[1:])]
    vec = jnp.concatenate(
        [g1[None], s1[None], *pair_order(bi), *pair_order(bo), g2[None], s2[None], bc[None], jnp.zeros((7, WIDTH), F32)]
    )
    inner, outer, we, wc = gather(inner_weight), gather(outer_weight), gather(expand_weight), gather(contract_weight)
    n = tokens.shape[0] * PATCHES
    hidden = we.shape[1]
    tok, cot = tokens.reshape(n, WIDTH), cotangent.reshape(n, WIDTH)
    table = jnp.asarray(TABLES, BF16)
    wide = ((n, 2 * WIDTH), BF16)
    flat = ((n, WIDTH), BF16)
    full = ((n, WIDTH), F32)
    pairs = ((2 * WIDTH, 2 * 2 * BS), BF16)
    sums = ((40, WIDTH), F32)
    a = plain_call(
        forward_body,
        dict(items=slot_items, tok=tok, cot=cot, table=table, vec=vec, inner=inner, outer=outer),
        dict(spec=wide, act=wide, slope=wide, bent=wide, mid=full, feed=flat, msk=flat, win=pairs, wout=pairs, stats=sums, sums=sums),
        {},
        "mixer_forward",
    )
    b = plain_call(
        mlp_body,
        dict(feed=a["feed"], msk=a["msk"], we=we, wc=wc, be=be.reshape(1, hidden)),
        dict(br=full, fg=full, dwe=((WIDTH, hidden), BF16), dwc=((WIDTH, hidden), BF16), dbe=((8, hidden), F32)),
        dict(hidden=((n, hidden), BF16), hgrad=((n, CHUNK), BF16)),
        "mlp",
    )
    c = plain_call(
        backward_body,
        dict(
            items=slot_items, tok=tok, table=table, vec=vec, spec=a["spec"], act=a["act"], slope=a["slope"], bent=a["bent"],
            mid=a["mid"], msk=a["msk"], br=b["br"], fg=b["fg"], win=a["win"], wout=a["wout"],
        ),
        dict(
            out=flat, igrad_out=full, dinner=((WIDTH, 2 * BS), F32), douter=((WIDTH, 2 * BS), F32),
            dbias=((16, 2 * WIDTH), F32), sums=sums, stats=sums,
        ),
        dict(mgrad=full, ograd=wide, igrad=wide),
        "mixer_backward",
    )

    def scatter(x):
        return lax.psum_scatter(x, "fsdp", scatter_dimension=0, tiled=True)

    def rows_of(x, at):
        return jnp.sum(x[at : at + 8], axis=0)

    def bias_of(at):
        parts = rows_of(c["dbias"], at).reshape(PAIRS, 2, 2, BS)
        return jnp.swapaxes(parts, 1, 2).reshape(2 * WIDTH)

    sums_ = a["sums"] + c["sums"]
    stats_ = a["stats"] + c["stats"]
    small = [
        rows_of(sums_, 24), rows_of(sums_, 32), bias_of(8), bias_of(0), rows_of(sums_, 0), rows_of(sums_, 8),
        rows_of(sums_, 16), jnp.sum(b["dbe"], axis=0),
    ]
    fsdp = lax.axis_size("fsdp")
    small = jnp.concatenate([v.reshape(fsdp, -1) for v in small], axis=1)
    weights = jnp.concatenate([c["dinner"].reshape(fsdp, -1), c["douter"].reshape(fsdp, -1)], axis=1)
    weights = jnp.concatenate([weights, small], axis=1).astype(BF16)
    own_small = scatter(weights.reshape(-1))
    own_we = scatter(b["dwe"])
    own_wc = scatter(b["dwc"].T)
    own_small, own_we, own_wc = lax.psum((own_small, own_we, own_wc), "rep")
    own_small = own_small.astype(F32)
    cut = inner_weight.size
    own_iw, own_ow = own_small[:cut].reshape(inner_weight.shape), own_small[cut : 2 * cut].reshape(inner_weight.shape)
    own = [own_small[2 * cut + x : 2 * cut + y] for x, y in zip(ends, ends[1:])]
    kinds = slot_items[:, None]
    valid = jnp.where((kinds == 0) | (jnp.arange(4)[None] < kinds), 1.0, 0.0)
    local = jnp.concatenate([jnp.sum(stats_.reshape(5, -1), axis=1), jnp.sum(valid)[None] * (PATCHES // 4 * WIDTH)])
    total = lax.psum(local, ("rep", "fsdp"))
    statistics = jnp.sqrt(total[:5] / total[5])
    return (
        c["out"].reshape(tokens.shape), c["igrad_out"].reshape(tokens.shape), own[0], own[1], own_iw, own[2], own_ow, own[3],
        own[4], own[5], own_we.astype(F32), own[7], own_wc.astype(F32), own[6], statistics,
    )


def specs():
    items = P(("rep", "fsdp"))
    big = P(("rep", "fsdp"), None, None)
    one, two = P("fsdp"), P("fsdp", None)
    ins = (big, big, items, one, one, two, one, two, one, one, one, two, one, two, one)
    outs = (big, big, one, one, two, one, two, one, one, one, two, one, two, one, P())
    return ins, outs


def solution(mesh):
    ins, outs = specs()
    return jax.shard_map(body_by_collectives, mesh=mesh, in_specs=ins, out_specs=outs, check_vma=False)
```

time: 634 us -> 361 us (0.57); the launches traced: 624 us -> 360 us
  matrix products: 214 us -> 0 us
  local copies, waits for them, and re-layouts: 120 us -> 17.6 us
  Pallas kernels: 0 us -> 95.1 us
  other arithmetic: 58.6 us -> 7.73 us
  waiting for transfers between devices: 68.3 us -> 119 us
  blocking collectives: 144 us -> 105 us
    dot_general x34 -> x0, matrix products: 214 us -> none  [the longest x1 42.2 us: body(): jnp.dot(feed_low, expand_full, preferred_element_type=jnp.float32)]
    pallas_call x0 -> x3, Pallas kernels: none -> 95.1 us  [plain_call(): pl.pallas_call(kernel, out_shape=[jax.ShapeDtypeStruct(*spec) for spec in...]
    reduce_scatter x2, waiting for transfers between devices: 0.01 us -> 69.8 us  [scatter(): return lax.psum_scatter(x, 'fsdp', scatter_dimension=0, tiled=True)]
    unnamed x9 -> x7, waiting for transfers between devices: 53.9 us -> 10.5 us
    unnamed x206 -> x16, local copies, waits for them, and re-layouts: 46.4 us -> 4.93 us
    reshape x12 -> x11, local copies, waits for them, and re-layouts: 34.2 us -> 1.34 us  [the longest x1 0.63 us: body_by_collectives(): own_small[cut:2 * cut].reshape(inner_weight.shape)]
    slice x10 -> x6, local copies, waits for them, and re-layouts: 28.5 us -> 2.35 us  [the longest x3 1.75 us: body_by_collectives(): own = [own_small[2 * cut + x:2 * cut + y] for x, y in zip(ends, ends[1:])]]
    reduce_sum x10 -> x6, other arithmetic: 26.3 us -> 1.71 us  [the longest x2 0.84 us: rows_of(): return jnp.sum(x[at:at + 8], axis=0)]
  transfers between devices with their start and end apart: 7 -> 6, of which waited for: 3 -> 4; matrix products, arithmetic and copies ran while one was open for 55% -> 4% of each run, Pallas kernels for 0% -> 7%
where the time goes in v1:
time: 361 us; the launch traced here: 360 us
  waiting for transfers between devices  119 us (33%)
  blocking collectives  105 us (29%)
  Pallas kernels  95.1 us (26%)
  local copies, waits for them, and re-layouts  17.6 us (5%)
  between operations  16.2 us (4%)
  other arithmetic  7.73 us (2%)
    pallas_call x3, Pallas kernels, plain_call(): pl.pallas_call(kernel, out_shape=[jax.ShapeDtypeStruct(*spec) for spec in...  95.1 us
    reduce_scatter x2, waiting for transfers between devices, scatter(): return lax.psum_scatter(x, 'fsdp', scatter_dimension=0, tiled=True)  69.8 us
    psum x1, blocking collectives, body_by_collectives(): total = lax.psum(local, ('rep', 'fsdp'))  39.6 us
    psum x1, waiting for transfers between devices, body_by_collectives(): own_small, own_we, own_wc = lax.psum((own_small, own_we, own_wc), 'rep')  38.4 us
    unnamed x1, blocking collectives  25.8 us
    all_gather x2, blocking collectives, gather(): return lax.all_gather(x, 'fsdp', axis=0, tiled=True)  19.9 us
    psum x1, blocking collectives, body_by_collectives(): own_small, own_we, own_wc = lax.psum((own_small, own_we, own_wc), 'rep')  19.3 us
    unnamed x7, waiting for transfers between devices  10.5 us
  transfers between devices with their start and end apart: 6, of which 4 were waited for; matrix products, arithmetic and copies ran while one was open for 4% of the time, Pallas kernels for 7%

profile of v1, /device:TPU:0, one launch (start us, length us, event | category | flops | bytes accessed | tf_op | source)
XLA Modules:
  0.0 360.2 jit_solution(10942952751471686295)
XLA Ops:
  8.7 1.3 fusion.5
  10.7 5.4 %concatenate.13 = bf16[832]{0:T(1024)(128)(2,1)S(1)} concatenate(bf16[64]{0:T(256)(128)(2,1)} %param.19, bf16[64]{0:T(256)(128)(2,1)} %param.20, bf16[128]{0:T(256)(128)(2,1)} %param.22, bf16[128]{0:T(256)(128)(2,1)} %param.24, bf16[64]{0:T(256)(128)(2,1)} %param.25, bf16[64]{0:T(256)(128)(2,1)} %param.26, bf16[64]{0:T(256)(128)(2,1)} %param.30, bf16[256]{0:T(256)(128)(2,1)} %param.28), dimensions={0} | concatenate | bytes 3328 | tf_op jit(solution)/shard_map/concatenate | solution.py:392
  16.3 25.8 %all-reduce = bf16[6656]{0:T(1024)(128)(2,1)S(1)} all-reduce(bf16[6656]{0:T(1024)(128)(2,1)S(1)} %dynamic-update-slice), channel_id=2, replica_groups=mesh['rep'=4,'fsdp'=8] {'fsdp'}, use_global_device_ids=true, to_apply=%add | all-reduce | flops 6656 | bytes 26624
  43.9 1.3 concatenate.14.refs_4_.refs_3_
  45.2 10.0 %all_gather.20.refs_5_ = bf16[512,128]{1,0:T(8,128)(2,1)} all-gather(bf16[64,128]{1,0:T(8,128)(2,1)} %param.21), channel_id=1, replica_groups=mesh['rep'=4,'fsdp'=8] {'fsdp'}, dimensions={0}, use_global_device_ids=true | all-gather | bytes 147456 | tf_op jit(solution)/shard_map/all_gather | solution.py:388
  55.2 10.0 %all_gather.21.refs_6_ = bf16[512,128]{1,0:T(8,128)(2,1)} all-gather(bf16[64,128]{1,0:T(8,128)(2,1)} %param.23), channel_id=1, replica_groups=mesh['rep'=4,'fsdp'=8] {'fsdp'}, dimensions={0}, use_global_device_ids=true | all-gather | bytes 147456 | tf_op jit(solution)/shard_map/all_gather | solution.py:388
  65.1 24.9 %mixer_forward.1 = (bf16[2048,1024]{1,0:T(8,128)(2,1)}, bf16[2048,1024]{1,0:T(8,128)(2,1)}, bf16[2048,1024]{1,0:T(8,128)(2,1)}, bf16[2048,1024]{1,0:T(8,128)(2,1...) custom-call(s32[8]{0:T(128)} %refs_0_.3, ...), custom_call_target="tpu_custom_call" | custom-call | tf_op jit(solution)/shard_map/mixer_forward/pallas_call | solution.py:310
  90.1 39.9 %mlp.1 = (f32[2048,512]{1,0:T(8,128)}, f32[2048,512]{1,0:T(8,128)}, bf16[512,2048]{1,0:T(8,128)(2,1)}, bf16[512,2048]{1,0:T(8,128)(2,1)}, f32[8,2048]{1,0:T(8,128)}) custom-call(bf16[2048,512]{1,0:T(8,128)(2,1)} %get-tuple-element.44.refs_0_, bf16[2048,512]{1,0:T(8,128)(2,1)} %get-tuple-element.43.refs_1_.refs_9_, ...), custom_call_target="tpu_custom_call" | custom-call | tf_op jit(solution)/shard_map/mlp/pallas_call | solution.py:310
  129.9 30.3 %mixer_backward.1 = (bf16[2048,512]{1,0:T(8,128)(2,1)}, f32[2048,512]{1,0:T(8,128)}, f32[512,128]{1,0:T(8,128)}, f32[512,128]{1,0:T(8,128)}, f32[16,1024]{1,0:T(...) custom-call(s32[8]{0:T(128)} %refs_0_.3, bf16[2048,512]{1,0:T(8,128)(2,1)} %bitcast.32, ...), custom_call_target="tpu_custom_call" | custom-call | tf_op jit(solution)/shard_map/mixer_backward/pallas_call | solution.py:310
  160.3 0.9 add.20
  161.6 1.0 convert.52
  162.7 1.0 convert.53
  163.7 0.8 slice_reduce_fusion
  165.0 1.0 convert_element_type.122
  169.6 39.6 %psum.31 = f32[6]{0:T(128)S(1)} all-reduce(f32[6]{0:T(128)S(1)} %pad_maximum_fusion), channel_id=1, replica_groups=mesh['rep'=4,'fsdp'=8] {'rep','fsdp'}, use_global_device_ids=true, to_apply=%region_17.18 | all-reduce | flops 6 | bytes 48 | tf_op jit(solution)/shard_map/psum | solution.py:467
  209.8 1.2 divide_sqrt_fusion
  210.9 8.0 %all-reduce.6.cloned.1.call-done = bf16[137728]{0:T(1024)(128)(2,1)} async-done(((bf16[137728]{0:T(1024)(128)(2,1)}), bf16[137728]{0:T(1024)(128)(2,1)}) %all-reduce.6.cloned.1.call-update) | async-done | bytes 275472
  219.0 0.9 dynamic-slice.2
  219.8 19.3 %psum.28 = bf16[17216]{0:T(1024)(128)(2,1)S(1)} all-reduce(bf16[17216]{0:T(1024)(128)(2,1)S(1)} %dynamic-slice.2), channel_id=1, replica_groups=mesh['rep'=4,'fsdp'=8] {'rep'}, use_global_device_ids=true, to_apply=%region_9.0 | all-reduce | flops 17216 | bytes 68864 | tf_op jit(solution)/shard_map/psum | solution.py:459
  239.2 25.0 %reduce-scatter.3.cloned.1.call-done = bf16[64,2048]{1,0:T(8,128)(2,1)} async-done(((bf16[512,2048]{1,0:T(8,128)(2,1)}), bf16[64,2048]{1,0:T(8,128)(2,1)}) %reduce-scatter.3.cloned.1.call-update) | async-done | bytes 262160 | tf_op jit(solution)/shard_map/reduce_scatter | solution.py:437
  264.2 44.7 %reduce-scatter.5.cloned.1.call-done = bf16[256,512]{0,1:T(8,128)(2,1)} async-done(((bf16[2048,512]{0,1:T(8,128)(2,1)}), bf16[256,512]{0,1:T(8,128)(2,1)}) %reduce-scatter.5.cloned.1.call-update) | async-done | bytes 262160 | tf_op jit(solution)/shard_map/reduce_scatter | solution.py:437
  311.3 38.4 %all-reduce.8.cloned.1.call-done = (bf16[256,512]{0,1:T(8,128)(2,1)}, bf16[64,2048]{1,0:T(8,128)(2,1)}) async-done(((bf16[256,512]{0,1:T(8,128)(2,1)}, bf16[64,2048]{1,0:T(8,128)(2,1)}), (bf16[256,512]{0,1:T(8,128)(2,1)}, bf16[64,2048]{1,0:T(8,128)(2,1)})) %all-reduce.8.cloned.1.call-update) | async-done | bytes 524304 | tf_op jit(solution)/shard_map/psum | solution.py:459
  349.7 1.8 convert_element_type.124
  351.5 1.9 copy.61
  (74 shorter events, 9.7 us)
Async XLA Ops:
  7.2 82.8 %all-gather.4.cloned.1.call-start = ((), (), s32[]{:S(2)}) async-start(), calls=%async_computation.2 | async-start | bytes 2359296 | tf_op jit(solution)/shard_map/all_gather | solution.py:388
  7.9 82.1 %all-gather.6.cloned.1.call-start = ((), (), s32[]{:S(2)}) async-start(), calls=%async_computation.3 | async-start | bytes 2359296 | tf_op jit(solution)/shard_map/all_gather | solution.py:388
  8.7 210.3 %all-reduce.6.cloned.1.call-start = ((), (), s32[]{:S(2)}) async-start(), calls=%async_computation.6 | async-start | bytes 552960
  129.9 30.3 %copy-start.2 = (f32[40,512]{1,0:T(8,128)S(1)}, f32[40,512]{1,0:T(8,128)}, u32[]{:S(2)}) copy-start(f32[40,512]{1,0:T(8,128)} %get-tuple-element.53) | copy-start | bytes 245764
  129.9 34.9 %copy-start.3 = (f32[8,2048]{1,0:T(8,128)S(1)}, f32[8,2048]{1,0:T(8,128)}, u32[]{:S(2)}) copy-start(f32[8,2048]{1,0:T(8,128)} %get-tuple-element.56) | copy-start | bytes 196612
  166.0 98.2 %reduce-scatter.3.cloned.1.call-start = ((), (), s32[]{:S(2)}) async-start(), calls=%async_computation.4 | async-start | bytes 2359296 | tf_op jit(solution)/shard_map/reduce_scatter | solution.py:437
  166.1 1.2 copy-start.4
  166.1 2.4 copy-start
  166.1 2.4 copy-start.1
  166.6 142.3 %reduce-scatter.5.cloned.1.call-start = ((), (), s32[]{:S(2)}) async-start(), calls=%async_computation.5 | async-start | bytes 2359296 | tf_op jit(solution)/shard_map/reduce_scatter | solution.py:437
  167.2 182.5 %all-reduce.8.cloned.1.call-start = ((), (), s32[]{:S(2)}) async-start(), calls=%async_computation.7 | async-start | bytes 1048576 | tf_op jit(solution)/shard_map/psum | solution.py:459
Sparse Core Ops, SparseCore 0:
  9.9 30.7 all-gather.3
  42.6 28.2 all-gather.5
  166.2 52.7 all-reduce.5
  222.1 42.0 reduce-scatter.2
  267.7 41.2 reduce-scatter.4
  311.2 38.4 all-reduce.7

commit v2 on v1

--- a/solution.py
+++ b/solution.py
@@ -16,6 +16,7 @@
 WIDTH = NB * BS
 HALF = PATCHES // 2
 PAIRS = NB // 2
+CHUNK = 512
 EPSILON = 1e-05
 SHRINK = 0.25
 F32 = jnp.float32
@@ -90,22 +91,26 @@
     return centre * scale, scale
 
 
+def kind_of(R, slot, lanes=WIDTH):
+    return jnp.full((1, lanes), R.items[slot], jnp.int32)
+
+
 def slot_facts(kind):
     whole = kind == 0
     pairs = jnp.where(whole, WHOLE_PAIRS, PART_PAIRS)
-    zeros = jnp.where(whole, WHOLE_ZEROS, PART_ZEROS)
     scale = jnp.where(whole, 1.0 / TABLE_SCALE, 1.0).astype(F32)
-    return whole, pairs, zeros, scale
+    return whole, pairs, scale
 
 
 def table_of(R, kind):
-    at = pl.multiple_of(jnp.minimum(kind, 1) * PATCHES, PATCHES)
-    return R.table[pl.ds(at, PATCHES), :]
+    whole = jnp.where(kind[:, :PATCHES] == 0, 1.0, 0.0).astype(F32)
+    first, second = whole.astype(BF16), (1.0 - whole).astype(BF16)
+    return R.table[pl.ds(0, PATCHES), :] * first + R.table[pl.ds(PATCHES, PATCHES), :] * second
 
 
 def spread(halves, pairs):
     top, bottom = halves[:HALF], halves[HALF:]
-    is_pair = lax.broadcasted_iota(jnp.int32, top.shape, 0) < pairs
+    is_pair = lax.broadcasted_iota(jnp.int32, top.shape, 0) < pairs[:, : top.shape[1]]
     imag = jnp.where(is_pair, bottom, 0.0)
     return top, imag, jnp.where(is_pair, top, bottom), -imag
 
@@ -113,15 +118,14 @@
 def fold(block, pairs):
     ra, ia = block[:HALF, :128], block[:HALF, 128:]
     rb, ib = block[HALF:, :128], block[HALF:, 128:]
-    is_pair = lax.broadcasted_iota(jnp.int32, ra.shape, 0) < pairs
+    is_pair = lax.broadcasted_iota(jnp.int32, ra.shape, 0) < pairs[:, : ra.shape[1]]
     return ra + jnp.where(is_pair, rb, 0.0), jnp.where(is_pair, ia - ib, rb)
 
 
 def complex_pairs(weight_ref, out_ref):
     low = lax.broadcasted_iota(jnp.int32, (BS, 128), 1) < BS
     for j in range(PAIRS):
-        first = weight_ref[pl.ds(128 * j, BS), :].astype(F32)
-        second = weight_ref[pl.ds(128 * j + BS, BS), :].astype(F32)
+        first, second = weight_ref[2 * j].astype(F32), weight_ref[2 * j + 1].astype(F32)
         real = jnp.concatenate([jnp.where(low, first, 0.0), jnp.where(low, 0.0, pltpu.roll(second, BS, 1))], axis=0)
         imag = jnp.concatenate([jnp.where(low, pltpu.roll(first, BS, 1), 0.0), jnp.where(low, 0.0, second)], axis=0)
         out_ref[pl.ds(256 * j, 256), :] = jnp.concatenate(
@@ -155,8 +159,8 @@
 
 
 def mixer_forward(R, slot):
-    kind = R.items[slot]
-    whole, pairs, zeros, scale = slot_facts(kind)
+    kind = kind_of(R, slot)
+    whole, pairs, scale = slot_facts(kind)
     rows = pl.ds(pl.multiple_of(slot * PATCHES, PATCHES), PATCHES)
     table = table_of(R, kind)
     x = R.tok[rows, :].astype(F32)
@@ -164,7 +168,7 @@
     R.stats[pl.ds(0, 8), :] += masked_squares(x, kind)
     spec = dot(table, xhat.astype(BF16)) * (R.vec[0:1, :] * scale)
     top = lax.broadcasted_iota(jnp.int32, (HALF, WIDTH), 0)
-    at_zero = (top >= pairs) & (top < pairs + zeros)
+    at_zero = (top >= pairs) & (top < pairs + jnp.where(whole, WHOLE_ZEROS, PART_ZEROS))
     shift = R.vec[1:2, :] * jnp.where(whole, float(SIDE), float(SIDE // 2)).astype(F32)
     spec = jnp.concatenate([spec[:HALF] + jnp.where(at_zero, shift, 0.0), spec[HALF:]], axis=0)
     ra, ia, rb, ib = [part.astype(BF16) for part in spread(spec, pairs)]
@@ -206,13 +210,14 @@
     R.msk[rows, :] = grad.astype(BF16)
 
 
-def mlp_chunk(R, rows, cols, first):
+def mlp_chunk(R, i, cols, first):
+    rows = pl.ds(pl.multiple_of(i * CHUNK, CHUNK), CHUNK)
     feed, grad = R.feed[rows, :], R.msk[rows, :]
     hidden, slope = gelu_and_slope(dot(feed, R.we[:, cols]) + R.be[0:1, cols])
     hidden = hidden.astype(BF16)
     R.hidden[rows, cols] = hidden
     back = (dot(grad, R.wc[cols, :], NT) * slope).astype(BF16)
-    R.hgrad[rows, :] = back
+    R.hgrad[pl.ds(i * (CHUNK // PATCHES), CHUNK // PATCHES)] = back.reshape(-1, PATCHES, CHUNK)
     R.dbe[:, cols] += sum8(back.astype(F32))
     branch = dot(hidden, R.wc[cols, :])
     fgrad = dot(back, R.we[:, cols], NT)
@@ -225,8 +230,8 @@
 
 
 def mixer_backward_first(R, slot):
-    kind = R.items[slot]
-    whole, pairs, zeros, scale = slot_facts(kind)
+    kind = kind_of(R, slot)
+    whole, pairs, scale = slot_facts(kind)
     rows = pl.ds(pl.multiple_of(slot * PATCHES, PATCHES), PATCHES)
     table = table_of(R, kind)
     branch = R.br[rows, :] + R.vec[8:9, :]
@@ -266,8 +271,8 @@
 
 
 def mixer_backward_second(R, slot, put):
-    kind = R.items[slot]
-    whole, pairs, zeros, scale = slot_facts(kind)
+    kind = kind_of(R, slot)
+    whole, pairs, scale = slot_facts(kind)
     rows = pl.ds(pl.multiple_of(slot * PATCHES, PATCHES), PATCHES)
     table = table_of(R, kind)
     tops, bottoms = [], []
@@ -284,14 +289,14 @@
     scaled = ngrad * R.vec[0:1, :]
     inner = scaled - jnp.mean(scaled, axis=-1, keepdims=True) - xhat * jnp.mean(scaled * xhat, axis=-1, keepdims=True)
     put(slot, rows, R.mgrad[rows, :] + inner * xscale)
+
 class Refs:
     pass
 
 
 VMEM = pl.BlockSpec(memory_space=pltpu.VMEM)
 SMEM = pl.BlockSpec(memory_space=pltpu.SMEM)
-ROOM = 62 * 2**20
-CHUNK = 512
+ROOM = 127 * 2**19
 
 
 def named(names, refs):
@@ -339,9 +344,9 @@
 
         @pl.loop(0, rows_all // CHUNK)
         def _(i):
-            mlp_chunk(R, pl.ds(pl.multiple_of(i * CHUNK, CHUNK), CHUNK), cols, at == 0)
-
-        R.dwe[:, cols] = dot(R.feed[...], R.hgrad[...], TN).astype(BF16)
+            mlp_chunk(R, i, cols, at == 0)
+
+        R.dwe[:, cols] = dot(R.feed[...], R.hgrad[...].reshape(-1, CHUNK), TN).astype(BF16)
 
     @pl.loop(0, hidden_all // CHUNK)
     def _(i):
@@ -407,7 +412,7 @@
     sums = ((40, WIDTH), F32)
     a = plain_call(
         forward_body,
-        dict(items=slot_items, tok=tok, cot=cot, table=table, vec=vec, inner=inner, outer=outer),
+        dict(items=slot_items, tok=tok, cot=cot, table=table, vec=vec, inner=inner.reshape(NB, BS, 2 * BS), outer=outer.reshape(NB, BS, 2 * BS)),
         dict(spec=wide, act=wide, slope=wide, bent=wide, mid=full, feed=flat, msk=flat, win=pairs, wout=pairs, stats=sums, sums=sums),
         {},
         "mixer_forward",
@@ -416,7 +421,7 @@
         mlp_body,
         dict(feed=a["feed"], msk=a["msk"], we=we, wc=wc, be=be.reshape(1, hidden)),
         dict(br=full, fg=full, dwe=((WIDTH, hidden), BF16), dwc=((WIDTH, hidden), BF16), dbe=((8, hidden), F32)),
-        dict(hidden=((n, hidden), BF16), hgrad=((n, CHUNK), BF16)),
+        dict(hidden=((n, hidden), BF16), hgrad=((n // PATCHES, PATCHES, CHUNK), BF16)),
         "mlp",
     )
     c = plain_call(
@@ -481,6 +486,595 @@
     return ins, outs
 
 
+MESH = pl.DeviceIdType.MESH
+ANY = pl.BlockSpec(memory_space=pl.ANY)
+FSDP = 8
+FIRST = 512
+
+
+def multiple(value, by):
+    return pl.multiple_of(value * by, by)
+
+
+class Place:
+    def __init__(self, copies):
+        self.z, self.f = lax.axis_index("rep"), lax.axis_index("fsdp")
+        self.core, self.chip = self.f & 1, self.f >> 1
+        self.copies = copies
+
+    def peer(self, mask):
+        return (self.z, self.f ^ mask)
+
+    def floor(self, offset):
+        return (lax.rem(self.z + offset, self.copies), self.f)
+
+
+def remote(src, dst, sems, at, device):
+    send, recv = sems
+    return pltpu.make_async_remote_copy(
+        src_ref=src, dst_ref=dst, send_sem=send.at[at], recv_sem=recv.at[at], device_id=device, device_id_type=MESH
+    )
+
+
+class Sum:
+    def __init__(self, place, own, from_core, from_chips, total, from_floors, done, sems):
+        self.p, self.own, self.from_core, self.from_chips = place, own, from_core, from_chips
+        self.total, self.from_floors, self.done = total, from_floors, done
+        self.core_sems, self.chip_sems, self.floor_sems, self.last_sems = sems
+        self.rows = done.shape[1] // place.copies
+
+    def core_copy(self, t):
+        other = 1 - self.p.core
+        return remote(self.own(t, pl.ds(0, FSDP // 2), other), self.from_core.at[t], self.core_sems, t, self.p.peer(1))
+
+    def chip_copy(self, t, k):
+        src = self.own(t, self.p.chip ^ k, self.p.core)
+        return remote(src, self.from_chips.at[t, k - 1], self.chip_sems, (t, k - 1), self.p.peer(2 * k))
+
+    def piece(self, floor):
+        return pl.ds(multiple(floor, self.rows), self.rows)
+
+    def floor_copy(self, t, d):
+        device = self.p.floor(d)
+        src = self.total.at[t, self.piece(device[0])]
+        return remote(src, self.from_floors.at[t, d - 1], self.floor_sems, (t, d - 1), device)
+
+    def last_copy(self, t, d):
+        mine = self.done.at[t, self.piece(self.p.z)]
+        return remote(mine, mine, self.last_sems, (t, d - 1), self.p.floor(d))
+
+    def last_arrival(self, t, d):
+        source = lax.rem(self.p.z + self.p.copies - d, self.p.copies)
+        theirs = self.done.at[t, self.piece(source)]
+        return remote(theirs, theirs, self.last_sems, (t, d - 1), self.p.floor(d))
+
+    def offsets(self):
+        return range(1, self.p.copies)
+
+    def start(self, t):
+        self.core_copy(t).start()
+
+    def to_chips(self, t):
+        self.core_copy(t).wait_recv()
+        for k in (3, 1, 2, 0):
+            at = self.p.chip ^ k
+            view = self.own(t, at, self.p.core)
+            view[...] = (view[...].astype(F32) + self.from_core[t, at].astype(F32)).astype(BF16)
+            if k:
+                self.chip_copy(t, k).start()
+
+    def to_floors(self, t):
+        total = self.own(t, self.p.chip, self.p.core)[...].astype(F32)
+        for k in (1, 2, 3):
+            self.chip_copy(t, k).wait_recv()
+            total = total + self.from_chips[t, k - 1].astype(F32)
+        self.total[t] = total.astype(BF16)
+        for d in self.offsets():
+            self.floor_copy(t, d).start()
+
+    def to_all(self, t):
+        mine = self.piece(self.p.z)
+        total = self.total[t, mine, :].astype(F32)
+        for d in self.offsets():
+            self.floor_copy(t, d).wait_recv()
+            total = total + self.from_floors[t, d - 1].astype(F32)
+        self.done[t, mine, :] = total.astype(BF16)
+        for d in self.offsets():
+            self.last_copy(t, d).start()
+
+    def finish(self, t):
+        for d in self.offsets():
+            self.last_arrival(t, d).wait_recv()
+
+    def sent(self, t):
+        self.core_copy(t).wait_send()
+        for k in (1, 2, 3):
+            self.chip_copy(t, k).wait_send()
+        for d in self.offsets():
+            self.floor_copy(t, d).wait_send()
+            self.last_copy(t, d).wait_send()
+
+
+class Gather:
+    def __init__(self, R, place):
+        self.R, self.p = R, place
+        self.deep, self.tall = R.we_in.shape[0], R.wc_in.shape[0]
+
+    def view(self, part, owner):
+        if part == 1:
+            return self.R.wc.at[pl.ds(multiple(owner, self.tall), self.tall), :]
+        cols = slice(0, FIRST) if part == 0 else slice(FIRST, None)
+        return self.R.we.at[pl.ds(multiple(owner, self.deep), self.deep), cols]
+
+    def copy(self, part, mask, target):
+        view = self.view(part, self.p.f ^ mask)
+        return pltpu.make_async_remote_copy(
+            src_ref=view,
+            dst_ref=view,
+            send_sem=self.R.gather_send.at[part, mask, target >> 1],
+            recv_sem=self.R.gather_recv.at[part, mask ^ target],
+            device_id=self.p.peer(target),
+            device_id_type=MESH,
+        )
+
+    def arrival(self, part, mask):
+        view = self.view(part, self.p.f ^ mask)
+        return pltpu.make_async_remote_copy(
+            src_ref=view,
+            dst_ref=view,
+            send_sem=self.R.gather_send.at[part, 0, 0],
+            recv_sem=self.R.gather_recv.at[part, mask],
+            device_id=self.p.peer(1),
+            device_id_type=MESH,
+        )
+
+    def start(self):
+        R, p = self.R, self.p
+        R.we[pl.ds(multiple(p.f, self.deep), self.deep), :] = R.we_in[...]
+        R.wc[pl.ds(multiple(p.f, self.tall), self.tall), :] = R.wc_in[...]
+        for part in (0, 1, 2):
+            for target in (6, 2, 4, 1):
+                self.copy(part, 0, target).start()
+
+    def pass_on(self, part):
+        for mask in (2, 4, 6):
+            self.arrival(part, mask).wait_recv()
+            self.copy(part, mask, 1).start()
+
+    def finish(self, part):
+        for mask in (1, 3, 5, 7):
+            self.arrival(part, mask).wait_recv()
+
+    def sent(self):
+        for part in (0, 1, 2):
+            for target in (6, 2, 4, 1):
+                self.copy(part, 0, target).wait_send()
+            for mask in (2, 4, 6):
+                self.copy(part, mask, 1).wait_send()
+
+
+def interleave(first, second):
+    low = lax.broadcasted_iota(jnp.int32, first.shape, 1) < BS
+    return (
+        jnp.where(low, first, pltpu.roll(second, BS, 1)),
+        jnp.where(low, pltpu.roll(first, BS, 1), second),
+    )
+
+
+def pack_small(R):
+    R.small[pl.ds(0, BS), :] = R.inner_in[...]
+    R.small[pl.ds(BS, BS), :] = R.outer_in[...]
+
+    def row(*refs):
+        return jnp.concatenate([ref[...].astype(F32) for ref in refs], axis=1)
+
+    none = jnp.zeros((1, BS), F32)
+    rows = [
+        row(R.fg_in, R.fs_in), R.ib_in[...].astype(F32), R.ob_in[...].astype(F32), row(R.gg_in, R.gs_in),
+        jnp.concatenate([R.cb_in[...].astype(F32), none], axis=1),
+        R.eb_in[:, :128].astype(F32), R.eb_in[:, 128:].astype(F32), jnp.zeros((9, 128), F32),
+    ]
+    R.small[pl.ds(2 * BS, 16), :] = jnp.concatenate(rows, axis=0).astype(BF16)
+
+
+def unpack_small(R):
+    for j in range(PAIRS):
+        cols = slice(128 * j, 128 * j + 128)
+        even = R.smalls[2 * j, pl.ds(2 * BS, 16), :].astype(F32)
+        odd = R.smalls[2 * j + 1, pl.ds(2 * BS, 16), :].astype(F32)
+        first, second = interleave(even, odd)
+        for row, (part, at) in enumerate(
+            [(first, 0), (second, 0), (first, 1), (second, 1), (first, 2), (second, 2), (first, 3), (second, 3), (first, 4)]
+        ):
+            R.vec[row : row + 1, cols] = part[at : at + 1]
+        for k, block in ((2 * j, even), (2 * j + 1, odd)):
+            R.be[0:1, 256 * k : 256 * k + 128] = block[5:6]
+            R.be[0:1, 256 * k + 128 : 256 * k + 256] = block[6:7]
+    for first, out in ((0, R.win), (BS, R.wout)):
+        complex_pairs(R.smalls.at[:, pl.ds(first, BS), :], out)
+
+
+def pack_sums(R):
+    slots = R.tok.shape[0] // PATCHES
+
+    def total(ref, at):
+        return jnp.sum(ref[pl.ds(at, 8), :], axis=0, keepdims=True)
+
+    feed_gain, feed_shift, contract, gain, shift = [total(R.sums, 8 * i) for i in range(5)]
+    outer, inner, expand = total(R.dbias, 0), total(R.dbias, 8), total(R.dbe, 0)
+    lane = lax.broadcasted_iota(jnp.int32, (1, 128), 1)
+    facts = jnp.zeros((1, 128), F32)
+    for i in range(5):
+        facts = jnp.where(lane == i, jnp.sum(total(R.stats, 8 * i), axis=1, keepdims=True), facts)
+    valid = jnp.zeros((1, 128), F32)
+    for slot in range(slots):
+        kind = kind_of(R, slot, 128)
+        valid = valid + jnp.where(kind == 0, 4, kind).astype(F32) * float(PATCHES // 4 * WIDTH)
+    facts = jnp.where(lane == 5, valid, facts)
+    none = jnp.zeros((1, 128), F32)
+    for j in range(PAIRS):
+        cols = slice(128 * j, 128 * j + 128)
+        real, imag = slice(256 * j, 256 * j + 128), slice(256 * j + 128, 256 * j + 256)
+        rows = [
+            interleave(gain[:, cols], shift[:, cols]),
+            interleave(inner[:, real], inner[:, imag]),
+            interleave(outer[:, real], outer[:, imag]),
+            interleave(feed_gain[:, cols], feed_shift[:, cols]),
+            interleave(contract[:, cols], none),
+        ]
+        for side in range(2):
+            k = 2 * j + side
+            R.vec_own[k] = jnp.concatenate(
+                [row[side] for row in rows]
+                + [expand[:, 256 * k : 256 * k + 128], expand[:, 256 * k + 128 : 256 * k + 256], facts],
+                axis=0,
+            )
+
+
+class Share:
+    def __init__(self, place, own, arrived, floors, sems):
+        self.p, self.own, self.arrived, self.floors = place, own, arrived, floors
+        self.peer_sems, self.floor_sems = sems
+
+    def peer_copy(self, k):
+        return remote(self.own.at[self.p.f ^ k], self.arrived.at[k - 1], self.peer_sems, k - 1, self.p.peer(k))
+
+    def floor_copy(self, d):
+        mine = self.floors.at[self.p.z]
+        return remote(mine, mine, self.floor_sems, d - 1, self.p.floor(d))
+
+    def floor_arrival(self, d):
+        theirs = self.floors.at[lax.rem(self.p.z + self.p.copies - d, self.p.copies)]
+        return remote(theirs, theirs, self.floor_sems, d - 1, self.p.floor(d))
+
+    def start(self):
+        for k in (6, 7, 2, 4, 3, 5, 1):
+            self.peer_copy(k).start()
+
+    def to_floors(self):
+        total = self.own[self.p.f].astype(F32)
+        for k in range(1, FSDP):
+            self.peer_copy(k).wait_recv()
+            total = total + self.arrived[k - 1].astype(F32)
+        self.floors[self.p.z] = total.astype(self.floors.dtype)
+        for d in range(1, self.p.copies):
+            self.floor_copy(d).start()
+
+    def finish(self):
+        for d in range(1, self.p.copies):
+            self.floor_arrival(d).wait_recv()
+        total = self.floors[0].astype(F32)
+        for z in range(1, self.p.copies):
+            total = total + self.floors[z].astype(F32)
+        return total
+
+    def sent(self):
+        for k in range(1, FSDP):
+            self.peer_copy(k).wait_send()
+        for d in range(1, self.p.copies):
+            self.floor_copy(d).wait_send()
+
+
+def layer(copies, R):
+    p = Place(copies)
+    n = R.tok.shape[0]
+    slots = n // PATCHES
+    hidden_all = R.we.shape[1]
+    chunks = hidden_all // CHUNK
+    blocks = n // CHUNK
+
+    def slot_rows(slot):
+        return pl.ds(multiple(slot, PATCHES), PATCHES)
+
+    def load(which, slot):
+        src, dst = ((R.tok_in, R.tok), (R.cot_in, R.msk))[which]
+        rows = slot_rows(slot)
+        return pltpu.make_async_copy(src.at[rows, :], dst.at[rows, :], R.load_sems.at[which, slot])
+
+    def store(which, slot):
+        src, dst = ((R.feed, R.out_ref), (R.fg, R.grad_ref))[which]
+        rows = slot_rows(slot)
+        return pltpu.make_async_copy(src.at[rows, :], dst.at[rows, :], R.store_sems.at[which, slot])
+
+    @pl.loop(0, slots)
+    def _(slot):
+        load(0, slot).start()
+        load(1, slot).start()
+
+    barrier = pltpu.get_barrier_semaphore()
+    for k in range(1, FSDP):
+        pl.semaphore_signal(barrier, inc=1, device_id=p.peer(k), device_id_type=MESH)
+    for d in range(1, copies):
+        pl.semaphore_signal(barrier, inc=1, device_id=p.floor(d), device_id_type=MESH)
+    pack_small(R)
+    pl.semaphore_wait(barrier, FSDP - 1 + copies - 1)
+
+    def small_copy(k):
+        return remote(R.small, R.smalls.at[p.f], (R.small_send, R.small_recv), k - 1, p.peer(k))
+
+    def small_arrival(k):
+        return remote(R.small, R.smalls.at[p.f ^ k], (R.small_send, R.small_recv), k - 1, p.peer(k))
+
+    for k in (6, 7, 2, 4, 3, 5, 1):
+        small_copy(k).start()
+    gather = Gather(R, p)
+    gather.start()
+    R.smalls[p.f] = R.small[...]
+    R.stats[...] = jnp.zeros_like(R.stats)
+    R.sums[...] = jnp.zeros_like(R.sums)
+    R.dbias[...] = jnp.zeros_like(R.dbias)
+    R.dbe[...] = jnp.zeros_like(R.dbe)
+    for k in range(1, FSDP):
+        small_arrival(k).wait_recv()
+    unpack_small(R)
+
+    @pl.loop(0, slots)
+    def _(slot):
+        load(0, slot).wait()
+        load(1, slot).wait()
+        mixer_forward(R, slot)
+        rows = slot_rows(slot)
+        R.br[rows, :] = jnp.zeros((PATCHES, WIDTH), F32)
+        R.fg[rows, :] = jnp.zeros((PATCHES, WIDTH), F32)
+
+        @pl.when(slot == slots // 2)
+        def _():
+            gather.pass_on(0)
+
+    gather.pass_on(1)
+    gather.finish(0)
+    gather.finish(1)
+
+    expand = Sum(
+        p, lambda t, chips, core: R.ew_own.at[t, chips, core], R.ew_core, R.ew_chips, R.ew_total, R.ew_floors, R.ew_done,
+        ((R.ew_s0, R.ew_r0), (R.ew_s1, R.ew_r1), (R.ew_s2, R.ew_r2), (R.ew_s3, R.ew_r3)),
+    )
+
+    @pl.loop(0, chunks)
+    def _(t):
+        cols = pl.ds(multiple(t, CHUNK), CHUNK)
+
+        @pl.loop(0, blocks)
+        def _(i):
+            @pl.when((t > 0) & (i == 1))
+            def _():
+                expand.to_chips(t - 1)
+
+            @pl.when((t > 0) & (i == 3))
+            def _():
+                expand.to_floors(t - 1)
+
+            @pl.when((t > 1) & (i == 1))
+            def _():
+                expand.to_all(t - 2)
+
+            mlp_chunk(R, i, cols, False)
+
+            @pl.when((t == 0) & (i == 1))
+            def _():
+                gather.pass_on(2)
+
+        @pl.when(t == 0)
+        def _():
+            gather.finish(2)
+
+        piece = dot(R.feed[...], R.hgrad[...].reshape(-1, CHUNK), TN).astype(BF16)
+        for k in range(FSDP):
+            R.ew_own[t, k // 2, k % 2] = piece[k * BS : (k + 1) * BS]
+        expand.start(t)
+
+    deep, tall = R.cw_done.shape[1:]
+
+    def contract_view(t, chips, core):
+        lanes = pl.ds(multiple(core, tall), tall)
+        if isinstance(chips, pl.Slice):
+            return R.hgrad.at[pl.ds(t * (FSDP // 2), FSDP // 2), :, lanes]
+        return R.hgrad.at[t * (FSDP // 2) + chips, :, lanes]
+
+    contract = Sum(
+        p, contract_view, R.cw_core, R.cw_chips, R.cw_total, R.cw_floors, R.cw_done,
+        ((R.cw_s0, R.cw_r0), (R.cw_s1, R.cw_r1), (R.cw_s2, R.cw_r2), (R.cw_s3, R.cw_r3)),
+    )
+    @pl.loop(0, 2)
+    def _(t):
+        @pl.loop(0, FSDP // 2)
+        def _(chip):
+            cols = pl.ds(multiple(chip, 2 * tall), 2 * tall)
+            piece = dot(R.msk[:, pl.ds(multiple(t, deep), deep)], R.hidden[:, cols], TN).astype(BF16)
+            R.hgrad[t * (FSDP // 2) + chip] = piece
+
+        contract.start(t)
+
+        @pl.when(t == 0)
+        def _():
+            expand.to_chips(chunks - 1)
+            expand.to_all(chunks - 2)
+
+        @pl.when(t == 1)
+        def _():
+            contract.to_chips(0)
+
+    contract.to_chips(1)
+
+    @pl.loop(0, slots)
+    def _(slot):
+        mixer_backward_first(R, slot)
+        store(0, slot).start()
+
+        @pl.when(slot == 1)
+        def _():
+            expand.to_floors(chunks - 1)
+
+        @pl.when(slot == 3)
+        def _():
+            contract.to_floors(0)
+            expand.to_all(chunks - 1)
+
+        @pl.when(slot == 6)
+        def _():
+            contract.to_floors(1)
+            contract.to_all(0)
+
+    def put_inner(j, value):
+        for side in range(2):
+            R.mix_own[2 * j + side, pl.ds(0, BS), :] = value[side * BS : (side + 1) * BS].astype(BF16)
+
+    def put_outer(j, value):
+        for side in range(2):
+            R.mix_own[2 * j + side, pl.ds(BS, BS), :] = value[side * BS : (side + 1) * BS].astype(BF16)
+
+    mixer_weight_gradients(R, put_inner, put_outer)
+    mixing = Share(p, R.mix_own, R.mix_peers, R.mix_floors, ((R.mix_s0, R.mix_r0), (R.mix_s1, R.mix_r1)))
+    mixing.start()
+
+    def put(slot, rows, value):
+        R.fg[rows, :] = value
+        store(1, slot).start()
+
+    @pl.loop(0, slots)
+    def _(slot):
+        mixer_backward_second(R, slot, put)
+
+        @pl.when(slot == 4)
+        def _():
+            contract.to_all(1)
+            mixing.to_floors()
+
+    pack_sums(R)
+    vectors = Share(p, R.vec_own, R.vec_peers, R.vec_floors, ((R.vec_s0, R.vec_r0), (R.vec_s1, R.vec_r1)))
+    vectors.start()
+    for t in range(chunks):
+        expand.finish(t)
+        R.ew_ref[:, t * CHUNK : (t + 1) * CHUNK] = R.ew_done[t].astype(F32)
+    for t in range(2):
+        contract.finish(t)
+        R.cw_ref[:, t * deep : (t + 1) * deep] = jnp.transpose(R.cw_done[t].astype(F32))
+    R.mix_ref[...] = mixing.finish()
+    vectors.to_floors()
+    R.vec_ref[...] = vectors.finish()
+    gather.sent()
+    for k in range(1, FSDP):
+        small_copy(k).wait_send()
+
+    @pl.loop(0, chunks)
+    def _(t):
+        expand.sent(t)
+
+    @pl.loop(0, 2)
+    def _(t):
+        contract.sent(t)
+
+    mixing.sent()
+    vectors.sent()
+
+    @pl.loop(0, slots)
+    def _(slot):
+        store(0, slot).wait()
+        store(1, slot).wait()
+
+
+def body_in_one(
+    copies, tokens, cotangent, slot_items, filter_gain, filter_shift, inner_weight, inner_bias, outer_weight, outer_bias,
+    feed_gain, feed_shift, expand_weight, expand_bias, contract_weight, contract_bias,
+):
+    slots = tokens.shape[0]
+    n = slots * PATCHES
+    deep, hidden = expand_weight.shape
+    tall = contract_weight.shape[0]
+    chunks = hidden // CHUNK
+    floors = copies - 1
+    ins = dict(
+        items=slot_items, tok_in=tokens.reshape(n, WIDTH), cot_in=cotangent.reshape(n, WIDTH), table=jnp.asarray(TABLES, BF16),
+        inner_in=inner_weight, outer_in=outer_weight, we_in=expand_weight, wc_in=contract_weight,
+        fg_in=filter_gain[None], fs_in=filter_shift[None], ib_in=inner_bias[None], ob_in=outer_bias[None],
+        gg_in=feed_gain[None], gs_in=feed_shift[None], cb_in=contract_bias[None], eb_in=expand_bias[None],
+    )
+    in_specs = [{"items": SMEM, "tok_in": ANY, "cot_in": ANY}.get(key, VMEM) for key in ins]
+    outs = dict(
+        out_ref=((n, WIDTH), BF16), grad_ref=((n, WIDTH), F32), ew_ref=((deep, hidden), F32), cw_ref=((tall, WIDTH), F32),
+        mix_ref=((2 * BS, 2 * BS), F32), vec_ref=((8, 128), F32),
+    )
+    out_specs = [{"out_ref": ANY, "grad_ref": ANY}.get(key, VMEM) for key in outs]
+    wide, flat, full = ((n, 2 * WIDTH), BF16), ((n, WIDTH), BF16), ((n, WIDTH), F32)
+    pairs, sums = ((2 * WIDTH, 4 * BS), BF16), ((40, WIDTH), F32)
+    memory = dict(
+        tok=flat, msk=flat, spec=wide, act=wide, slope=wide, bent=wide, mid=full, feed=flat, br=full, fg=full,
+        hidden=((n, hidden), BF16), hgrad=((n // PATCHES, PATCHES, CHUNK), BF16), we=((WIDTH, hidden), BF16), wc=((hidden, WIDTH), BF16),
+        win=pairs, wout=pairs, vec=((16, WIDTH), F32), be=((8, hidden), F32), stats=sums, sums=sums,
+        dbias=((16, 2 * WIDTH), F32), dbe=((8, hidden), F32),
+        small=((144, 128), BF16), smalls=((FSDP, 144, 128), BF16),
+        ew_own=((chunks, 4, 2, deep, CHUNK), BF16), ew_core=((chunks, 4, deep, CHUNK), BF16),
+        ew_chips=((chunks, 3, deep, CHUNK), BF16), ew_total=((chunks, deep, CHUNK), BF16),
+        ew_floors=((chunks, floors, deep // copies, CHUNK), BF16), ew_done=((chunks, deep, CHUNK), BF16),
+        cw_core=((2, 4, WIDTH // 2, tall), BF16),
+        cw_chips=((2, 3, WIDTH // 2, tall), BF16), cw_total=((2, WIDTH // 2, tall), BF16),
+        cw_floors=((2, floors, WIDTH // 2 // copies, tall), BF16), cw_done=((2, WIDTH // 2, tall), BF16),
+        mix_own=((FSDP, 128, 128), BF16), mix_peers=((FSDP - 1, 128, 128), BF16), mix_floors=((copies, 128, 128), BF16),
+        vec_own=((FSDP, 8, 128), F32), vec_peers=((FSDP - 1, 8, 128), F32), vec_floors=((copies, 8, 128), F32),
+    )
+    sems = dict(
+        load_sems=(2, slots), store_sems=(2, slots), small_send=(7,), small_recv=(7,),
+        gather_send=(3, 8, 4), gather_recv=(3, 8),
+    )
+    for key, parts in (("ew", chunks), ("cw", 2)):
+        for step, shape in enumerate(((parts,), (parts, 3), (parts, floors), (parts, floors))):
+            sems[f"{key}_s{step}"] = sems[f"{key}_r{step}"] = shape
+    for key in ("mix", "vec"):
+        for step, shape in enumerate(((FSDP - 1,), (floors,))):
+            sems[f"{key}_s{step}"] = sems[f"{key}_r{step}"] = shape
+    names = list(ins) + list(outs) + list(memory) + list(sems)
+
+    def kernel(*refs):
+        R = named(names, refs)
+        R.mgrad, R.out, R.ograd, R.igrad, R.cot = R.fg, R.feed, R.bent, R.slope, R.msk
+        layer(copies, R)
+
+    o = dict(
+        zip(
+            outs,
+            pl.pallas_call(
+                kernel,
+                out_shape=[jax.ShapeDtypeStruct(*spec) for spec in outs.values()],
+                in_specs=in_specs,
+                out_specs=out_specs,
+                scratch_shapes=[pltpu.VMEM(*spec) for spec in memory.values()]
+                + [pltpu.SemaphoreType.DMA(shape) for shape in sems.values()],
+                compiler_params=pltpu.CompilerParams(vmem_limit_bytes=ROOM, collective_id=0, has_side_effects=True),
+                name="mega",
+            )(*ins.values()),
+        )
+    )
+    vec = o["vec_ref"]
+    return (
+        o["out_ref"].reshape(tokens.shape), o["grad_ref"].reshape(tokens.shape), vec[0, :BS], vec[0, BS:], o["mix_ref"][:BS],
+        vec[1], o["mix_ref"][BS:], vec[2], vec[3, :BS], vec[3, BS:], o["ew_ref"], vec[5:7].reshape(-1), o["cw_ref"],
+        vec[4, :BS], jnp.sqrt(vec[7, :5] / vec[7, 5]),
+    )
+
+
 def solution(mesh):
     ins, outs = specs()
-    return jax.shard_map(body_by_collectives, mesh=mesh, in_specs=ins, out_specs=outs, check_vma=False)
+    whole = body_by_collectives
+    if mesh.shape["fsdp"] == FSDP and mesh.shape["rep"] in (2, 4):
+        whole = functools.partial(body_in_one, mesh.shape["rep"])
+    return jax.shard_map(whole, mesh=mesh, in_specs=ins, out_specs=outs, check_vma=False)

time: 361 us -> 126 us (0.35)
  waiting for transfers between devices: 119 us -> 0 us
  blocking collectives: 105 us -> 0 us
  between operations: 16.2 us -> 0.66 us
  Pallas kernels: 95.1 us -> 108 us
  other arithmetic: 7.73 us -> 1.84 us
    reduce_scatter x2 -> x0, waiting for transfers between devices: 69.8 us -> none  [scatter(): return lax.psum_scatter(x, 'fsdp', scatter_dimension=0, tiled=True)]
    psum x2 -> x0, blocking collectives: 58.9 us -> none  [the longest x1 39.6 us: body_by_collectives(): total = lax.psum(local, ('rep', 'fsdp'))]
    psum x1 -> x0, waiting for transfers between devices: 38.4 us -> none  [body_by_collectives(): own_small, own_we, own_wc = lax.psum((own_small, own_we, own_wc), 'rep')]
    unnamed x1 -> x0, blocking collectives: 25.8 us -> none
    all_gather x2 -> x0, blocking collectives: 19.9 us -> none  [gather(): return lax.all_gather(x, 'fsdp', axis=0, tiled=True)]
    pallas_call x3 -> x1, Pallas kernels: 95.1 us -> 108 us  [body_in_one(): pl.pallas_call(kernel, out_shape=[jax.ShapeDtypeStruct(*spec) for spec in...]
    unnamed x7 -> x0, waiting for transfers between devices: 10.5 us -> none
    concatenate x3 -> x0, local copies, waits for them, and re-layouts: 6.78 us -> none  [the longest x1 5.43 us: body_by_collectives(): packed = lax.all_gather(jnp.concatenate(vectors), 'fsdp', axis=0)]
  transfers between devices with their start and end apart: 6 -> 0, of which waited for: 4 -> 0; matrix products, arithmetic and copies ran while one was open for 4% -> 0% of each run, Pallas kernels for 7% -> 0%
where the time goes in v2:
time: 126 us; the launch traced here: 125 us
  Pallas kernels  108 us (86%)
  local copies, waits for them, and re-layouts  14.6 us (12%)
  other arithmetic  1.84 us (1%)
    pallas_call x1, Pallas kernels, body_in_one(): pl.pallas_call(kernel, out_shape=[jax.ShapeDtypeStruct(*spec) for spec in...  108 us
    unnamed x10, local copies, waits for them, and re-layouts  6.81 us

profile of v2, /device:TPU:0, one launch (start us, length us, event | category | flops | bytes accessed | tf_op | source)
XLA Modules:
  0.0 125.2 jit_solution(14461249738992448179)
XLA Ops:
  0.6 1.2 broadcast_in_dim.31.refs_15_
  1.9 108.0 %mega.1 = (bf16[2048,512]{1,0:T(8,128)(2,1)}, f32[2048,512]{1,0:T(8,128)}, f32[64,2048]{1,0:T(8,128)}, f32[256,512]{1,0:T(8,128)}, f32[128,128]{1,0:T(8,128)}, /*index=5*/f32[8,128]{1,0:T(8,128)}) custom-call(s32[8]{0:T(128)} %refs_0_.1, bf16[2048,512]{1,0:T(8,128)(2,1)} %bitcast.31, bf16[2048,512]{1,0:T(8,128)(2,1)} %bitcast.32, ...), custom_call_target="tpu_custom_call" | custom-call | tf_op jit(solution)/shard_map/mega/pallas_call | solution.py:1055
  109.9 1.5 %slice_bitcast_fusion.1 = (f32[64]{0:T(128)}, f32[64]{0:T(128)}, f32[64]{0:T(128)}, f32[64]{0:T(128)}, f32[64]{0:T(128)}) fusion(f32[8,128]{1,0:T(8,128)} %get-tuple-element.23), kind=kLoop, calls=%fused_computation.2 | loop fusion | bytes 2560 | tf_op jit(solution)/shard_map/squeeze | solution.py:1071
  111.3 1.4 %fusion = (f32[64,128]{1,0:T(8,128)}, f32[64,128]{1,0:T(8,128)}) fusion(f32[128,128]{1,0:T(8,128)} %get-tuple-element.24), kind=kLoop, calls=%fused_computation.9 | loop fusion | bytes 131072 | tf_op jit(solution)/shard_map/slice | solution.py:1070
  112.7 1.3 %slice_bitcast_fusion.4 = (f32[128]{0:T(128)}, f32[128]{0:T(128)}) fusion(f32[8,128]{1,0:T(8,128)} %get-tuple-element.23), kind=kLoop, calls=%fused_computation.5 | loop fusion | bytes 2048 | tf_op jit(solution)/shard_map/squeeze | solution.py:1070
  114.0 1.2 slice_bitcast_fusion
  115.2 1.3 %slice.47 = f32[1,1]{1,0:T(1,128)} slice(f32[8,128]{1,0:T(8,128)} %get-tuple-element.23), slice={[7:8], [5:6]} | slice | bytes 8 | tf_op jit(solution)/shard_map/slice | solution.py:1071
  116.5 1.8 %sqrt_bitcast_fusion = f32[5]{0:T(128)} fusion(f32[8,128]{1,0:T(8,128)} %get-tuple-element.23, f32[]{:T(128)} %bitcast.19), kind=kLoop, calls=%fused_computation.1 | loop fusion | flops 5 | bytes 44 | tf_op jit(solution)/shard_map/sqrt | solution.py:1071
  118.3 0.0 copy-start
  118.3 3.2 %copy.35 = bf16[8,256,512]{2,1,0:T(8,128)(2,1)} copy(bf16[8,256,512]{2,1,0:T(8,128)(2,1)} %bitcast.33) | data formatting | bytes 4194304
  121.5 0.0 copy-done
  121.5 0.0 copy-start.2
  121.5 0.0 copy-start.1
  121.5 2.0 %copy.36 = f32[8,256,512]{2,1,0:T(8,128)} copy(f32[8,256,512]{2,1,0:T(8,128)S(1)} %bitcast.30) | data formatting | bytes 8388608
  123.6 0.0 copy-done.2
  123.6 0.8 copy.37
  124.4 0.0 copy-done.1
  124.4 0.8 copy.38
Async XLA Ops:
  118.3 3.2 %copy-start = (f32[2048,512]{1,0:T(8,128)S(1)}, f32[2048,512]{1,0:T(8,128)}, u32[]{:S(2)}) copy-start(f32[2048,512]{1,0:T(8,128)} %get-tuple-element.22) | copy-start | bytes 12582916
  121.5 2.0 %copy-start.2 = (f32[64,2048]{1,0:T(8,128)S(1)}, f32[64,2048]{1,0:T(8,128)}, u32[]{:S(2)}) copy-start(f32[64,2048]{1,0:T(8,128)} %get-tuple-element.61) | copy-start | bytes 1572868
  121.5 2.8 %copy-start.1 = (f32[256,512]{1,0:T(8,128)S(1)}, f32[256,512]{1,0:T(8,128)}, u32[]{:S(2)}) copy-start(f32[256,512]{1,0:T(8,128)} %get-tuple-element.63) | copy-start | bytes 1572868

commit v3 on v2

--- a/solution.py
+++ b/solution.py
@@ -122,6 +122,14 @@
     return ra + jnp.where(is_pair, rb, 0.0), jnp.where(is_pair, ia - ib, rb)
 
 
+def interleave(first, second):
+    low = lax.broadcasted_iota(jnp.int32, first.shape, 1) < BS
+    return (
+        jnp.where(low, first, pltpu.roll(second, BS, 1)),
+        jnp.where(low, pltpu.roll(first, BS, 1), second),
+    )
+
+
 def complex_pairs(weight_ref, out_ref):
     low = lax.broadcasted_iota(jnp.int32, (BS, 128), 1) < BS
     for j in range(PAIRS):
@@ -158,15 +166,24 @@
     return jnp.where((kind == 0) | (quadrant < kind), values, 0.0)
 
 
+def mixer_start(R, slot):
+    kind = kind_of(R, slot)
+    whole, pairs, scale = slot_facts(kind)
+    rows = pl.ds(pl.multiple_of(slot * PATCHES, PATCHES), PATCHES)
+    x = R.tok[rows, :].astype(F32)
+    xhat, _ = row_stats(x)
+    R.stats[pl.ds(0, 8), :] += masked_squares(x, kind)
+    R.mid[rows, :] = dot(table_of(R, kind), xhat.astype(BF16))
+    grad = masked(R.cot[rows, :].astype(F32), kind)
+    R.sums[pl.ds(16, 8), :] += sum8(grad)
+    R.msk[rows, :] = grad.astype(BF16)
+
+
 def mixer_forward(R, slot):
     kind = kind_of(R, slot)
     whole, pairs, scale = slot_facts(kind)
     rows = pl.ds(pl.multiple_of(slot * PATCHES, PATCHES), PATCHES)
-    table = table_of(R, kind)
-    x = R.tok[rows, :].astype(F32)
-    xhat, _ = row_stats(x)
-    R.stats[pl.ds(0, 8), :] += masked_squares(x, kind)
-    spec = dot(table, xhat.astype(BF16)) * (R.vec[0:1, :] * scale)
+    spec = R.mid[rows, :] * (R.vec[0:1, :] * scale)
     top = lax.broadcasted_iota(jnp.int32, (HALF, WIDTH), 0)
     at_zero = (top >= pairs) & (top < pairs + jnp.where(whole, WHOLE_ZEROS, PART_ZEROS))
     shift = R.vec[1:2, :] * jnp.where(whole, float(SIDE), float(SIDE // 2)).astype(F32)
@@ -198,35 +215,35 @@
         tops.append(u.astype(BF16))
         bottoms.append(v.astype(BF16))
     folded = jnp.concatenate([jnp.concatenate(tops, axis=1), jnp.concatenate(bottoms, axis=1)], axis=0)
-    mixer_out = dot(table, folded, TN) * scale
+    mixer_out = dot(table_of(R, kind), folded, TN) * scale
     R.stats[pl.ds(8, 8), :] += masked_squares(mixer_out, kind)
-    middle = x + mixer_out
+    middle = R.tok[rows, :].astype(F32) + mixer_out
     R.stats[pl.ds(16, 8), :] += masked_squares(middle, kind)
     R.mid[rows, :] = middle
     yhat, _ = row_stats(middle)
     R.feed[rows, :] = (yhat * R.vec[6:7, :] + R.vec[7:8, :]).astype(BF16)
-    grad = masked(R.cot[rows, :].astype(F32), kind)
-    R.sums[pl.ds(16, 8), :] += sum8(grad)
-    R.msk[rows, :] = grad.astype(BF16)
-
-
-def mlp_chunk(R, i, cols, first):
+
+
+def mlp_front(R, i, cols, we, wc):
     rows = pl.ds(pl.multiple_of(i * CHUNK, CHUNK), CHUNK)
-    feed, grad = R.feed[rows, :], R.msk[rows, :]
-    hidden, slope = gelu_and_slope(dot(feed, R.we[:, cols]) + R.be[0:1, cols])
+    hidden, slope = gelu_and_slope(dot(R.feed[rows, :], we) + R.be[0:1, cols])
     hidden = hidden.astype(BF16)
-    R.hidden[rows, cols] = hidden
-    back = (dot(grad, R.wc[cols, :], NT) * slope).astype(BF16)
-    R.hgrad[pl.ds(i * (CHUNK // PATCHES), CHUNK // PATCHES)] = back.reshape(-1, PATCHES, CHUNK)
-    R.dbe[:, cols] += sum8(back.astype(F32))
-    branch = dot(hidden, R.wc[cols, :])
-    fgrad = dot(back, R.we[:, cols], NT)
-    if first:
-        R.br[rows, :] = branch
-        R.fg[rows, :] = fgrad
-    else:
-        R.br[rows, :] += branch
-        R.fg[rows, :] += fgrad
+    R.hidden[rows, :] = hidden
+    back = dot(R.msk[rows, :], wc, NT) * slope
+    R.dbe[:, cols] += sum8(back)
+    back = back.astype(BF16)
+    R.hgrad[rows, :] = back
+    return rows, hidden, back
+
+
+def mlp_back(R, rows, hidden, back, we, wc):
+    R.br[rows, :] += dot(hidden, wc)
+    R.fg[rows, :] += dot(back, we, NT)
+
+
+def mlp_chunk(R, i, cols, we, wc):
+    rows, hidden, back = mlp_front(R, i, cols, we, wc)
+    mlp_back(R, rows, hidden, back, we, wc)
 
 
 def mixer_backward_first(R, slot):
@@ -332,26 +349,25 @@
 
     @pl.loop(0, R.tok.shape[0] // PATCHES)
     def _(slot):
+        mixer_start(R, slot)
         mixer_forward(R, slot)
 
 
 def mlp_body(R):
-    rows_all = R.feed.shape[0]
-    hidden_all = R.we.shape[1]
     R.dbe[...] = jnp.zeros_like(R.dbe)
-    for at in range(0, hidden_all, CHUNK):
-        cols = slice(at, at + CHUNK)
-
-        @pl.loop(0, rows_all // CHUNK)
+    R.br[...] = jnp.zeros_like(R.br)
+    R.fg[...] = jnp.zeros_like(R.fg)
+
+    @pl.loop(0, R.we.shape[1] // CHUNK)
+    def _(t):
+        cols = pl.ds(pl.multiple_of(t * CHUNK, CHUNK), CHUNK)
+
+        @pl.loop(0, R.feed.shape[0] // CHUNK)
         def _(i):
-            mlp_chunk(R, i, cols, at == 0)
-
-        R.dwe[:, cols] = dot(R.feed[...], R.hgrad[...].reshape(-1, CHUNK), TN).astype(BF16)
-
-    @pl.loop(0, hidden_all // CHUNK)
-    def _(i):
-        cols = pl.ds(pl.multiple_of(i * CHUNK, CHUNK), CHUNK)
-        R.dwc[:, cols] = dot(R.msk[...], R.hidden[:, cols], TN).astype(BF16)
+            mlp_chunk(R, i, cols, R.we[:, cols], R.wc[cols, :])
+
+        R.dwe[:, cols] = dot(R.feed[...], R.hgrad[...], TN).astype(BF16)
+        R.dwc[:, cols] = dot(R.msk[...], R.hidden[...], TN).astype(BF16)
 
 
 def backward_body(R):
@@ -421,7 +437,7 @@
         mlp_body,
         dict(feed=a["feed"], msk=a["msk"], we=we, wc=wc, be=be.reshape(1, hidden)),
         dict(br=full, fg=full, dwe=((WIDTH, hidden), BF16), dwc=((WIDTH, hidden), BF16), dbe=((8, hidden), F32)),
-        dict(hidden=((n, hidden), BF16), hgrad=((n // PATCHES, PATCHES, CHUNK), BF16)),
+        dict(hidden=((n, CHUNK), BF16), hgrad=((n, CHUNK), BF16)),
         "mlp",
     )
     c = plain_call(
@@ -490,6 +506,7 @@
 ANY = pl.BlockSpec(memory_space=pl.ANY)
 FSDP = 8
 FIRST = 512
+EARLY = 2
 
 
 def multiple(value, by):
@@ -517,36 +534,39 @@
 
 
 class Sum:
-    def __init__(self, place, own, from_core, from_chips, total, from_floors, done, sems):
-        self.p, self.own, self.from_core, self.from_chips = place, own, from_core, from_chips
-        self.total, self.from_floors, self.done = total, from_floors, done
-        self.core_sems, self.chip_sems, self.floor_sems, self.last_sems = sems
-        self.rows = done.shape[1] // place.copies
+    def __init__(self, place, R):
+        self.p, self.R = place, R
+        self.rows = R.sum_done.shape[1] // place.copies
 
     def core_copy(self, t):
+        R = self.R
         other = 1 - self.p.core
-        return remote(self.own(t, pl.ds(0, FSDP // 2), other), self.from_core.at[t], self.core_sems, t, self.p.peer(1))
+        return remote(R.sum_own.at[t, :, other], R.sum_core.at[t], (R.sum_s0, R.sum_r0), t, self.p.peer(1))
 
     def chip_copy(self, t, k):
-        src = self.own(t, self.p.chip ^ k, self.p.core)
-        return remote(src, self.from_chips.at[t, k - 1], self.chip_sems, (t, k - 1), self.p.peer(2 * k))
+        R = self.R
+        src = R.sum_own.at[t, self.p.chip ^ k, self.p.core]
+        return remote(src, R.sum_chips.at[t, k - 1], (R.sum_s1, R.sum_r1), (t, k - 1), self.p.peer(2 * k))
 
     def piece(self, floor):
         return pl.ds(multiple(floor, self.rows), self.rows)
 
     def floor_copy(self, t, d):
+        R = self.R
         device = self.p.floor(d)
-        src = self.total.at[t, self.piece(device[0])]
-        return remote(src, self.from_floors.at[t, d - 1], self.floor_sems, (t, d - 1), device)
+        src = R.sum_total.at[t, self.piece(device[0])]
+        return remote(src, R.sum_floors.at[t, d - 1], (R.sum_s2, R.sum_r2), (t, d - 1), device)
 
     def last_copy(self, t, d):
-        mine = self.done.at[t, self.piece(self.p.z)]
-        return remote(mine, mine, self.last_sems, (t, d - 1), self.p.floor(d))
+        R = self.R
+        mine = R.sum_done.at[t, self.piece(self.p.z)]
+        return remote(mine, mine, (R.sum_s3, R.sum_r3), (t, d - 1), self.p.floor(d))
 
     def last_arrival(self, t, d):
+        R = self.R
         source = lax.rem(self.p.z + self.p.copies - d, self.p.copies)
-        theirs = self.done.at[t, self.piece(source)]
-        return remote(theirs, theirs, self.last_sems, (t, d - 1), self.p.floor(d))
+        theirs = R.sum_done.at[t, self.piece(source)]
+        return remote(theirs, theirs, (R.sum_s3, R.sum_r3), (t, d - 1), self.p.floor(d))
 
     def offsets(self):
         return range(1, self.p.copies)
@@ -555,30 +575,33 @@
         self.core_copy(t).start()
 
     def to_chips(self, t):
+        R = self.R
         self.core_copy(t).wait_recv()
         for k in (3, 1, 2, 0):
             at = self.p.chip ^ k
-            view = self.own(t, at, self.p.core)
-            view[...] = (view[...].astype(F32) + self.from_core[t, at].astype(F32)).astype(BF16)
+            mine = R.sum_own[t, at, self.p.core].astype(F32) + R.sum_core[t, at].astype(F32)
+            R.sum_own[t, at, self.p.core] = mine.astype(BF16)
             if k:
                 self.chip_copy(t, k).start()
 
     def to_floors(self, t):
-        total = self.own(t, self.p.chip, self.p.core)[...].astype(F32)
+        R = self.R
+        total = R.sum_own[t, self.p.chip, self.p.core].astype(F32)
         for k in (1, 2, 3):
             self.chip_copy(t, k).wait_recv()
-            total = total + self.from_chips[t, k - 1].astype(F32)
-        self.total[t] = total.astype(BF16)
+            total = total + R.sum_chips[t, k - 1].astype(F32)
+        R.sum_total[t] = total.astype(BF16)
         for d in self.offsets():
             self.floor_copy(t, d).start()
 
     def to_all(self, t):
+        R = self.R
         mine = self.piece(self.p.z)
-        total = self.total[t, mine, :].astype(F32)
+        total = R.sum_total[t, mine, :].astype(F32)
         for d in self.offsets():
             self.floor_copy(t, d).wait_recv()
-            total = total + self.from_floors[t, d - 1].astype(F32)
-        self.done[t, mine, :] = total.astype(BF16)
+            total = total + R.sum_floors[t, d - 1].astype(F32)
+        R.sum_done[t, mine, :] = total.astype(BF16)
         for d in self.offsets():
             self.last_copy(t, d).start()
 
@@ -598,67 +621,61 @@
 class Gather:
     def __init__(self, R, place):
         self.R, self.p = R, place
-        self.deep, self.tall = R.we_in.shape[0], R.wc_in.shape[0]
-
-    def view(self, part, owner):
-        if part == 1:
-            return self.R.wc.at[pl.ds(multiple(owner, self.tall), self.tall), :]
-        cols = slice(0, FIRST) if part == 0 else slice(FIRST, None)
-        return self.R.we.at[pl.ds(multiple(owner, self.deep), self.deep), cols]
-
-    def copy(self, part, mask, target):
-        view = self.view(part, self.p.f ^ mask)
+
+    def lay(self):
+        R, f = self.R, self.p.f
+        deep = R.we_in.shape[0]
+        chunks = R.w.shape[0]
+        for t in range(chunks):
+            R.w[t, f, :, CHUNK:] = R.wc_in[pl.ds(t * deep, deep), :]
+        for t in range(0, chunks, 2):
+            for m in range(CHUNK // 128):
+                at = m * 4 * chunks * BS // 2 + t * BS
+                even = R.we_in[:, at : at + 128].astype(F32)
+                odd = R.we_in[:, at + chunks * BS : at + chunks * BS + 128].astype(F32)
+                for side, part in enumerate(interleave(even, odd)):
+                    R.w[t + side, f, :, 128 * m : 128 * m + 128] = part.astype(BF16)
+
+    def copy(self, t, mask, target):
+        view = self.R.w.at[t, self.p.f ^ mask]
         return pltpu.make_async_remote_copy(
             src_ref=view,
             dst_ref=view,
-            send_sem=self.R.gather_send.at[part, mask, target >> 1],
-            recv_sem=self.R.gather_recv.at[part, mask ^ target],
+            send_sem=self.R.gather_send.at[t, mask, target >> 1],
+            recv_sem=self.R.gather_recv.at[t, mask ^ target],
             device_id=self.p.peer(target),
             device_id_type=MESH,
         )
 
-    def arrival(self, part, mask):
-        view = self.view(part, self.p.f ^ mask)
+    def arrival(self, t, mask):
+        view = self.R.w.at[t, self.p.f ^ mask]
         return pltpu.make_async_remote_copy(
             src_ref=view,
             dst_ref=view,
-            send_sem=self.R.gather_send.at[part, 0, 0],
-            recv_sem=self.R.gather_recv.at[part, mask],
+            send_sem=self.R.gather_send.at[t, 0, 0],
+            recv_sem=self.R.gather_recv.at[t, mask],
             device_id=self.p.peer(1),
             device_id_type=MESH,
         )
 
-    def start(self):
-        R, p = self.R, self.p
-        R.we[pl.ds(multiple(p.f, self.deep), self.deep), :] = R.we_in[...]
-        R.wc[pl.ds(multiple(p.f, self.tall), self.tall), :] = R.wc_in[...]
-        for part in (0, 1, 2):
-            for target in (6, 2, 4, 1):
-                self.copy(part, 0, target).start()
-
-    def pass_on(self, part):
+    def start(self, t):
+        for target in (6, 2, 4, 1):
+            self.copy(t, 0, target).start()
+
+    def pass_on(self, t):
         for mask in (2, 4, 6):
-            self.arrival(part, mask).wait_recv()
-            self.copy(part, mask, 1).start()
-
-    def finish(self, part):
+            self.arrival(t, mask).wait_recv()
+            self.copy(t, mask, 1).start()
+
+    def finish(self, t):
         for mask in (1, 3, 5, 7):
-            self.arrival(part, mask).wait_recv()
-
-    def sent(self):
-        for part in (0, 1, 2):
-            for target in (6, 2, 4, 1):
-                self.copy(part, 0, target).wait_send()
-            for mask in (2, 4, 6):
-                self.copy(part, mask, 1).wait_send()
-
-
-def interleave(first, second):
-    low = lax.broadcasted_iota(jnp.int32, first.shape, 1) < BS
-    return (
-        jnp.where(low, first, pltpu.roll(second, BS, 1)),
-        jnp.where(low, pltpu.roll(first, BS, 1), second),
-    )
+            self.arrival(t, mask).wait_recv()
+
+    def sent(self, t):
+        for target in (6, 2, 4, 1):
+            self.copy(t, 0, target).wait_send()
+        for mask in (2, 4, 6):
+            self.copy(t, mask, 1).wait_send()
 
 
 def pack_small(R):
@@ -672,7 +689,7 @@
     rows = [
         row(R.fg_in, R.fs_in), R.ib_in[...].astype(F32), R.ob_in[...].astype(F32), row(R.gg_in, R.gs_in),
         jnp.concatenate([R.cb_in[...].astype(F32), none], axis=1),
-        R.eb_in[:, :128].astype(F32), R.eb_in[:, 128:].astype(F32), jnp.zeros((9, 128), F32),
+        R.eb_in[...].astype(F32), jnp.zeros((9, 128), F32),
     ]
     R.small[pl.ds(2 * BS, 16), :] = jnp.concatenate(rows, axis=0).astype(BF16)
 
@@ -687,9 +704,8 @@
             [(first, 0), (second, 0), (first, 1), (second, 1), (first, 2), (second, 2), (first, 3), (second, 3), (first, 4)]
         ):
             R.vec[row : row + 1, cols] = part[at : at + 1]
-        for k, block in ((2 * j, even), (2 * j + 1, odd)):
-            R.be[0:1, 256 * k : 256 * k + 128] = block[5:6]
-            R.be[0:1, 256 * k + 128 : 256 * k + 256] = block[6:7]
+        for t in range(R.be.shape[1] // CHUNK):
+            R.be[0:1, t * CHUNK + 128 * j : t * CHUNK + 128 * j + 128] = (first, second)[t % 2][5 + t // 2 : 6 + t // 2]
     for first, out in ((0, R.win), (BS, R.wout)):
         complex_pairs(R.smalls.at[:, pl.ds(first, BS), :], out)
 
@@ -722,13 +738,11 @@
             interleave(feed_gain[:, cols], feed_shift[:, cols]),
             interleave(contract[:, cols], none),
         ]
+        for t in range(0, R.be.shape[1] // CHUNK, 2):
+            low, high = [expand[:, (t + s) * CHUNK + 128 * j : (t + s) * CHUNK + 128 * j + 128] for s in range(2)]
+            rows.append(interleave(low, high))
         for side in range(2):
-            k = 2 * j + side
-            R.vec_own[k] = jnp.concatenate(
-                [row[side] for row in rows]
-                + [expand[:, 256 * k : 256 * k + 128], expand[:, 256 * k + 128 : 256 * k + 256], facts],
-                axis=0,
-            )
+            R.vec_own[2 * j + side] = jnp.concatenate([row[side] for row in rows] + [facts], axis=0)
 
 
 class Share:
@@ -779,9 +793,9 @@
     p = Place(copies)
     n = R.tok.shape[0]
     slots = n // PATCHES
-    hidden_all = R.we.shape[1]
-    chunks = hidden_all // CHUNK
+    chunks = R.w.shape[0]
     blocks = n // CHUNK
+    last = chunks - 1
 
     def slot_rows(slot):
         return pl.ds(multiple(slot, PATCHES), PATCHES)
@@ -795,62 +809,71 @@
         src, dst = ((R.feed, R.out_ref), (R.fg, R.grad_ref))[which]
         rows = slot_rows(slot)
         return pltpu.make_async_copy(src.at[rows, :], dst.at[rows, :], R.store_sems.at[which, slot])
-
-    @pl.loop(0, slots)
-    def _(slot):
-        load(0, slot).start()
-        load(1, slot).start()
 
     barrier = pltpu.get_barrier_semaphore()
     for k in range(1, FSDP):
         pl.semaphore_signal(barrier, inc=1, device_id=p.peer(k), device_id_type=MESH)
     for d in range(1, copies):
         pl.semaphore_signal(barrier, inc=1, device_id=p.floor(d), device_id_type=MESH)
-    pack_small(R)
-    pl.semaphore_wait(barrier, FSDP - 1 + copies - 1)
-
-    def small_copy(k):
-        return remote(R.small, R.smalls.at[p.f], (R.small_send, R.small_recv), k - 1, p.peer(k))
-
-    def small_arrival(k):
-        return remote(R.small, R.smalls.at[p.f ^ k], (R.small_send, R.small_recv), k - 1, p.peer(k))
-
-    for k in (6, 7, 2, 4, 3, 5, 1):
-        small_copy(k).start()
-    gather = Gather(R, p)
-    gather.start()
-    R.smalls[p.f] = R.small[...]
+    for slot in range(slots):
+        load(0, slot).start()
+        load(1, slot).start()
     R.stats[...] = jnp.zeros_like(R.stats)
     R.sums[...] = jnp.zeros_like(R.sums)
     R.dbias[...] = jnp.zeros_like(R.dbias)
     R.dbe[...] = jnp.zeros_like(R.dbe)
+    pack_small(R)
+    R.smalls[p.f] = R.small[...]
+    gather = Gather(R, p)
+    gather.lay()
+
+    def begin(slot):
+        load(0, slot).wait()
+        load(1, slot).wait()
+        mixer_start(R, slot)
+        rows = slot_rows(slot)
+        R.br[rows, :] = jnp.zeros((PATCHES, WIDTH), F32)
+        R.fg[rows, :] = jnp.zeros((PATCHES, WIDTH), F32)
+
+    pl.loop(0, EARLY)(begin)
+    pl.semaphore_wait(barrier, FSDP - 1 + copies - 1)
+
+    def small_copy(k):
+        return remote(R.small, R.smalls.at[p.f], (R.small_send, R.small_recv), k - 1, p.peer(k))
+
+    def small_arrival(k):
+        return remote(R.small, R.smalls.at[p.f ^ k], (R.small_send, R.small_recv), k - 1, p.peer(k))
+
+    for k in (6, 7, 2, 4, 3, 5, 1):
+        small_copy(k).start()
+    gather.start(0)
+    gather.start(1)
+    pl.loop(EARLY, slots)(begin)
     for k in range(1, FSDP):
         small_arrival(k).wait_recv()
     unpack_small(R)
 
     @pl.loop(0, slots)
     def _(slot):
-        load(0, slot).wait()
-        load(1, slot).wait()
         mixer_forward(R, slot)
-        rows = slot_rows(slot)
-        R.br[rows, :] = jnp.zeros((PATCHES, WIDTH), F32)
-        R.fg[rows, :] = jnp.zeros((PATCHES, WIDTH), F32)
-
-        @pl.when(slot == slots // 2)
-        def _():
-            gather.pass_on(0)
-
-    gather.pass_on(1)
+
+    gather.start(2)
+    gather.start(3)
+    gather.pass_on(0)
     gather.finish(0)
-    gather.finish(1)
-
-    expand = Sum(
-        p, lambda t, chips, core: R.ew_own.at[t, chips, core], R.ew_core, R.ew_chips, R.ew_total, R.ew_floors, R.ew_done,
-        ((R.ew_s0, R.ew_r0), (R.ew_s1, R.ew_r1), (R.ew_s2, R.ew_r2), (R.ew_s3, R.ew_r3)),
-    )
-
-    @pl.loop(0, chunks)
+    sums = Sum(p, R)
+
+    def weights(t):
+        return [R.w[t, :, :, pl.ds(at, CHUNK)].reshape(-1, CHUNK) for at in (0, CHUNK)]
+
+    def weight_gradients(t):
+        for at, (left, right) in ((0, (R.feed, R.hgrad)), (CHUNK, (R.hidden, R.msk))):
+            piece = dot(left[...], right[...], TN).astype(BF16)
+            for k in range(FSDP):
+                R.sum_own[t, k // 2, k % 2, :, at : at + CHUNK] = piece[k * BS : (k + 1) * BS]
+        sums.start(t)
+
+    @pl.loop(0, last)
     def _(t):
         cols = pl.ds(multiple(t, CHUNK), CHUNK)
 
@@ -858,132 +881,98 @@
         def _(i):
             @pl.when((t > 0) & (i == 1))
             def _():
-                expand.to_chips(t - 1)
-
-            @pl.when((t > 0) & (i == 3))
-            def _():
-                expand.to_floors(t - 1)
+                sums.to_chips(t - 1)
 
             @pl.when((t > 1) & (i == 1))
             def _():
-                expand.to_all(t - 2)
-
-            mlp_chunk(R, i, cols, False)
-
-            @pl.when((t == 0) & (i == 1))
+                sums.to_floors(t - 2)
+
+            mlp_chunk(R, i, cols, *weights(t))
+
+            @pl.when(i == 2)
             def _():
-                gather.pass_on(2)
-
-        @pl.when(t == 0)
+                gather.pass_on(t + 1)
+
+        weight_gradients(t)
+        gather.finish(t + 1)
+
+    cols = slice(last * CHUNK, (last + 1) * CHUNK)
+
+    @pl.loop(0, blocks)
+    def _(i):
+        @pl.when(i == 1)
         def _():
-            gather.finish(2)
-
-        piece = dot(R.feed[...], R.hgrad[...].reshape(-1, CHUNK), TN).astype(BF16)
-        for k in range(FSDP):
-            R.ew_own[t, k // 2, k % 2] = piece[k * BS : (k + 1) * BS]
-        expand.start(t)
-
-    deep, tall = R.cw_done.shape[1:]
-
-    def contract_view(t, chips, core):
-        lanes = pl.ds(multiple(core, tall), tall)
-        if isinstance(chips, pl.Slice):
-            return R.hgrad.at[pl.ds(t * (FSDP // 2), FSDP // 2), :, lanes]
-        return R.hgrad.at[t * (FSDP // 2) + chips, :, lanes]
-
-    contract = Sum(
-        p, contract_view, R.cw_core, R.cw_chips, R.cw_total, R.cw_floors, R.cw_done,
-        ((R.cw_s0, R.cw_r0), (R.cw_s1, R.cw_r1), (R.cw_s2, R.cw_r2), (R.cw_s3, R.cw_r3)),
-    )
-    @pl.loop(0, 2)
-    def _(t):
-        @pl.loop(0, FSDP // 2)
-        def _(chip):
-            cols = pl.ds(multiple(chip, 2 * tall), 2 * tall)
-            piece = dot(R.msk[:, pl.ds(multiple(t, deep), deep)], R.hidden[:, cols], TN).astype(BF16)
-            R.hgrad[t * (FSDP // 2) + chip] = piece
-
-        contract.start(t)
-
-        @pl.when(t == 0)
+            sums.to_all(last - 3)
+            sums.to_chips(last - 1)
+            sums.to_floors(last - 2)
+
+        mlp_front(R, i, cols, *weights(last))
+
+    weight_gradients(last)
+
+    @pl.loop(0, blocks)
+    def _(i):
+        rows = pl.ds(multiple(i, CHUNK), CHUNK)
+        mlp_back(R, rows, R.hidden[rows, :], R.hgrad[rows, :], *weights(last))
+
+        @pl.when(i == 1)
         def _():
-            expand.to_chips(chunks - 1)
-            expand.to_all(chunks - 2)
-
-        @pl.when(t == 1)
-        def _():
-            contract.to_chips(0)
-
-    contract.to_chips(1)
+            sums.to_chips(last)
+            sums.to_floors(last - 1)
+            sums.to_all(last - 2)
 
     @pl.loop(0, slots)
     def _(slot):
         mixer_backward_first(R, slot)
         store(0, slot).start()
 
-        @pl.when(slot == 1)
+        @pl.when(slot == 2)
         def _():
-            expand.to_floors(chunks - 1)
+            sums.to_all(last - 1)
+
+        @pl.when(slot == 5)
+        def _():
+            sums.to_floors(last)
+
+    def put(first):
+        def write(j, value):
+            for side in range(2):
+                R.mix_own[2 * j + side, pl.ds(first, BS), :] = value[side * BS : (side + 1) * BS].astype(BF16)
+
+        return write
+
+    mixer_weight_gradients(R, put(0), put(BS))
+    mixing = Share(p, R.mix_own, R.mix_peers, R.mix_floors, ((R.mix_s0, R.mix_r0), (R.mix_s1, R.mix_r1)))
+    mixing.start()
+
+    def put_grad(slot, rows, value):
+        R.fg[rows, :] = value
+        store(1, slot).start()
+
+    @pl.loop(0, slots)
+    def _(slot):
+        mixer_backward_second(R, slot, put_grad)
 
         @pl.when(slot == 3)
         def _():
-            contract.to_floors(0)
-            expand.to_all(chunks - 1)
-
-        @pl.when(slot == 6)
-        def _():
-            contract.to_floors(1)
-            contract.to_all(0)
-
-    def put_inner(j, value):
-        for side in range(2):
-            R.mix_own[2 * j + side, pl.ds(0, BS), :] = value[side * BS : (side + 1) * BS].astype(BF16)
-
-    def put_outer(j, value):
-        for side in range(2):
-            R.mix_own[2 * j + side, pl.ds(BS, BS), :] = value[side * BS : (side + 1) * BS].astype(BF16)
-
-    mixer_weight_gradients(R, put_inner, put_outer)
-    mixing = Share(p, R.mix_own, R.mix_peers, R.mix_floors, ((R.mix_s0, R.mix_r0), (R.mix_s1, R.mix_r1)))
-    mixing.start()
-
-    def put(slot, rows, value):
-        R.fg[rows, :] = value
-        store(1, slot).start()
-
-    @pl.loop(0, slots)
-    def _(slot):
-        mixer_backward_second(R, slot, put)
-
-        @pl.when(slot == 4)
-        def _():
-            contract.to_all(1)
-            mixing.to_floors()
+            sums.to_all(last)
 
     pack_sums(R)
     vectors = Share(p, R.vec_own, R.vec_peers, R.vec_floors, ((R.vec_s0, R.vec_r0), (R.vec_s1, R.vec_r1)))
     vectors.start()
+    mixing.to_floors()
+    vectors.to_floors()
+    R.mix_ref[...] = mixing.finish()
     for t in range(chunks):
-        expand.finish(t)
-        R.ew_ref[:, t * CHUNK : (t + 1) * CHUNK] = R.ew_done[t].astype(F32)
-    for t in range(2):
-        contract.finish(t)
-        R.cw_ref[:, t * deep : (t + 1) * deep] = jnp.transpose(R.cw_done[t].astype(F32))
-    R.mix_ref[...] = mixing.finish()
-    vectors.to_floors()
+        sums.finish(t)
+    done_out = pltpu.make_async_copy(R.sum_done, R.done_ref, R.keep_sems.at[0])
+    done_out.start()
     R.vec_ref[...] = vectors.finish()
-    gather.sent()
     for k in range(1, FSDP):
         small_copy(k).wait_send()
-
-    @pl.loop(0, chunks)
-    def _(t):
-        expand.sent(t)
-
-    @pl.loop(0, 2)
-    def _(t):
-        contract.sent(t)
-
+    for t in range(chunks):
+        gather.sent(t)
+        sums.sent(t)
     mixing.sent()
     vectors.sent()
 
@@ -991,6 +980,8 @@
     def _(slot):
         store(0, slot).wait()
         store(1, slot).wait()
+
+    done_out.wait()
 
 
 def body_in_one(
@@ -1007,38 +998,35 @@
         items=slot_items, tok_in=tokens.reshape(n, WIDTH), cot_in=cotangent.reshape(n, WIDTH), table=jnp.asarray(TABLES, BF16),
         inner_in=inner_weight, outer_in=outer_weight, we_in=expand_weight, wc_in=contract_weight,
         fg_in=filter_gain[None], fs_in=filter_shift[None], ib_in=inner_bias[None], ob_in=outer_bias[None],
-        gg_in=feed_gain[None], gs_in=feed_shift[None], cb_in=contract_bias[None], eb_in=expand_bias[None],
-    )
-    in_specs = [{"items": SMEM, "tok_in": ANY, "cot_in": ANY}.get(key, VMEM) for key in ins]
+        gg_in=feed_gain[None], gs_in=feed_shift[None], cb_in=contract_bias[None], eb_in=expand_bias.reshape(2, 128),
+    )
+    places = dict.fromkeys(("tok_in", "cot_in", "out_ref", "grad_ref", "done_ref"), ANY)
+    places["items"] = SMEM
     outs = dict(
-        out_ref=((n, WIDTH), BF16), grad_ref=((n, WIDTH), F32), ew_ref=((deep, hidden), F32), cw_ref=((tall, WIDTH), F32),
+        out_ref=((n, WIDTH), BF16), grad_ref=((n, WIDTH), F32), done_ref=((chunks, deep, 2 * CHUNK), BF16),
         mix_ref=((2 * BS, 2 * BS), F32), vec_ref=((8, 128), F32),
     )
-    out_specs = [{"out_ref": ANY, "grad_ref": ANY}.get(key, VMEM) for key in outs]
     wide, flat, full = ((n, 2 * WIDTH), BF16), ((n, WIDTH), BF16), ((n, WIDTH), F32)
     pairs, sums = ((2 * WIDTH, 4 * BS), BF16), ((40, WIDTH), F32)
+    both = 2 * CHUNK
     memory = dict(
         tok=flat, msk=flat, spec=wide, act=wide, slope=wide, bent=wide, mid=full, feed=flat, br=full, fg=full,
-        hidden=((n, hidden), BF16), hgrad=((n // PATCHES, PATCHES, CHUNK), BF16), we=((WIDTH, hidden), BF16), wc=((hidden, WIDTH), BF16),
+        hidden=((n, CHUNK), BF16), hgrad=((n, CHUNK), BF16), w=((chunks, FSDP, deep, both), BF16),
         win=pairs, wout=pairs, vec=((16, WIDTH), F32), be=((8, hidden), F32), stats=sums, sums=sums,
         dbias=((16, 2 * WIDTH), F32), dbe=((8, hidden), F32),
         small=((144, 128), BF16), smalls=((FSDP, 144, 128), BF16),
-        ew_own=((chunks, 4, 2, deep, CHUNK), BF16), ew_core=((chunks, 4, deep, CHUNK), BF16),
-        ew_chips=((chunks, 3, deep, CHUNK), BF16), ew_total=((chunks, deep, CHUNK), BF16),
-        ew_floors=((chunks, floors, deep // copies, CHUNK), BF16), ew_done=((chunks, deep, CHUNK), BF16),
-        cw_core=((2, 4, WIDTH // 2, tall), BF16),
-        cw_chips=((2, 3, WIDTH // 2, tall), BF16), cw_total=((2, WIDTH // 2, tall), BF16),
-        cw_floors=((2, floors, WIDTH // 2 // copies, tall), BF16), cw_done=((2, WIDTH // 2, tall), BF16),
+        sum_own=((chunks, 4, 2, deep, both), BF16), sum_core=((chunks, 4, deep, both), BF16),
+        sum_chips=((chunks, 3, deep, both), BF16), sum_total=((chunks, deep, both), BF16),
+        sum_floors=((chunks, floors, deep // copies, both), BF16), sum_done=((chunks, deep, both), BF16),
         mix_own=((FSDP, 128, 128), BF16), mix_peers=((FSDP - 1, 128, 128), BF16), mix_floors=((copies, 128, 128), BF16),
         vec_own=((FSDP, 8, 128), F32), vec_peers=((FSDP - 1, 8, 128), F32), vec_floors=((copies, 8, 128), F32),
     )
     sems = dict(
-        load_sems=(2, slots), store_sems=(2, slots), small_send=(7,), small_recv=(7,),
-        gather_send=(3, 8, 4), gather_recv=(3, 8),
-    )
-    for key, parts in (("ew", chunks), ("cw", 2)):
-        for step, shape in enumerate(((parts,), (parts, 3), (parts, floors), (parts, floors))):
-            sems[f"{key}_s{step}"] = sems[f"{key}_r{step}"] = shape
+        load_sems=(2, slots), store_sems=(2, slots), small_send=(7,), small_recv=(7,), keep_sems=(1,),
+        gather_send=(chunks, 8, 4), gather_recv=(chunks, 8),
+    )
+    for step, shape in enumerate(((chunks,), (chunks, 3), (chunks, floors), (chunks, floors))):
+        sems[f"sum_s{step}"] = sems[f"sum_r{step}"] = shape
     for key in ("mix", "vec"):
         for step, shape in enumerate(((FSDP - 1,), (floors,))):
             sems[f"{key}_s{step}"] = sems[f"{key}_r{step}"] = shape
@@ -1055,8 +1043,8 @@
             pl.pallas_call(
                 kernel,
                 out_shape=[jax.ShapeDtypeStruct(*spec) for spec in outs.values()],
-                in_specs=in_specs,
-                out_specs=out_specs,
+                in_specs=[places.get(key, VMEM) for key in ins],
+                out_specs=[places.get(key, VMEM) for key in outs],
                 scratch_shapes=[pltpu.VMEM(*spec) for spec in memory.values()]
                 + [pltpu.SemaphoreType.DMA(shape) for shape in sems.values()],
                 compiler_params=pltpu.CompilerParams(vmem_limit_bytes=ROOM, collective_id=0, has_side_effects=True),
@@ -1064,12 +1052,78 @@
             )(*ins.values()),
         )
     )
-    vec = o["vec_ref"]
-    return (
-        o["out_ref"].reshape(tokens.shape), o["grad_ref"].reshape(tokens.shape), vec[0, :BS], vec[0, BS:], o["mix_ref"][:BS],
-        vec[1], o["mix_ref"][BS:], vec[2], vec[3, :BS], vec[3, BS:], o["ew_ref"], vec[5:7].reshape(-1), o["cw_ref"],
-        vec[4, :BS], jnp.sqrt(vec[7, :5] / vec[7, 5]),
-    )
+    return finishing(tokens.shape, o, deep, hidden, tall)
+
+
+PIECES = 8
+
+
+def finishing(shape, o, deep, hidden, tall):
+    ends = dict(
+        out=(o["out_ref"].shape, BF16), grad=(o["grad_ref"].shape, F32), fg=((1, BS), F32), fs=((1, BS), F32),
+        inner=((BS, 2 * BS), F32), ib=((1, 128), F32), outer=((BS, 2 * BS), F32), ob=((1, 128), F32), gg=((1, BS), F32),
+        gs=((1, BS), F32), ew=((deep, hidden), F32), eb=((2, 128), F32), cw=((tall, WIDTH), F32), cb=((1, BS), F32),
+        stat=((1, 5), F32),
+    )
+    names = list(o) + list(ends) + ["grad_held", "out_held", "sems"]
+
+    def kernel(*refs):
+        R = named(names, refs)
+        ways = []
+        for which, (src, held, dst) in enumerate(((R.grad_ref, R.grad_held, R.grad), (R.out_ref, R.out_held, R.out))):
+            size = src.shape[0] // PIECES
+            for i in range(PIECES):
+                rows = pl.ds(i * size, size)
+                ways.append(
+                    (
+                        pltpu.make_async_copy(src.at[rows], held.at[rows], R.sems.at[0, which, i]),
+                        pltpu.make_async_copy(held.at[rows], dst.at[rows], R.sems.at[1, which, i]),
+                    )
+                )
+        for come, _ in ways:
+            come.start()
+        for come, go in ways:
+            come.wait()
+            go.start()
+        chunks, deep = R.done_ref.shape[:2]
+        for t in range(0, chunks, 2):
+            for m in range(CHUNK // 128):
+                low, high = [R.done_ref[t + side, :, 128 * m : 128 * m + 128].astype(F32) for side in range(2)]
+                at = m * 4 * chunks * BS // 2 + t * BS
+                for side, part in enumerate(interleave(low, high)):
+                    R.ew[:, at + side * chunks * BS : at + side * chunks * BS + 128] = part
+        for t in range(chunks):
+            R.cw[pl.ds(t * deep, deep), :] = R.done_ref[t, :, CHUNK:].astype(F32)
+        R.inner[...], R.outer[...] = R.mix_ref[:BS], R.mix_ref[BS:]
+        vec = R.vec_ref[...]
+        R.fg[...], R.fs[...] = vec[0:1, :BS], vec[0:1, BS:]
+        R.ib[...], R.ob[...] = vec[1:2], vec[2:3]
+        R.gg[...], R.gs[...] = vec[3:4, :BS], vec[3:4, BS:]
+        R.cb[...], R.eb[...] = vec[4:5, :BS], vec[5:7]
+        lane = lax.broadcasted_iota(jnp.int32, (1, 128), 1)
+        total = jnp.sum(jnp.where(lane == 5, vec[7:8], 0.0), axis=1, keepdims=True)
+        R.stat[...] = jnp.sqrt(vec[7:8] / total)[:, :5]
+        for _, go in ways:
+            go.wait()
+
+    places = dict.fromkeys(("out_ref", "grad_ref", "out", "grad"), ANY)
+    values = pl.pallas_call(
+        kernel,
+        out_shape=[jax.ShapeDtypeStruct(*spec) for spec in ends.values()],
+        in_specs=[places.get(key, VMEM) for key in o],
+        out_specs=[places.get(key, VMEM) for key in ends],
+        scratch_shapes=[
+            pltpu.VMEM(o["grad_ref"].shape, F32), pltpu.VMEM(o["out_ref"].shape, BF16), pltpu.SemaphoreType.DMA((2, 2, PIECES)),
+        ],
+        compiler_params=pltpu.CompilerParams(vmem_limit_bytes=ROOM),
+        name="finishing",
+    )(*o.values())
+    e = dict(zip(ends, values))
+    for key in ("out", "grad"):
+        e[key] = e[key].reshape(shape)
+    for key in ("fg", "fs", "ib", "ob", "gg", "gs", "eb", "cb", "stat"):
+        e[key] = e[key].reshape(-1)
+    return tuple(e.values())
 
 
 def solution(mesh):

time: 126 us -> 102 us (0.81)
  local copies, waits for them, and re-layouts: 14.6 us -> 0 us
  Pallas kernels: 108 us -> 101 us
  other arithmetic: 1.84 us -> 0 us
    pallas_call x1, Pallas kernels: 108 us -> 93.5 us  [body_in_one(): pl.pallas_call(kernel, out_shape=[jax.ShapeDtypeStruct(*spec) for spec in...]
    pallas_call x0 -> x1, Pallas kernels: none -> 7.63 us  [finishing(): pl.pallas_call(kernel, out_shape=[jax.ShapeDtypeStruct(*spec) for spec in...]
    unnamed x10 -> x0, local copies, waits for them, and re-layouts: 6.81 us -> none
    squeeze x2 -> x0, local copies, waits for them, and re-layouts: 2.72 us -> none  [the longest x1 1.45 us: body_in_one(): vec[4, :BS]]
    slice x2 -> x0, local copies, waits for them, and re-layouts: 2.66 us -> none  [the longest x1 1.4 us: body_in_one(): o['mix_ref'][BS:]]
    sqrt x1 -> x0, other arithmetic: 1.84 us -> none  [body_in_one(): jnp.sqrt(vec[7, :5] / vec[7, 5])]
where the time goes in v3:
time: 102 us
  Pallas kernels  101 us (99%)
    pallas_call x1, Pallas kernels, body_in_one(): pl.pallas_call(kernel, out_shape=[jax.ShapeDtypeStruct(*spec) for spec in...  93.5 us
    pallas_call x1, Pallas kernels, finishing(): pl.pallas_call(kernel, out_shape=[jax.ShapeDtypeStruct(*spec) for spec in...  7.63 us

profile of v3, /device:TPU:0, one launch (start us, length us, event | category | flops | bytes accessed | tf_op | source)
XLA Modules:
  0.0 101.9 jit_solution(6971107141123997071)
XLA Ops:
  0.7 93.5 %mega.1 = (bf16[2048,512]{1,0:T(8,128)(2,1)}, f32[2048,512]{1,0:T(8,128)}, bf16[4,64,1024]{2,1,0:T(8,128)(2,1)}, f32[128,128]{1,0:T(8,128)}, f32[8,128]{1,0:T(8,128)}) custom-call(s32[8]{0:T(128)} %refs_0_.1, bf16[2048,512]{1,0:T(8,128)(2,1)} %bitcast.21, bf16[2048,512]{1,0:T(8,128)(2,1)} %bitcast.22, bf16[512,256]{1,0:T(8,128)(2,1)} %constant.2.clone.refs_3_, ...), custom_call_target="tpu_custom_call" | custom-call | tf_op jit(solution)/shard_map/mega/pallas_call | solution.py:1043
  94.1 7.6 %finishing.1 = (bf16[2048,512]{1,0:T(8,128)(2,1)}, f32[2048,512]{1,0:T(8,128)}, f32[1,64]{1,0:T(1,128)}, f32[1,64]{1,0:T(1,128)}, f32[64,128]{1,0:T(8,128)}, /*i...) custom-call(bf16[2048,512]{1,0:T(8,128)(2,1)} %get-tuple-element.35., ...), custom_call_target="tpu_custom_call" | custom-call | tf_op jit(solution)/shard_map/finishing/pallas_call | solution.py:1110

commit v4 on v3

v4 whole, which is shorter than its diff:
```python
import functools
import math

import jax
import jax.numpy as jnp
import numpy as np
from jax import lax
from jax.experimental import pallas as pl
from jax.experimental.pallas import tpu as pltpu
from jax.sharding import PartitionSpec as P

BS = 64
NB = 8
SIDE = 16
PATCHES = SIDE * SIDE
WIDTH = NB * BS
HALF = PATCHES // 2
TAIL = 16
PAIRS = NB // 2
CHUNK = 512
EPSILON = 1e-05
SHRINK = 0.25
F32 = jnp.float32
BF16 = jnp.bfloat16
NT = (((1,), (1,)), ((), ()))
TN = (((0,), (0,)), ((), ()))
TABLE_SCALE = 1.132805


def frequency_order(side):
    pairs, selfs = [], []
    for a in range(side):
        for b in range(side):
            other = ((-a) % side, (-b) % side)
            if other == (a, b):
                selfs.append((a, b))
            elif (a, b) < other:
                pairs.append((a, b))
    return pairs, selfs


def spectrum_table(side):
    tiles = SIDE // side
    pairs, selfs = frequency_order(side)
    row = np.arange(PATCHES) // SIDE
    col = np.arange(PATCHES) % SIDE
    top, bottom = [], []
    for kind in ("pair", "self"):
        for qr in range(tiles):
            for qc in range(tiles):
                inside = (row // side == qr) & (col // side == qc)
                listed = pairs if kind == "pair" else selfs
                for at, (a, b) in enumerate(listed):
                    angle = 2.0 * math.pi / side * ((a * row + b * col) % side)
                    if kind == "pair":
                        top.append(np.where(inside, np.cos(angle), 0.0) / side)
                        bottom.append(np.where(inside, -np.sin(angle), 0.0) / side)
    extra = []
    for at in range(len(selfs)):
        for qr in range(tiles):
            for qc in range(tiles):
                inside = (row // side == qr) & (col // side == qc)
                a, b = selfs[at]
                angle = 2.0 * math.pi / side * ((a * row + b * col) % side)
                extra.append(np.where(inside, np.cos(angle), 0.0) / side)
    half = len(extra) // 2
    return np.array(top + extra[:half] + bottom + extra[half:]), len(top), tiles * tiles


WHOLE_TABLE, WHOLE_PAIRS, WHOLE_ZEROS = spectrum_table(SIDE)
PART_TABLE, PART_PAIRS, PART_ZEROS = spectrum_table(SIDE // 2)
TABLES = np.concatenate([WHOLE_TABLE * TABLE_SCALE, PART_TABLE], axis=0)


def dot(a, b, dims=(((1,), (0,)), ((), ()))):
    return lax.dot_general(a, b, dims, preferred_element_type=F32)


def sum8(values):
    return jnp.sum(values.reshape(-1, 8, values.shape[-1]), axis=0)


def gelu_and_slope(v):
    phi = 0.5 * lax.erf(v * 0.7071067811865476) + 0.5
    bell = jnp.exp2(v * v * (-0.5 / math.log(2.0))) * (1.0 / math.sqrt(2.0 * math.pi))
    return v * phi, phi + v * bell


def row_stats(values):
    mean = jnp.mean(values, axis=-1, keepdims=True)
    centre = values - mean
    spread = jnp.mean(centre * centre, axis=-1, keepdims=True)
    scale = lax.rsqrt(spread + EPSILON)
    return centre * scale, scale, spread + mean * mean


def turns(*steps):
    left = list(steps)
    while left:
        for step in list(left):
            if next(step, None) is None:
                left.remove(step)
        yield True


def run(*steps):
    for _ in turns(*steps):
        pass


def chain(*steps):
    for step in steps:
        yield from step


def weave(first, count, second):
    ended = False
    while not ended:
        for _ in range(count):
            if next(first, None) is None:
                ended = True
        next(second, None)
    for _ in second:
        pass


def kind_of(R, slot, lanes=WIDTH):
    return jnp.full((1, lanes), R.items[slot], jnp.int32)


def slot_facts(kind):
    whole = kind == 0
    pairs = jnp.where(whole, WHOLE_PAIRS, PART_PAIRS)
    scale = jnp.where(whole, 1.0 / TABLE_SCALE, 1.0).astype(F32)
    return whole, pairs, scale


def table_of(R, kind):
    whole = jnp.where(kind[:, :PATCHES] == 0, 1.0, 0.0).astype(F32)
    first, second = whole.astype(BF16), (1.0 - whole).astype(BF16)
    return R.table[pl.ds(0, PATCHES), :] * first + R.table[pl.ds(PATCHES, PATCHES), :] * second


def tail_pairs(pairs, lanes):
    row = lax.broadcasted_iota(jnp.int32, (TAIL, lanes), 0) + (HALF - TAIL)
    return row < pairs[:, :lanes]


def spread(halves, pairs):
    head = HALF - TAIL
    is_pair = tail_pairs(pairs, halves.shape[1])
    top, bottom = halves[:HALF], halves[HALF:]
    low_imag = jnp.where(is_pair, bottom[head:], 0.0)
    low_real = jnp.where(is_pair, top[head:], bottom[head:])
    imag = jnp.concatenate([bottom[:head], low_imag], axis=0)
    return top, imag, jnp.concatenate([top[:head], low_real], axis=0)


def fold(block, pairs):
    head = HALF - TAIL
    is_pair = tail_pairs(pairs, 128)
    ra, ia = block[:HALF, :128], block[:HALF, 128:]
    rb, ib = block[HALF:, :128], block[HALF:, 128:]
    top = [ra[:head] + rb[:head], ra[head:] + jnp.where(is_pair, rb[head:], 0.0)]
    bottom = [ia[:head] - ib[:head], jnp.where(is_pair, ia[head:] - ib[head:], rb[head:])]
    return jnp.concatenate(top, axis=0), jnp.concatenate(bottom, axis=0)


def interleave(first, second):
    low = lax.broadcasted_iota(jnp.int32, first.shape, 1) < BS
    return (
        jnp.where(low, first, pltpu.roll(second, BS, 1)),
        jnp.where(low, pltpu.roll(first, BS, 1), second),
    )


def complex_pairs(weight_ref, out_ref, up_ref=None):
    low = lax.broadcasted_iota(jnp.int32, (BS, 128), 1) < BS
    for j in range(PAIRS):
        first, second = weight_ref[2 * j].astype(F32), weight_ref[2 * j + 1].astype(F32)
        real = jnp.concatenate([jnp.where(low, first, 0.0), jnp.where(low, 0.0, pltpu.roll(second, BS, 1))], axis=0)
        imag = jnp.concatenate([jnp.where(low, pltpu.roll(first, BS, 1), 0.0), jnp.where(low, 0.0, second)], axis=0)
        matrix = jnp.concatenate(
            [jnp.concatenate([real, imag], axis=1), jnp.concatenate([-imag, real], axis=1)], axis=0
        )
        out_ref[pl.ds(256 * j, 256), :] = matrix.astype(BF16)
        if up_ref is not None:
            up_ref[pl.ds(256 * j, 256), :] = (matrix * (1.0 / SHRINK)).astype(BF16)


def pair_gradient(product):
    real = product[:128, :128] + product[128:, 128:]
    imag = product[:128, 128:] - product[128:, :128]
    low = lax.broadcasted_iota(jnp.int32, (BS, 128), 1) < BS
    first = jnp.where(low, real[:BS], pltpu.roll(imag[:BS], BS, 1))
    second = jnp.where(low, pltpu.roll(real[BS:], BS, 1), imag[BS:])
    return jnp.concatenate([first, second], axis=0)


def masked_squares(values, kind):
    squares = values * values
    parts = jnp.sum(squares.reshape(2, 8, 2, 8, squares.shape[-1]), axis=1)
    total = parts[0, 0]
    for q in range(1, 4):
        valid = jnp.where((kind == 0) | (q < kind), 1.0, 0.0).astype(F32)
        total = total + valid * parts[q // 2, q % 2]
    return total


def quadrant_of(shape):
    position = lax.broadcasted_iota(jnp.int32, shape, 0)
    return (position >> 7) * 2 + ((position >> 3) & 1)


def masked(values, kind):
    kind = kind[:, : values.shape[1]]
    return jnp.where((kind == 0) | (quadrant_of(values.shape) < kind), values, 0.0)


def add_mean_squares(R, at, means, kind):
    R.stats[pl.ds(at, 8), 0:1] += sum8(masked(means, kind)) * float(WIDTH)


def mixer_start(R, slot):
    kind = kind_of(R, slot)
    whole, pairs, scale = slot_facts(kind)
    rows = pl.ds(pl.multiple_of(slot * PATCHES, PATCHES), PATCHES)
    x = R.tok[rows, :].astype(F32)
    xhat, _, means = row_stats(x)
    add_mean_squares(R, 0, means, kind)
    R.mid[rows, :] = dot(table_of(R, kind), xhat.astype(BF16))
    grad = masked(R.cot[rows, :].astype(F32), kind)
    R.sums[pl.ds(16, 8), :] += sum8(grad)
    R.msk[rows, :] = grad.astype(BF16)


def mixer_forward(R, slot):
    kind = kind_of(R, slot)
    whole, pairs, scale = slot_facts(kind)
    rows = pl.ds(pl.multiple_of(slot * PATCHES, PATCHES), PATCHES)
    spec = R.mid[rows, :] * (R.vec[0:1, :] * scale)
    row = lax.broadcasted_iota(jnp.int32, (TAIL, WIDTH), 0) + (HALF - TAIL)
    at_zero = (row >= pairs) & (row < pairs + jnp.where(whole, WHOLE_ZEROS, PART_ZEROS))
    shift = R.vec[1:2, :] * jnp.where(whole, float(SIDE), float(SIDE // 2)).astype(F32)
    zeros = spec[HALF - TAIL : HALF] + jnp.where(at_zero, shift, 0.0)
    spec = jnp.concatenate([spec[: HALF - TAIL], zeros, spec[HALF:]], axis=0)
    ra, ia, rb = [part.astype(BF16) for part in spread(spec, pairs)]
    tops, bottoms = [], []
    for j in range(PAIRS):
        lanes = slice(256 * j, 256 * j + 256)
        cols = slice(128 * j, 128 * j + 128)
        low = jnp.concatenate(
            [
                jnp.concatenate([ra[:, cols], ia[:, cols]], axis=1),
                jnp.concatenate([rb[:, cols], -ia[:, cols]], axis=1),
            ],
            axis=0,
        )
        R.spec[rows, lanes] = low
        yield True
        pre = dot(low, R.win[pl.ds(256 * j, 256), :]) + jnp.concatenate([R.vec[2:3, cols], R.vec[3:4, cols]], axis=1)
        act, slope = gelu_and_slope(pre)
        act = act.astype(BF16)
        R.act[rows, lanes] = act
        R.slope[rows, lanes] = slope.astype(BF16)
        yield True
        post = dot(act, R.wout_up[pl.ds(256 * j, 256), :]) + jnp.concatenate(
            [R.vec[4:5, cols], R.vec[5:6, cols]], axis=1
        )
        bent = jnp.tanh(post)
        R.bent[rows, lanes] = (bent * bent).astype(BF16)
        u, v = fold(post - bent, pairs)
        tops.append(u.astype(BF16))
        bottoms.append(v.astype(BF16))
    yield True
    folded = jnp.concatenate([jnp.concatenate(tops, axis=1), jnp.concatenate(bottoms, axis=1)], axis=0)
    mixer_out = dot(table_of(R, kind), folded, TN) * (scale * SHRINK)
    R.stats[pl.ds(8, 8), :] += masked_squares(mixer_out, kind)
    middle = R.tok[rows, :].astype(F32) + mixer_out
    R.mid[rows, :] = middle
    yield True
    yhat, _, means = row_stats(middle)
    add_mean_squares(R, 16, means, kind)
    R.feed[rows, :] = (yhat * R.vec[6:7, :] + R.vec[7:8, :]).astype(BF16)
    yield True


def mlp_front(R, i, cols, we, wc):
    rows = pl.ds(pl.multiple_of(i * CHUNK, CHUNK), CHUNK)
    hidden, slope = gelu_and_slope(dot(R.feed[rows, :], we) + R.be[0:1, cols])
    hidden = hidden.astype(BF16)
    R.hidden[rows, :] = hidden
    yield True
    back = dot(R.msk[rows, :], wc, NT) * slope
    R.dbe[:, cols] += sum8(back)
    back = back.astype(BF16)
    R.hgrad[rows, :] = back
    yield True


def mlp_back(R, i, we, wc, first=False):
    rows = pl.ds(pl.multiple_of(i * CHUNK, CHUNK), CHUNK)
    branch = dot(R.hidden[rows, :], wc)
    R.br[rows, :] = branch if first else R.br[rows, :] + branch
    yield True
    grad = dot(R.hgrad[rows, :], we, NT)
    R.fg[rows, :] = grad if first else R.fg[rows, :] + grad
    yield True


def mlp_chunk(R, i, cols, we, wc, first=False):
    return chain(mlp_front(R, i, cols, we, wc), mlp_back(R, i, we, wc, first))


def mixer_backward_first(R, slot):
    kind = kind_of(R, slot)
    whole, pairs, scale = slot_facts(kind)
    rows = pl.ds(pl.multiple_of(slot * PATCHES, PATCHES), PATCHES)
    feed_grad = R.fg[rows, :]
    yhat, yscale, _ = row_stats(R.mid[rows, :])
    R.sums[pl.ds(0, 8), :] += sum8(feed_grad * yhat)
    R.sums[pl.ds(8, 8), :] += sum8(feed_grad)
    scaled = feed_grad * R.vec[6:7, :]
    yield True
    inner = scaled - jnp.mean(scaled, axis=-1, keepdims=True) - yhat * jnp.mean(scaled * yhat, axis=-1, keepdims=True)
    mgrad = R.msk[rows, :].astype(F32) + inner * yscale
    R.mgrad[rows, :] = mgrad
    yield True
    ra_all, ia_all, rb_all = spread(dot(table_of(R, kind), mgrad.astype(BF16)) * scale, pairs)
    for j in range(PAIRS):
        lanes = slice(256 * j, 256 * j + 256)
        cols = slice(128 * j, 128 * j + 128)
        ra, ia, rb = ra_all[:, cols], ia_all[:, cols], rb_all[:, cols]
        grad = jnp.concatenate([jnp.concatenate([ra, ia], axis=1), jnp.concatenate([rb, -ia], axis=1)], axis=0)
        grad = grad * R.bent[rows, lanes].astype(F32)
        R.dbias[pl.ds(0, 8), lanes] += sum8(grad)
        grad = grad.astype(BF16)
        R.dmix[1, j] += dot(R.act[rows, lanes], grad, TN)
        yield True
        grad = dot(grad, R.wout[pl.ds(256 * j, 256), :], NT) * R.slope[rows, lanes].astype(F32)
        R.dbias[pl.ds(8, 8), lanes] += sum8(grad)
        grad = grad.astype(BF16)
        R.igrad[rows, lanes] = grad
        R.dmix[0, j] += dot(R.spec[rows, lanes], grad, TN)
        yield True


def block_result(R, slot):
    kind = kind_of(R, slot)
    rows = pl.ds(pl.multiple_of(slot * PATCHES, PATCHES), PATCHES)
    branch = R.br[rows, :] + R.vec[8:9, :]
    result = R.mid[rows, :] + branch
    R.stats[pl.ds(24, 8), :] += masked_squares(branch, kind)
    R.stats[pl.ds(32, 8), :] += masked_squares(result, kind)
    R.out[rows, :] = result.astype(BF16)
    yield True


def mixer_weight_gradients(R, put):
    for j in range(PAIRS):
        for which in range(2):
            put(which, j, pair_gradient(R.dmix[which, j]))


def mixer_backward_second(R, slot):
    kind = kind_of(R, slot)
    whole, pairs, scale = slot_facts(kind)
    rows = pl.ds(pl.multiple_of(slot * PATCHES, PATCHES), PATCHES)
    tops, bottoms = [], []
    for j in range(PAIRS):
        lanes = slice(256 * j, 256 * j + 256)
        u, v = fold(dot(R.igrad[rows, lanes], R.win[pl.ds(256 * j, 256), :], NT), pairs)
        tops.append(u.astype(BF16))
        bottoms.append(v.astype(BF16))
        yield True
    folded = jnp.concatenate([jnp.concatenate(tops, axis=1), jnp.concatenate(bottoms, axis=1)], axis=0)
    ngrad = dot(table_of(R, kind), folded, TN) * scale
    R.ngrad[rows, :] = ngrad
    xhat, _, _ = row_stats(R.tok[rows, :].astype(F32))
    yield True
    R.sums[pl.ds(24, 8), :] += sum8(ngrad * xhat)
    R.sums[pl.ds(32, 8), :] += sum8(ngrad)
    yield True


def norm_backward(R, slot):
    rows = pl.ds(pl.multiple_of(slot * PATCHES, PATCHES), PATCHES)
    xhat, xscale, _ = row_stats(R.tok[rows, :].astype(F32))
    scaled = R.ngrad[rows, :] * R.vec[0:1, :]
    yield True
    inner = scaled - jnp.mean(scaled, axis=-1, keepdims=True) - xhat * jnp.mean(scaled * xhat, axis=-1, keepdims=True)
    R.igrad_out[rows, :] = R.mgrad[rows, :] + inner * xscale
    yield True

class Refs:
    pass


VMEM = pl.BlockSpec(memory_space=pltpu.VMEM)
SMEM = pl.BlockSpec(memory_space=pltpu.SMEM)
ROOM = 127 * 2**19


def named(names, refs):
    R = Refs()
    for name, ref in zip(names, refs):
        setattr(R, name, ref)
    return R


def plain_call(body, ins, outs, scratch, name):
    names = list(ins) + list(outs) + list(scratch)

    def kernel(*refs):
        body(named(names, refs))

    values = pl.pallas_call(
        kernel,
        out_shape=[jax.ShapeDtypeStruct(*spec) for spec in outs.values()],
        in_specs=[SMEM if key == "items" else VMEM for key in ins],
        out_specs=[VMEM for _ in outs],
        scratch_shapes=[pltpu.VMEM(*spec) for spec in scratch.values()],
        compiler_params=pltpu.CompilerParams(vmem_limit_bytes=ROOM),
        name=name,
    )(*ins.values())
    return dict(zip(outs, values))


def forward_body(R):
    complex_pairs(R.inner, R.win)
    complex_pairs(R.outer, R.wout, R.wout_up)
    R.stats[...] = jnp.zeros_like(R.stats)
    R.sums[...] = jnp.zeros_like(R.sums)

    @pl.loop(0, R.tok.shape[0] // PATCHES)
    def _(slot):
        mixer_start(R, slot)
        run(mixer_forward(R, slot))


def mlp_body(R):
    R.dbe[...] = jnp.zeros_like(R.dbe)
    R.br[...] = jnp.zeros_like(R.br)
    R.fg[...] = jnp.zeros_like(R.fg)

    @pl.loop(0, R.we.shape[1] // CHUNK)
    def _(t):
        cols = pl.ds(pl.multiple_of(t * CHUNK, CHUNK), CHUNK)

        @pl.loop(0, R.feed.shape[0] // CHUNK)
        def _(i):
            run(mlp_chunk(R, i, cols, R.we[:, cols], R.wc[cols, :]))

        R.dwe[:, cols] = dot(R.feed[...], R.hgrad[...], TN).astype(BF16)
        R.dwc[:, cols] = dot(R.msk[...], R.hidden[...], TN).astype(BF16)


def backward_body(R):
    R.stats[...] = jnp.zeros_like(R.stats)
    R.sums[...] = jnp.zeros_like(R.sums)
    R.dbias[...] = jnp.zeros_like(R.dbias)
    R.dmix[...] = jnp.zeros_like(R.dmix)
    slots = R.tok.shape[0] // PATCHES

    @pl.loop(0, slots)
    def _(slot):
        run(block_result(R, slot), mixer_backward_first(R, slot))

    def put_mix(which, j, value):
        (R.dinner, R.douter)[which][pl.ds(128 * j, 128), :] = value

    mixer_weight_gradients(R, put_mix)

    @pl.loop(0, slots)
    def _(slot):
        run(chain(mixer_backward_second(R, slot), norm_backward(R, slot)))


def pair_order(vector):
    parts = vector.reshape(NB, 2, BS)
    return parts[:, 0].reshape(1, WIDTH), parts[:, 1].reshape(1, WIDTH)


def body_by_collectives(
    tokens, cotangent, slot_items, filter_gain, filter_shift, inner_weight, inner_bias, outer_weight, outer_bias,
    feed_gain, feed_shift, expand_weight, expand_bias, contract_weight, contract_bias,
):
    def gather(x):
        return lax.all_gather(x, "fsdp", axis=0, tiled=True)

    vectors = (filter_gain, filter_shift, inner_bias, outer_bias, feed_gain, feed_shift, contract_bias, expand_bias)
    sizes = [v.shape[0] for v in vectors]
    packed = lax.all_gather(jnp.concatenate(vectors), "fsdp", axis=0)
    ends = np.cumsum([0] + sizes)
    g1, s1, bi, bo, g2, s2, bc, be = [packed[:, a:b].reshape(-1).astype(F32) for a, b in zip(ends, ends[1:])]
    vec = jnp.concatenate(
        [g1[None], s1[None], *pair_order(bi), *pair_order(bo / SHRINK), g2[None], s2[None], bc[None], jnp.zeros((7, WIDTH), F32)]
    )
    inner, outer, we, wc = gather(inner_weight), gather(outer_weight), gather(expand_weight), gather(contract_weight)
    n = tokens.shape[0] * PATCHES
    hidden = we.shape[1]
    tok, cot = tokens.reshape(n, WIDTH), cotangent.reshape(n, WIDTH)
    table = jnp.asarray(TABLES, BF16)
    wide = ((n, 2 * WIDTH), BF16)
    flat = ((n, WIDTH), BF16)
    full = ((n, WIDTH), F32)
    pairs = ((2 * WIDTH, 2 * 2 * BS), BF16)
    sums = ((40, WIDTH), F32)
    a = plain_call(
        forward_body,
        dict(items=slot_items, tok=tok, cot=cot, table=table, vec=vec, inner=inner.reshape(NB, BS, 2 * BS), outer=outer.reshape(NB, BS, 2 * BS)),
        dict(spec=wide, act=wide, slope=wide, bent=wide, mid=full, feed=flat, msk=flat, win=pairs, wout=pairs, stats=sums, sums=sums),
        dict(wout_up=pairs),
        "mixer_forward",
    )
    b = plain_call(
        mlp_body,
        dict(feed=a["feed"], msk=a["msk"], we=we, wc=wc, be=be.reshape(1, hidden)),
        dict(br=full, fg=full, dwe=((WIDTH, hidden), BF16), dwc=((WIDTH, hidden), BF16), dbe=((8, hidden), F32)),
        dict(hidden=((n, CHUNK), BF16), hgrad=((n, CHUNK), BF16)),
        "mlp",
    )
    c = plain_call(
        backward_body,
        dict(
            items=slot_items, tok=tok, table=table, vec=vec, spec=a["spec"], act=a["act"], slope=a["slope"], bent=a["bent"],
            mid=a["mid"], msk=a["msk"], br=b["br"], fg=b["fg"], win=a["win"], wout=a["wout"],
        ),
        dict(
            out=flat, igrad_out=full, dinner=((WIDTH, 2 * BS), F32), douter=((WIDTH, 2 * BS), F32),
            dbias=((16, 2 * WIDTH), F32), sums=sums, stats=sums,
        ),
        dict(mgrad=full, igrad=wide, ngrad=full, dmix=((2, PAIRS, 256, 256), F32)),
        "mixer_backward",
    )

    def scatter(x):
        return lax.psum_scatter(x, "fsdp", scatter_dimension=0, tiled=True)

    def rows_of(x, at):
        return jnp.sum(x[at : at + 8], axis=0)

    def bias_of(at):
        parts = rows_of(c["dbias"], at).reshape(PAIRS, 2, 2, BS)
        return jnp.swapaxes(parts, 1, 2).reshape(2 * WIDTH)

    sums_ = a["sums"] + c["sums"]
    stats_ = a["stats"] + c["stats"]
    small = [
        rows_of(sums_, 24), rows_of(sums_, 32), bias_of(8), bias_of(0), rows_of(sums_, 0), rows_of(sums_, 8),
        rows_of(sums_, 16), jnp.sum(b["dbe"], axis=0),
    ]
    fsdp = lax.axis_size("fsdp")
    small = jnp.concatenate([v.reshape(fsdp, -1) for v in small], axis=1)
    weights = jnp.concatenate([c["dinner"].reshape(fsdp, -1), c["douter"].reshape(fsdp, -1)], axis=1)
    weights = jnp.concatenate([weights, small], axis=1).astype(BF16)
    own_small = scatter(weights.reshape(-1))
    own_we = scatter(b["dwe"])
    own_wc = scatter(b["dwc"].T)
    own_small, own_we, own_wc = lax.psum((own_small, own_we, own_wc), "rep")
    own_small = own_small.astype(F32)
    cut = inner_weight.size
    own_iw, own_ow = own_small[:cut].reshape(inner_weight.shape), own_small[cut : 2 * cut].reshape(inner_weight.shape)
    own = [own_small[2 * cut + x : 2 * cut + y] for x, y in zip(ends, ends[1:])]
    kinds = slot_items[:, None]
    valid = jnp.where((kinds == 0) | (jnp.arange(4)[None] < kinds), 1.0, 0.0)
    local = jnp.concatenate([jnp.sum(stats_.reshape(5, -1), axis=1), jnp.sum(valid)[None] * (PATCHES // 4 * WIDTH)])
    total = lax.psum(local, ("rep", "fsdp"))
    statistics = jnp.sqrt(total[:5] / total[5])
    return (
        c["out"].reshape(tokens.shape), c["igrad_out"].reshape(tokens.shape), own[0], own[1], own_iw, own[2], own_ow, own[3],
        own[4], own[5], own_we.astype(F32), own[7], own_wc.astype(F32), own[6], statistics,
    )


def specs():
    items = P(("rep", "fsdp"))
    big = P(("rep", "fsdp"), None, None)
    one, two = P("fsdp"), P("fsdp", None)
    ins = (big, big, items, one, one, two, one, two, one, one, one, two, one, two, one)
    outs = (big, big, one, one, two, one, two, one, one, one, two, one, two, one, P())
    return ins, outs


MESH = pl.DeviceIdType.MESH
AHEAD = 2
ANY = pl.BlockSpec(memory_space=pl.ANY)
FSDP = 8


def multiple(value, by):
    return pl.multiple_of(value * by, by)


class Place:
    def __init__(self, copies):
        self.z, self.f = lax.axis_index("rep"), lax.axis_index("fsdp")
        self.core, self.chip = self.f & 1, self.f >> 1
        self.copies = copies

    def peer(self, mask):
        return (self.z, self.f ^ mask)

    def floor(self, offset):
        return (lax.rem(self.z + offset, self.copies), self.f)


def remote(src, dst, send, recv, device):
    return pltpu.make_async_remote_copy(
        src_ref=src, dst_ref=dst, send_sem=send, recv_sem=recv, device_id=device, device_id_type=MESH
    )


class Sum:
    def __init__(self, place, R):
        self.p, self.R = place, R
        self.rows = R.sum_done.shape[1] // place.copies

    def copy(self, step, t, src, dst, device):
        return remote(src, dst, self.R.sum_send.at[step], self.R.sum_recv.at[step, t], device)

    def wait(self, step, t):
        view = (self.R.sum_core, self.R.sum_chips, self.R.sum_floors, self.R.sum_floors)[step].at[t]
        self.copy(step, t, view, view, self.p.peer(1)).wait_recv()

    def piece(self, floor):
        return pl.ds(multiple(floor, self.rows), self.rows)

    def offsets(self):
        return range(1, self.p.copies)

    def start(self, t):
        other = 1 - self.p.core
        self.copy(0, t, self.R.sum_own.at[t, :, other], self.R.sum_core.at[t], self.p.peer(1)).start()

    def to_chips(self, t):
        R = self.R
        self.wait(0, t)
        for k in (3, 1, 2, 0):
            at = self.p.chip ^ k
            mine = R.sum_own[t, at, self.p.core].astype(F32) + R.sum_core[t, at].astype(F32)
            R.sum_own[t, at, self.p.core] = mine.astype(BF16)
            if k:
                self.copy(1, t, R.sum_own.at[t, at, self.p.core], R.sum_chips.at[t, k - 1], self.p.peer(2 * k)).start()

    def to_floors(self, t):
        R = self.R
        self.wait(1, t)
        total = R.sum_own[t, self.p.chip, self.p.core].astype(F32)
        for k in (1, 2, 3):
            total = total + R.sum_chips[t, k - 1].astype(F32)
        R.sum_total[t] = total.astype(BF16)
        for d in self.offsets():
            device = self.p.floor(d)
            self.copy(2, t, R.sum_total.at[t, self.piece(device[0])], R.sum_floors.at[t, d - 1], device).start()

    def to_all(self, t):
        R = self.R
        self.wait(2, t)
        mine = self.piece(self.p.z)
        total = R.sum_total[t, mine, :].astype(F32)
        for d in self.offsets():
            total = total + R.sum_floors[t, d - 1].astype(F32)
        R.sum_done[t, mine, :] = total.astype(BF16)
        for d in self.offsets():
            self.copy(3, t, R.sum_done.at[t, mine], R.sum_done.at[t, mine], self.p.floor(d)).start()

    def finish(self, t):
        self.wait(3, t)

    def sent(self):
        R = self.R
        for step, view in enumerate((R.sum_core, R.sum_chips, R.sum_floors, R.sum_floors)):
            self.copy(step, 0, view, view, self.p.peer(1)).wait_send()


class Gather:
    def __init__(self, R, place):
        self.R, self.p = R, place

    def bring(self):
        R = self.R
        deep, tall = R.we_in.shape[0], R.wc_in.shape[0]
        for m in range(R.we_in.shape[1] // CHUNK):
            self.local(R.we_in.at[:, pl.ds(m * CHUNK, CHUNK)], R.hidden.at[pl.ds(m * deep, deep), :]).start()
        for t in range(R.w.shape[0]):
            self.local(R.wc_in.at[pl.ds(t * deep, deep), :], R.w.at[t, self.p.f, :, pl.ds(CHUNK, CHUNK)]).start()

    def local(self, src, dst):
        return pltpu.make_async_copy(src, dst, self.R.keep_sems.at[0])

    def lay(self):
        R = self.R
        deep, tall = R.we_in.shape[0], R.wc_in.shape[0]
        all_of = R.hidden.at[pl.ds(0, 2 * R.wc_in.shape[0]), :]
        self.local(all_of, all_of).wait()
        for t in range(0, R.w.shape[0], 2):
            for m in range(R.we_in.shape[1] // CHUNK):
                held = R.hidden[pl.ds(m * deep, deep), :].astype(F32)
                even, odd = [held[:, at + t * BS : at + t * BS + 128] for at in (0, tall)]
                for side, part in enumerate(interleave(even, odd)):
                    R.w[t + side, self.p.f, :, 128 * m : 128 * m + 128] = part.astype(BF16)

    def copy(self, t, mask, target):
        R = self.R
        view = R.w.at[t, self.p.f ^ mask]
        recv = R.gather_core if target == 1 else R.gather_chips
        return remote(view, view, R.gather_send.at[0], recv.at[t], self.p.peer(target))

    def wait(self, t, sems, count):
        view = self.R.w.at[t, pl.ds(0, count)]
        remote(view, view, self.R.gather_send.at[0], sems.at[t], self.p.peer(1)).wait_recv()

    def start(self, t):
        for target in (6, 2, 4, 1):
            self.copy(t, 0, target).start()

    def pass_on(self, t):
        self.wait(t, self.R.gather_chips, 3)
        for mask in (2, 4, 6):
            self.copy(t, mask, 1).start()

    def finish(self, t):
        self.wait(t, self.R.gather_core, 4)

    def sent(self):
        view = self.R.w.at[:, pl.ds(0, 7)]
        remote(view, view, self.R.gather_send.at[0], self.R.gather_core.at[0], self.p.peer(1)).wait_send()


def pack_small(R):
    R.small[pl.ds(0, BS), :] = R.inner_in[...]
    R.small[pl.ds(BS, BS), :] = R.outer_in[...]

    def row(*refs):
        return jnp.concatenate([ref[...].astype(F32) for ref in refs], axis=1)

    none = jnp.zeros((1, BS), F32)
    rows = [
        row(R.fg_in, R.fs_in), R.ib_in[...].astype(F32), R.ob_in[...].astype(F32), row(R.gg_in, R.gs_in),
        jnp.concatenate([R.cb_in[...].astype(F32), none], axis=1),
        R.eb_in[...].astype(F32), jnp.zeros((9, 128), F32),
    ]
    R.small[pl.ds(2 * BS, 16), :] = jnp.concatenate(rows, axis=0).astype(BF16)


def unpack_small(R):
    for j in range(PAIRS):
        cols = slice(128 * j, 128 * j + 128)
        even = R.smalls[2 * j, pl.ds(2 * BS, 16), :].astype(F32)
        odd = R.smalls[2 * j + 1, pl.ds(2 * BS, 16), :].astype(F32)
        first, second = interleave(even, odd)
        for row, (part, at) in enumerate(
            [(first, 0), (second, 0), (first, 1), (second, 1), (first, 2), (second, 2), (first, 3), (second, 3), (first, 4)]
        ):
            R.vec[row : row + 1, cols] = part[at : at + 1] * (1.0 / SHRINK if at == 2 else 1.0)
        for t in range(R.be.shape[1] // CHUNK):
            R.be[0:1, t * CHUNK + 128 * j : t * CHUNK + 128 * j + 128] = (first, second)[t % 2][5 + t // 2 : 6 + t // 2]
    complex_pairs(R.smalls.at[:, pl.ds(0, BS), :], R.win)
    complex_pairs(R.smalls.at[:, pl.ds(BS, BS), :], R.wout, R.wout_up)


def pack_sums(R):
    slots = R.tok.shape[0] // PATCHES

    def total(ref, at):
        return jnp.sum(ref[pl.ds(at, 8), :], axis=0, keepdims=True)

    feed_gain, feed_shift, contract, gain, shift = [total(R.sums, 8 * i) for i in range(5)]
    outer, inner, expand = total(R.dbias, 0), total(R.dbias, 8), total(R.dbe, 0)
    lane = lax.broadcasted_iota(jnp.int32, (1, 128), 1)
    facts = jnp.zeros((1, 128), F32)
    for i in range(5):
        facts = jnp.where(lane == i, jnp.sum(total(R.stats, 8 * i), axis=1, keepdims=True), facts)
    valid = jnp.zeros((1, 128), F32)
    for slot in range(slots):
        kind = kind_of(R, slot, 128)
        valid = valid + jnp.where(kind == 0, 4, kind).astype(F32) * float(PATCHES // 4 * WIDTH)
    facts = jnp.where(lane == 5, valid, facts)
    none = jnp.zeros((1, 128), F32)
    for j in range(PAIRS):
        cols = slice(128 * j, 128 * j + 128)
        real, imag = slice(256 * j, 256 * j + 128), slice(256 * j + 128, 256 * j + 256)
        rows = [
            interleave(gain[:, cols], shift[:, cols]),
            interleave(inner[:, real], inner[:, imag]),
            interleave(outer[:, real], outer[:, imag]),
            interleave(feed_gain[:, cols], feed_shift[:, cols]),
            interleave(contract[:, cols], none),
        ]
        for t in range(0, R.be.shape[1] // CHUNK, 2):
            low, high = [expand[:, (t + s) * CHUNK + 128 * j : (t + s) * CHUNK + 128 * j + 128] for s in range(2)]
            rows.append(interleave(low, high))
        for side in range(2):
            R.vec_own[2 * j + side] = jnp.concatenate([row[side] for row in rows] + [facts], axis=0)


class Share:
    def __init__(self, place, own, arrived, floors, sems):
        self.p, self.own, self.arrived, self.floors, self.sems = place, own, arrived, floors, sems

    def copy(self, step, src, dst, device):
        return remote(src, dst, self.sems.at[2 * step], self.sems.at[2 * step + 1], device)

    def views(self):
        return self.arrived, self.floors.at[pl.ds(0, self.p.copies - 1)]

    def wait(self, step):
        view = self.views()[step]
        self.copy(step, view, view, self.p.peer(1)).wait_recv()

    def start(self):
        for k in (6, 7, 2, 4, 3, 5, 1):
            self.copy(0, self.own.at[self.p.f ^ k], self.arrived.at[k - 1], self.p.peer(k)).start()

    def to_floors(self):
        self.wait(0)
        total = self.own[self.p.f].astype(F32)
        for k in range(1, FSDP):
            total = total + self.arrived[k - 1].astype(F32)
        self.floors[self.p.z] = total.astype(self.floors.dtype)
        mine = self.floors.at[self.p.z]
        for d in range(1, self.p.copies):
            self.copy(1, mine, mine, self.p.floor(d)).start()

    def finish(self):
        self.wait(1)
        total = self.floors[0].astype(F32)
        for z in range(1, self.p.copies):
            total = total + self.floors[z].astype(F32)
        return total

    def sent(self):
        for step, view in enumerate(self.views()):
            self.copy(step, view, view, self.p.peer(1)).wait_send()


def layer(copies, R):
    p = Place(copies)
    n = R.tok.shape[0]
    slots = n // PATCHES
    chunks = R.w.shape[0]
    blocks = n // CHUNK
    last = chunks - 1

    def loads(i):
        rows = pl.ds(multiple(i, CHUNK), CHUNK)
        return [
            pltpu.make_async_copy(src.at[rows, :], dst.at[rows, :], R.load_sems.at[i])
            for src, dst in ((R.tok_in, R.tok), (R.cot_in, R.msk))
        ]

    def loaded(i):
        both = R.tok.at[pl.ds(0, 2 * CHUNK), :]
        pltpu.make_async_copy(both, both, R.load_sems.at[i]).wait()

    stores = ((R.feed, R.out_ref), (R.fg, R.grad_ref))

    def store(which, i):
        rows = pl.ds(multiple(i, CHUNK), CHUNK)
        src, dst = stores[which]
        pltpu.make_async_copy(src.at[rows, :], dst.at[rows, :], R.store_sems.at[which]).start()

    gather = Gather(R, p)
    gather.bring()
    barrier = pltpu.get_barrier_semaphore()
    for k in range(1, FSDP):
        pl.semaphore_signal(barrier, inc=1, device_id=p.peer(k), device_id_type=MESH)
    for d in range(1, copies):
        pl.semaphore_signal(barrier, inc=1, device_id=p.floor(d), device_id_type=MESH)
    for i in range(blocks):
        for load in loads(i):
            load.start()
    R.stats[...] = jnp.zeros_like(R.stats)
    R.sums[...] = jnp.zeros_like(R.sums)
    R.dbias[...] = jnp.zeros_like(R.dbias)
    R.dbe[...] = jnp.zeros_like(R.dbe)
    R.dmix[...] = jnp.zeros_like(R.dmix)
    pack_small(R)
    R.smalls[p.f] = R.small[...]
    gather.lay()

    def begin(i):
        loaded(i)
        for side in range(CHUNK // PATCHES):
            mixer_start(R, i * (CHUNK // PATCHES) + side)

    pl.semaphore_wait(barrier, FSDP - 1 + copies - 1)

    def small_copy(dst, k):
        return remote(R.small, dst, R.small_sems.at[0], R.small_sems.at[1], p.peer(k))

    for k in (6, 7, 2, 4, 3, 5, 1):
        small_copy(R.smalls.at[p.f], k).start()
    gather.start(0)
    pl.loop(0, blocks)(begin)
    seven = R.smalls.at[pl.ds(0, FSDP - 1)]
    remote(seven, seven, R.small_sems.at[0], R.small_sems.at[1], p.peer(1)).wait_recv()
    unpack_small(R)
    sums = Sum(p, R)

    def weights(t):
        return [R.w[t, :, :, pl.ds(at, CHUNK)].reshape(-1, CHUNK) for at in (0, CHUNK)]

    def weight_gradients(t):
        for at, (left, right) in ((0, (R.feed, R.hgrad)), (CHUNK, (R.hidden, R.msk))):
            piece = dot(left[...], right[...], TN).astype(BF16)
            for k in range(FSDP):
                R.sum_own[t, k // 2, k % 2, :, at : at + CHUNK] = piece[k * BS : (k + 1) * BS]
        sums.start(t)

    def chunk_cols(t):
        return slice(t * CHUNK, (t + 1) * CHUNK)

    def two(step, i):
        return step(R, 2 * i), step(R, 2 * i + 1)

    @pl.loop(0, AHEAD)
    def _(i):
        run(*two(mixer_forward, i))

        @pl.when(i == AHEAD - 1)
        def _():
            gather.start(1)
            gather.pass_on(0)

    gather.finish(0)

    @pl.loop(AHEAD, blocks)
    def _(i):
        weave(chain(*two(mixer_forward, i)), 5, mlp_chunk(R, i - AHEAD, chunk_cols(0), *weights(0), first=True))

        @pl.when(i == blocks - 2)
        def _():
            gather.start(2)

    @pl.loop(blocks - AHEAD, blocks)
    def _(i):
        run(mlp_chunk(R, i, chunk_cols(0), *weights(0), first=True))

        @pl.when(i == blocks - AHEAD)
        def _():
            gather.start(3)
            gather.pass_on(1)

    weight_gradients(0)
    gather.finish(1)

    @pl.loop(1, last)
    def _(t):
        cols = pl.ds(multiple(t, CHUNK), CHUNK)

        @pl.loop(0, blocks)
        def _(i):
            @pl.when(i == 1)
            def _():
                sums.to_chips(t - 1)

            @pl.when((t > 1) & (i == 1))
            def _():
                sums.to_floors(t - 2)

            run(mlp_chunk(R, i, cols, *weights(t)))

            @pl.when(i == 2)
            def _():
                gather.pass_on(t + 1)

        weight_gradients(t)
        gather.finish(t + 1)

    @pl.loop(0, blocks)
    def _(i):
        @pl.when(i == 1)
        def _():
            sums.to_all(last - 3)
            sums.to_chips(last - 1)
            sums.to_floors(last - 2)

        run(mlp_front(R, i, chunk_cols(last), *weights(last)))

    weight_gradients(last)

    run(mlp_back(R, 0, *weights(last)))

    @pl.loop(1, blocks)
    def _(i):
        weave(turns(*two(mixer_backward_first, i - 1)), 4, mlp_back(R, i, *weights(last)))

        @pl.when(i == 1)
        def _():
            sums.to_chips(last)
            sums.to_floors(last - 1)
            sums.to_all(last - 2)

        @pl.when(i == blocks - 1)
        def _():
            sums.to_all(last - 1)

    run(*two(mixer_backward_first, blocks - 1))
    sums.to_floors(last)

    def put(which, j, value):
        for side in range(2):
            R.mix_own[2 * j + side, pl.ds(which * BS, BS), :] = value[side * BS : (side + 1) * BS].astype(BF16)

    mixer_weight_gradients(R, put)
    mixing = Share(p, R.mix_own, R.mix_peers, R.mix_floors, R.mix_sems)
    mixing.start()

    @pl.loop(0, blocks)
    def _(i):
        run(*two(block_result, i), *two(mixer_backward_second, i))
        store(0, i)

        @pl.when(i == 1)
        def _():
            sums.to_all(last)

    pack_sums(R)
    vectors = Share(p, R.vec_own, R.vec_peers, R.vec_floors, R.vec_sems)
    vectors.start()
    mixing.to_floors()

    @pl.loop(0, blocks)
    def _(i):
        run(*two(norm_backward, i))
        store(1, i)

    vectors.to_floors()
    for t in range(chunks):
        sums.finish(t)
    done_out = pltpu.make_async_copy(R.sum_done, R.done_ref, R.store_sems.at[2])
    done_out.start()
    R.mix_ref[...] = mixing.finish()
    R.vec_ref[...] = vectors.finish()
    remote(seven, seven, R.small_sems.at[0], R.small_sems.at[1], p.peer(1)).wait_send()
    gather.sent()
    sums.sent()
    mixing.sent()
    vectors.sent()
    for which, (src, dst) in enumerate(stores):
        pltpu.make_async_copy(src, dst, R.store_sems.at[which]).wait()
    done_out.wait()


def body_in_one(
    copies, tokens, cotangent, slot_items, filter_gain, filter_shift, inner_weight, inner_bias, outer_weight, outer_bias,
    feed_gain, feed_shift, expand_weight, expand_bias, contract_weight, contract_bias,
):
    slots = tokens.shape[0]
    n = slots * PATCHES
    deep, hidden = expand_weight.shape
    tall = contract_weight.shape[0]
    chunks = hidden // CHUNK
    floors = copies - 1
    ins = dict(
        items=slot_items, tok_in=tokens.reshape(n, WIDTH), cot_in=cotangent.reshape(n, WIDTH), table=jnp.asarray(TABLES, BF16),
        inner_in=inner_weight, outer_in=outer_weight, we_in=expand_weight, wc_in=contract_weight,
        fg_in=filter_gain[None], fs_in=filter_shift[None], ib_in=inner_bias[None], ob_in=outer_bias[None],
        gg_in=feed_gain[None], gs_in=feed_shift[None], cb_in=contract_bias[None], eb_in=expand_bias.reshape(2, 128),
    )
    places = dict.fromkeys(("tok_in", "cot_in", "we_in", "wc_in", "out_ref", "grad_ref", "done_ref"), ANY)
    places["items"] = SMEM
    outs = dict(
        out_ref=((n, WIDTH), BF16), grad_ref=((n, WIDTH), F32), done_ref=((chunks, deep, 2 * CHUNK), BF16),
        mix_ref=((2 * BS, 2 * BS), F32), vec_ref=((8, 128), F32),
    )
    wide, flat, full = ((n, 2 * WIDTH), BF16), ((n, WIDTH), BF16), ((n, WIDTH), F32)
    pairs, sums = ((2 * WIDTH, 4 * BS), BF16), ((40, WIDTH), F32)
    both = 2 * CHUNK
    memory = dict(
        tok=flat, msk=flat, spec=wide, act=wide, slope=wide, bent=wide, mid=full, feed=flat, br=full, fg=full,
        hidden=((n, CHUNK), BF16), hgrad=((n, CHUNK), BF16), w=((chunks, FSDP, deep, both), BF16),
        win=pairs, wout=pairs, wout_up=pairs, vec=((16, WIDTH), F32), be=((8, hidden), F32), stats=sums, sums=sums,
        dbias=((16, 2 * WIDTH), F32), dbe=((8, hidden), F32),
        dmix=((2, PAIRS, 256, 256), F32), small=((144, 128), BF16), smalls=((FSDP, 144, 128), BF16),
        sum_own=((chunks, 4, 2, deep, both), BF16), sum_core=((chunks, 4, deep, both), BF16),
        sum_chips=((chunks, 3, deep, both), BF16), sum_total=((chunks, deep, both), BF16),
        sum_floors=((chunks, floors, deep // copies, both), BF16), sum_done=((chunks, deep, both), BF16),
        mix_own=((FSDP, 128, 128), BF16), mix_peers=((FSDP - 1, 128, 128), BF16), mix_floors=((copies, 128, 128), BF16),
        vec_own=((FSDP, 8, 128), F32), vec_peers=((FSDP - 1, 8, 128), F32), vec_floors=((copies, 8, 128), F32),
    )
    sems = dict(
        load_sems=(n // CHUNK,), store_sems=(3,), keep_sems=(1,), small_sems=(2,), gather_send=(1,), gather_chips=(chunks,),
        gather_core=(chunks,), sum_send=(4,), sum_recv=(4, chunks), mix_sems=(4,), vec_sems=(4,),
    )
    names = list(ins) + list(outs) + list(memory) + list(sems)

    def kernel(*refs):
        R = named(names, refs)
        R.mgrad, R.out, R.igrad, R.cot = R.fg, R.feed, R.slope, R.msk
        R.ngrad, R.igrad_out = R.mid, R.fg
        layer(copies, R)

    o = dict(
        zip(
            outs,
            pl.pallas_call(
                kernel,
                out_shape=[jax.ShapeDtypeStruct(*spec) for spec in outs.values()],
                in_specs=[places.get(key, VMEM) for key in ins],
                out_specs=[places.get(key, VMEM) for key in outs],
                scratch_shapes=[pltpu.VMEM(*spec) for spec in memory.values()]
                + [pltpu.SemaphoreType.DMA(shape) for shape in sems.values()],
                compiler_params=pltpu.CompilerParams(vmem_limit_bytes=ROOM, collective_id=0, has_side_effects=True),
                name="mega",
            )(*ins.values()),
        )
    )
    return finishing(tokens.shape, o, deep, hidden, tall)


PIECES = 2


def finishing(shape, o, deep, hidden, tall):
    ends = dict(
        out=(o["out_ref"].shape, BF16), grad=(o["grad_ref"].shape, F32), fg=((1, BS), F32), fs=((1, BS), F32),
        inner=((BS, 2 * BS), F32), ib=((1, 128), F32), outer=((BS, 2 * BS), F32), ob=((1, 128), F32), gg=((1, BS), F32),
        gs=((1, BS), F32), ew=((deep, hidden), F32), eb=((2, 128), F32), cw=((tall, WIDTH), F32), cb=((1, BS), F32),
        stat=((1, 5), F32),
    )
    names = list(o) + list(ends) + ["grad_held", "out_held", "done_held", "mix_held", "vec_held", "ew_held", "cw_held", "come_sems", "go_sems", "done_sems"]

    def kernel(*refs):
        R = named(names, refs)
        def way(which, i):
            src, held, dst = ((R.grad_ref, R.grad_held, R.grad), (R.out_ref, R.out_held, R.out))[which]
            size = src.shape[0] // PIECES
            rows = pl.ds(i * size, size)
            come = pltpu.make_async_copy(src.at[rows], held.at[rows], R.come_sems.at[which, i])
            return come, pltpu.make_async_copy(held.at[rows], dst.at[rows], R.go_sems.at[which])

        smalls = [
            pltpu.make_async_copy(src, held, R.done_sems.at[i])
            for i, (src, held) in enumerate(((R.done_ref, R.done_held), (R.mix_ref, R.mix_held), (R.vec_ref, R.vec_held)))
        ]
        ways = [way(which, i) for i in range(PIECES) for which in range(2)]
        for small in smalls:
            small.start()
        for come, _ in ways:
            come.start()
        for small in smalls:
            small.wait()
        chunks, deep = R.done_ref.shape[:2]
        for t in range(0, chunks, 2):
            for m in range(CHUNK // 128):
                low, high = [R.done_held[t + side, :, 128 * m : 128 * m + 128].astype(F32) for side in range(2)]
                at = 2 * m * tall + t * BS
                for side, part in enumerate(interleave(low, high)):
                    R.ew_held[:, at + side * tall : at + side * tall + 128] = part
        for t in range(chunks):
            R.cw_held[pl.ds(t * deep, deep), :] = R.done_held[t, :, CHUNK:].astype(F32)
        ends = [
            pltpu.make_async_copy(R.ew_held, R.ew, R.done_sems.at[3]),
            pltpu.make_async_copy(R.cw_held, R.cw, R.done_sems.at[4]),
        ]
        for end in ends:
            end.start()
        R.inner[...], R.outer[...] = R.mix_held[:BS], R.mix_held[BS:]
        vec = R.vec_held[...]
        R.fg[...], R.fs[...] = vec[0:1, :BS], vec[0:1, BS:]
        R.ib[...], R.ob[...] = vec[1:2], vec[2:3]
        R.gg[...], R.gs[...] = vec[3:4, :BS], vec[3:4, BS:]
        R.cb[...], R.eb[...] = vec[4:5, :BS], vec[5:7]
        lane = lax.broadcasted_iota(jnp.int32, (1, 128), 1)
        total = jnp.sum(jnp.where(lane == 5, vec[7:8], 0.0), axis=1, keepdims=True)
        R.stat[...] = jnp.sqrt(vec[7:8] / total)[:, :5]
        for come, go in ways:
            come.wait()
            go.start()
        for which, (held, dst) in enumerate(((R.grad_held, R.grad), (R.out_held, R.out))):
            pltpu.make_async_copy(held, dst, R.go_sems.at[which]).wait()
        for end in ends:
            end.wait()

    places = dict.fromkeys(("out_ref", "grad_ref", "done_ref", "mix_ref", "vec_ref", "out", "grad", "ew", "cw"), ANY)
    values = pl.pallas_call(
        kernel,
        out_shape=[jax.ShapeDtypeStruct(*spec) for spec in ends.values()],
        in_specs=[places.get(key, VMEM) for key in o],
        out_specs=[places.get(key, VMEM) for key in ends],
        scratch_shapes=[
            pltpu.VMEM(o["grad_ref"].shape, F32), pltpu.VMEM(o["out_ref"].shape, BF16), pltpu.VMEM(o["done_ref"].shape, BF16),
            pltpu.VMEM(o["mix_ref"].shape, F32), pltpu.VMEM(o["vec_ref"].shape, F32),
            pltpu.VMEM((deep, hidden), F32), pltpu.VMEM((tall, WIDTH), F32), pltpu.SemaphoreType.DMA((2, PIECES)),
            pltpu.SemaphoreType.DMA((2,)), pltpu.SemaphoreType.DMA((5,)),
        ],
        compiler_params=pltpu.CompilerParams(vmem_limit_bytes=ROOM),
        name="finishing",
    )(*o.values())
    e = dict(zip(ends, values))
    for key in ("out", "grad"):
        e[key] = e[key].reshape(shape)
    for key in ("fg", "fs", "ib", "ob", "gg", "gs", "eb", "cb", "stat"):
        e[key] = e[key].reshape(-1)
    return tuple(e.values())


def solution(mesh):
    ins, outs = specs()
    whole = body_by_collectives
    if mesh.shape["fsdp"] == FSDP and mesh.shape["rep"] in (2, 4):
        whole = functools.partial(body_in_one, mesh.shape["rep"])
    return jax.shard_map(whole, mesh=mesh, in_specs=ins, out_specs=outs, check_vma=False)
```

time: 102 us -> 93.6 us (0.918)
  Pallas kernels: 101 us -> 92.6 us
    pallas_call x1, Pallas kernels: 93.5 us -> 86.2 us  [body_in_one(): pl.pallas_call(kernel, out_shape=[jax.ShapeDtypeStruct(*spec) for spec in...]
    pallas_call x1, Pallas kernels: 7.63 us -> 6.48 us  [finishing(): pl.pallas_call(kernel, out_shape=[jax.ShapeDtypeStruct(*spec) for spec in...]
where the time goes in v4:
time: 93.6 us; the launch traced here: 93.5 us
  Pallas kernels  92.6 us (99%)
    pallas_call x1, Pallas kernels, body_in_one(): pl.pallas_call(kernel, out_shape=[jax.ShapeDtypeStruct(*spec) for spec in...  86.2 us
    pallas_call x1, Pallas kernels, finishing(): pl.pallas_call(kernel, out_shape=[jax.ShapeDtypeStruct(*spec) for spec in...  6.48 us

profile of v4, /device:TPU:0, one launch (start us, length us, event | category | flops | bytes accessed | tf_op | source)
XLA Modules:
  0.0 93.5 jit_solution(5950388151973618953)
XLA Ops:
  0.7 86.2 %mega.1 = (bf16[2048,512]{1,0:T(8,128)(2,1)}, f32[2048,512]{1,0:T(8,128)}, bf16[4,64,1024]{2,1,0:T(8,128)(2,1)}, f32[128,128]{1,0:T(8,128)}, f32[8,128]{1,0:T(8,128)}) custom-call(s32[8]{0:T(128)} %refs_0_.1, bf16[2048,512]{1,0:T(8,128)(2,1)} %bitcast.21, bf16[2048,512]{1,0:T(8,128)(2,1)} %bitcast.22, bf16[512,256]{1,0:T(8,128)(2,1)} %constant.2.clone.refs_3_, ...), custom_call_target="tpu_custom_call" | custom-call | tf_op jit(solution)/shard_map/mega/pallas_call | solution.py:1099
  86.8 6.5 %finishing.1 = (bf16[2048,512]{1,0:T(8,128)(2,1)}, f32[2048,512]{1,0:T(8,128)}, f32[1,64]{1,0:T(1,128)}, f32[1,64]{1,0:T(1,128)}, f32[64,128]{1,0:T(8,128)}, /*i...) custom-call(bf16[2048,512]{1,0:T(8,128)(2,1)} %get-tuple-element.35., ...), custom_call_target="tpu_custom_call" | custom-call | tf_op jit(solution)/shard_map/finishing/pallas_call | solution.py:1179

commit v5 on v4

--- a/solution.py
+++ b/solution.py
@@ -177,7 +177,7 @@
 def complex_pairs(weight_ref, out_ref, up_ref=None):
     low = lax.broadcasted_iota(jnp.int32, (BS, 128), 1) < BS
     for j in range(PAIRS):
-        first, second = weight_ref[2 * j].astype(F32), weight_ref[2 * j + 1].astype(F32)
+        first, second = weight_ref[j, 0].astype(F32), weight_ref[j, 1].astype(F32)
         real = jnp.concatenate([jnp.where(low, first, 0.0), jnp.where(low, 0.0, pltpu.roll(second, BS, 1))], axis=0)
         imag = jnp.concatenate([jnp.where(low, pltpu.roll(first, BS, 1), 0.0), jnp.where(low, 0.0, second)], axis=0)
         matrix = jnp.concatenate(
@@ -335,14 +335,23 @@
         grad = grad * R.bent[rows, lanes].astype(F32)
         R.dbias[pl.ds(0, 8), lanes] += sum8(grad)
         grad = grad.astype(BF16)
-        R.dmix[1, j] += dot(R.act[rows, lanes], grad, TN)
+        R.ograd[rows, lanes] = grad
         yield True
         grad = dot(grad, R.wout[pl.ds(256 * j, 256), :], NT) * R.slope[rows, lanes].astype(F32)
         R.dbias[pl.ds(8, 8), lanes] += sum8(grad)
         grad = grad.astype(BF16)
         R.igrad[rows, lanes] = grad
-        R.dmix[0, j] += dot(R.spec[rows, lanes], grad, TN)
         yield True
+
+
+def mixer_products(R, i, first=False):
+    rows = pl.ds(pl.multiple_of(i * CHUNK, CHUNK), CHUNK)
+    for j in range(PAIRS):
+        lanes = slice(256 * j, 256 * j + 256)
+        for which, (left, right) in enumerate(((R.spec, R.igrad), (R.act, R.ograd))):
+            product = dot(left[rows, lanes], right[rows, lanes], TN)
+            R.dmix[which, j] = product if first else R.dmix[which, j] + product
+            yield True
 
 
 def block_result(R, slot):
@@ -465,6 +474,10 @@
     @pl.loop(0, slots)
     def _(slot):
         run(block_result(R, slot), mixer_backward_first(R, slot))
+
+    @pl.loop(0, slots * PATCHES // CHUNK)
+    def _(i):
+        run(mixer_products(R, i))
 
     def put_mix(which, j, value):
         (R.dinner, R.douter)[which][pl.ds(128 * j, 128), :] = value
@@ -508,7 +521,7 @@
     sums = ((40, WIDTH), F32)
     a = plain_call(
         forward_body,
-        dict(items=slot_items, tok=tok, cot=cot, table=table, vec=vec, inner=inner.reshape(NB, BS, 2 * BS), outer=outer.reshape(NB, BS, 2 * BS)),
+        dict(items=slot_items, tok=tok, cot=cot, table=table, vec=vec, inner=inner.reshape(PAIRS, 2, BS, 2 * BS), outer=outer.reshape(PAIRS, 2, BS, 2 * BS)),
         dict(spec=wide, act=wide, slope=wide, bent=wide, mid=full, feed=flat, msk=flat, win=pairs, wout=pairs, stats=sums, sums=sums),
         dict(wout_up=pairs),
         "mixer_forward",
@@ -530,7 +543,7 @@
             out=flat, igrad_out=full, dinner=((WIDTH, 2 * BS), F32), douter=((WIDTH, 2 * BS), F32),
             dbias=((16, 2 * WIDTH), F32), sums=sums, stats=sums,
         ),
-        dict(mgrad=full, igrad=wide, ngrad=full, dmix=((2, PAIRS, 256, 256), F32)),
+        dict(mgrad=full, ograd=wide, igrad=wide, ngrad=full, dmix=((2, PAIRS, 256, 256), F32)),
         "mixer_backward",
     )
 
@@ -638,8 +651,7 @@
         self.wait(0, t)
         for k in (3, 1, 2, 0):
             at = self.p.chip ^ k
-            mine = R.sum_own[t, at, self.p.core].astype(F32) + R.sum_core[t, at].astype(F32)
-            R.sum_own[t, at, self.p.core] = mine.astype(BF16)
+            R.sum_own[t, at, self.p.core] = R.sum_own[t, at, self.p.core] + R.sum_core[t, at]
             if k:
                 self.copy(1, t, R.sum_own.at[t, at, self.p.core], R.sum_chips.at[t, k - 1], self.p.peer(2 * k)).start()
 
@@ -684,7 +696,7 @@
         for m in range(R.we_in.shape[1] // CHUNK):
             self.local(R.we_in.at[:, pl.ds(m * CHUNK, CHUNK)], R.hidden.at[pl.ds(m * deep, deep), :]).start()
         for t in range(R.w.shape[0]):
-            self.local(R.wc_in.at[pl.ds(t * deep, deep), :], R.w.at[t, self.p.f, :, pl.ds(CHUNK, CHUNK)]).start()
+            self.local(R.wc_in.at[pl.ds(t * deep, deep), :], R.w.at[t, self.p.chip, self.p.core, :, pl.ds(CHUNK, CHUNK)]).start()
 
     def local(self, src, dst):
         return pltpu.make_async_copy(src, dst, self.R.keep_sems.at[0])
@@ -699,33 +711,52 @@
                 held = R.hidden[pl.ds(m * deep, deep), :].astype(F32)
                 even, odd = [held[:, at + t * BS : at + t * BS + 128] for at in (0, tall)]
                 for side, part in enumerate(interleave(even, odd)):
-                    R.w[t + side, self.p.f, :, 128 * m : 128 * m + 128] = part.astype(BF16)
-
-    def copy(self, t, mask, target):
-        R = self.R
-        view = R.w.at[t, self.p.f ^ mask]
-        recv = R.gather_core if target == 1 else R.gather_chips
-        return remote(view, view, R.gather_send.at[0], recv.at[t], self.p.peer(target))
-
-    def wait(self, t, sems, count):
-        view = self.R.w.at[t, pl.ds(0, count)]
-        remote(view, view, self.R.gather_send.at[0], sems.at[t], self.p.peer(1)).wait_recv()
+                    R.w[t + side, self.p.chip, self.p.core, :, 128 * m : 128 * m + 128] = part.astype(BF16)
 
     def start(self, t):
-        for target in (6, 2, 4, 1):
-            self.copy(t, 0, target).start()
+        R, p = self.R, self.p
+        view = R.w.at[t, p.chip, p.core]
+        for k in (1, 2, 3):
+            remote(view, view, R.gather_send.at[0], R.gather_chips.at[t], p.peer(2 * k)).start()
 
     def pass_on(self, t):
-        self.wait(t, self.R.gather_chips, 3)
-        for mask in (2, 4, 6):
-            self.copy(t, mask, 1).start()
+        R, p = self.R, self.p
+        three, view = R.w.at[t, pl.ds(0, 3), 0], R.w.at[t, :, p.core]
+        remote(three, three, R.gather_send.at[0], R.gather_chips.at[t], p.peer(1)).wait_recv()
+        remote(view, view, R.gather_send.at[1], R.gather_core.at[t], p.peer(1)).start()
 
     def finish(self, t):
-        self.wait(t, self.R.gather_core, 4)
+        R, p = self.R, self.p
+        view = R.w.at[t, :, 1 - p.core]
+        remote(view, view, R.gather_send.at[1], R.gather_core.at[t], p.peer(1)).wait_recv()
 
     def sent(self):
-        view = self.R.w.at[:, pl.ds(0, 7)]
-        remote(view, view, self.R.gather_send.at[0], self.R.gather_core.at[0], self.p.peer(1)).wait_send()
+        R, p = self.R, self.p
+        for at, view in enumerate((R.w.at[pl.ds(0, 3), :, 0], R.w.at[:, :, 0])):
+            remote(view, view, R.gather_send.at[at], R.gather_core.at[0], p.peer(1)).wait_send()
+
+
+class SmallGather:
+    def __init__(self, R, place):
+        self.R, self.p = R, place
+
+    def way(self, view, step, device):
+        return remote(view, view, self.R.small_sems.at[2 * step], self.R.small_sems.at[2 * step + 1], device)
+
+    def start(self):
+        for k in (1, 2, 3):
+            self.way(self.R.smalls.at[self.p.chip, self.p.core], 0, self.p.peer(2 * k)).start()
+
+    def pass_on(self):
+        self.way(self.R.smalls.at[pl.ds(0, 3), 0], 0, self.p.peer(1)).wait_recv()
+        self.way(self.R.smalls.at[:, self.p.core], 1, self.p.peer(1)).start()
+
+    def finish(self):
+        self.way(self.R.smalls.at[:, 1 - self.p.core], 1, self.p.peer(1)).wait_recv()
+
+    def sent(self):
+        self.way(self.R.smalls.at[pl.ds(0, 3), 0], 0, self.p.peer(1)).wait_send()
+        self.way(self.R.smalls.at[:, 0], 1, self.p.peer(1)).wait_send()
 
 
 def pack_small(R):
@@ -747,8 +778,8 @@
 def unpack_small(R):
     for j in range(PAIRS):
         cols = slice(128 * j, 128 * j + 128)
-        even = R.smalls[2 * j, pl.ds(2 * BS, 16), :].astype(F32)
-        odd = R.smalls[2 * j + 1, pl.ds(2 * BS, 16), :].astype(F32)
+        even = R.smalls[j, 0, pl.ds(2 * BS, 16), :].astype(F32)
+        odd = R.smalls[j, 1, pl.ds(2 * BS, 16), :].astype(F32)
         first, second = interleave(even, odd)
         for row, (part, at) in enumerate(
             [(first, 0), (second, 0), (first, 1), (second, 1), (first, 2), (second, 2), (first, 3), (second, 3), (first, 4)]
@@ -756,8 +787,8 @@
             R.vec[row : row + 1, cols] = part[at : at + 1] * (1.0 / SHRINK if at == 2 else 1.0)
         for t in range(R.be.shape[1] // CHUNK):
             R.be[0:1, t * CHUNK + 128 * j : t * CHUNK + 128 * j + 128] = (first, second)[t % 2][5 + t // 2 : 6 + t // 2]
-    complex_pairs(R.smalls.at[:, pl.ds(0, BS), :], R.win)
-    complex_pairs(R.smalls.at[:, pl.ds(BS, BS), :], R.wout, R.wout_up)
+    complex_pairs(R.smalls.at[:, :, pl.ds(0, BS), :], R.win)
+    complex_pairs(R.smalls.at[:, :, pl.ds(BS, BS), :], R.wout, R.wout_up)
 
 
 def pack_sums(R):
@@ -875,9 +906,8 @@
     R.sums[...] = jnp.zeros_like(R.sums)
     R.dbias[...] = jnp.zeros_like(R.dbias)
     R.dbe[...] = jnp.zeros_like(R.dbe)
-    R.dmix[...] = jnp.zeros_like(R.dmix)
     pack_small(R)
-    R.smalls[p.f] = R.small[...]
+    R.smalls[p.chip, p.core] = R.small[...]
     gather.lay()
 
     def begin(i):
@@ -887,20 +917,17 @@
 
     pl.semaphore_wait(barrier, FSDP - 1 + copies - 1)
 
-    def small_copy(dst, k):
-        return remote(R.small, dst, R.small_sems.at[0], R.small_sems.at[1], p.peer(k))
-
-    for k in (6, 7, 2, 4, 3, 5, 1):
-        small_copy(R.smalls.at[p.f], k).start()
+    small = SmallGather(R, p)
+    small.start()
     gather.start(0)
     pl.loop(0, blocks)(begin)
-    seven = R.smalls.at[pl.ds(0, FSDP - 1)]
-    remote(seven, seven, R.small_sems.at[0], R.small_sems.at[1], p.peer(1)).wait_recv()
+    small.pass_on()
+    small.finish()
     unpack_small(R)
     sums = Sum(p, R)
 
     def weights(t):
-        return [R.w[t, :, :, pl.ds(at, CHUNK)].reshape(-1, CHUNK) for at in (0, CHUNK)]
+        return [R.w[t, :, :, :, pl.ds(at, CHUNK)].reshape(-1, CHUNK) for at in (0, CHUNK)]
 
     def weight_gradients(t):
         for at, (left, right) in ((0, (R.feed, R.hgrad)), (CHUNK, (R.hidden, R.msk))):
@@ -981,24 +1008,24 @@
 
     weight_gradients(last)
 
+    def first_back(i, *beside):
+        weave(turns(*two(mixer_backward_first, i)), 1, turns(*beside))
+
     run(mlp_back(R, 0, *weights(last)))
-
-    @pl.loop(1, blocks)
+    first_back(0, mlp_back(R, 1, *weights(last)))
+    sums.to_chips(last)
+    sums.to_floors(last - 1)
+    sums.to_all(last - 2)
+    first_back(1, mlp_back(R, 2, *weights(last)), mixer_products(R, 0, first=True))
+
+    @pl.loop(3, blocks)
     def _(i):
-        weave(turns(*two(mixer_backward_first, i - 1)), 4, mlp_back(R, i, *weights(last)))
-
-        @pl.when(i == 1)
-        def _():
-            sums.to_chips(last)
-            sums.to_floors(last - 1)
-            sums.to_all(last - 2)
-
-        @pl.when(i == blocks - 1)
-        def _():
-            sums.to_all(last - 1)
-
-    run(*two(mixer_backward_first, blocks - 1))
+        first_back(i - 1, mlp_back(R, i, *weights(last)), mixer_products(R, i - 2))
+
+    sums.to_all(last - 1)
+    first_back(blocks - 1, mixer_products(R, blocks - 2))
     sums.to_floors(last)
+    run(mixer_products(R, blocks - 1))
 
     def put(which, j, value):
         for side in range(2):
@@ -1034,7 +1061,7 @@
     done_out.start()
     R.mix_ref[...] = mixing.finish()
     R.vec_ref[...] = vectors.finish()
-    remote(seven, seven, R.small_sems.at[0], R.small_sems.at[1], p.peer(1)).wait_send()
+    small.sent()
     gather.sent()
     sums.sent()
     mixing.sent()
@@ -1071,10 +1098,10 @@
     both = 2 * CHUNK
     memory = dict(
         tok=flat, msk=flat, spec=wide, act=wide, slope=wide, bent=wide, mid=full, feed=flat, br=full, fg=full,
-        hidden=((n, CHUNK), BF16), hgrad=((n, CHUNK), BF16), w=((chunks, FSDP, deep, both), BF16),
+        hidden=((n, CHUNK), BF16), hgrad=((n, CHUNK), BF16), w=((chunks, FSDP // 2, 2, deep, both), BF16),
         win=pairs, wout=pairs, wout_up=pairs, vec=((16, WIDTH), F32), be=((8, hidden), F32), stats=sums, sums=sums,
         dbias=((16, 2 * WIDTH), F32), dbe=((8, hidden), F32),
-        dmix=((2, PAIRS, 256, 256), F32), small=((144, 128), BF16), smalls=((FSDP, 144, 128), BF16),
+        dmix=((2, PAIRS, 256, 256), F32), small=((144, 128), BF16), smalls=((FSDP // 2, 2, 144, 128), BF16),
         sum_own=((chunks, 4, 2, deep, both), BF16), sum_core=((chunks, 4, deep, both), BF16),
         sum_chips=((chunks, 3, deep, both), BF16), sum_total=((chunks, deep, both), BF16),
         sum_floors=((chunks, floors, deep // copies, both), BF16), sum_done=((chunks, deep, both), BF16),
@@ -1082,14 +1109,14 @@
         vec_own=((FSDP, 8, 128), F32), vec_peers=((FSDP - 1, 8, 128), F32), vec_floors=((copies, 8, 128), F32),
     )
     sems = dict(
-        load_sems=(n // CHUNK,), store_sems=(3,), keep_sems=(1,), small_sems=(2,), gather_send=(1,), gather_chips=(chunks,),
+        load_sems=(n // CHUNK,), store_sems=(3,), keep_sems=(1,), small_sems=(4,), gather_send=(2,), gather_chips=(chunks,),
         gather_core=(chunks,), sum_send=(4,), sum_recv=(4, chunks), mix_sems=(4,), vec_sems=(4,),
     )
     names = list(ins) + list(outs) + list(memory) + list(sems)
 
     def kernel(*refs):
         R = named(names, refs)
-        R.mgrad, R.out, R.igrad, R.cot = R.fg, R.feed, R.slope, R.msk
+        R.mgrad, R.out, R.ograd, R.igrad, R.cot = R.fg, R.feed, R.bent, R.slope, R.msk
         R.ngrad, R.igrad_out = R.mid, R.fg
         layer(copies, R)
 

time: 93.6 us -> 90.8 us (0.970)
  Pallas kernels: 92.6 us -> 89.8 us
    pallas_call x1, Pallas kernels: 86.2 us -> 83.3 us  [body_in_one(): pl.pallas_call(kernel, out_shape=[jax.ShapeDtypeStruct(*spec) for spec in...]
where the time goes in v5:
time: 90.8 us; the launch traced here: 90.6 us
  Pallas kernels  89.8 us (99%)
    pallas_call x1, Pallas kernels, body_in_one(): pl.pallas_call(kernel, out_shape=[jax.ShapeDtypeStruct(*spec) for spec in...  83.3 us
    pallas_call x1, Pallas kernels, finishing(): pl.pallas_call(kernel, out_shape=[jax.ShapeDtypeStruct(*spec) for spec in...  6.48 us

profile of v5, /device:TPU:0, one launch (start us, length us, event | category | flops | bytes accessed | tf_op | source)
XLA Modules:
  0.0 90.6 jit_solution(10357467097893010646)
XLA Ops:
  0.7 83.3 %mega.1 = (bf16[2048,512]{1,0:T(8,128)(2,1)}, f32[2048,512]{1,0:T(8,128)}, bf16[4,64,1024]{2,1,0:T(8,128)(2,1)}, f32[128,128]{1,0:T(8,128)}, f32[8,128]{1,0:T(8,128)}) custom-call(s32[8]{0:T(128)} %refs_0_.1, bf16[2048,512]{1,0:T(8,128)(2,1)} %bitcast.21, bf16[2048,512]{1,0:T(8,128)(2,1)} %bitcast.22, bf16[512,256]{1,0:T(8,128)(2,1)} %constant.2.clone.refs_3_, ...), custom_call_target="tpu_custom_call" | custom-call | tf_op jit(solution)/shard_map/mega/pallas_call | solution.py:1126
  84.0 6.5 %finishing.1 = (bf16[2048,512]{1,0:T(8,128)(2,1)}, f32[2048,512]{1,0:T(8,128)}, f32[1,64]{1,0:T(1,128)}, f32[1,64]{1,0:T(1,128)}, f32[64,128]{1,0:T(8,128)}, /*i...) custom-call(bf16[2048,512]{1,0:T(8,128)(2,1)} %get-tuple-element.35., ...), custom_call_target="tpu_custom_call" | custom-call | tf_op jit(solution)/shard_map/finishing/pallas_call | solution.py:1206

commit v6 on v5

--- a/solution.py
+++ b/solution.py
@@ -983,7 +983,7 @@
             def _():
                 sums.to_chips(t - 1)
 
-            @pl.when((t > 1) & (i == 1))
+            @pl.when((t > 1) & (i == 3))
             def _():
                 sums.to_floors(t - 2)
 
@@ -1000,8 +1000,14 @@
     def _(i):
         @pl.when(i == 1)
         def _():
+            sums.to_chips(last - 1)
+
+        @pl.when(i == 2)
+        def _():
             sums.to_all(last - 3)
-            sums.to_chips(last - 1)
+
+        @pl.when(i == 3)
+        def _():
             sums.to_floors(last - 2)
 
         run(mlp_front(R, i, chunk_cols(last), *weights(last)))
@@ -1015,8 +1021,9 @@
     first_back(0, mlp_back(R, 1, *weights(last)))
     sums.to_chips(last)
     sums.to_floors(last - 1)
+    first_back(1, mlp_back(R, 2, *weights(last)), mixer_products(R, 0, first=True))
+
     sums.to_all(last - 2)
-    first_back(1, mlp_back(R, 2, *weights(last)), mixer_products(R, 0, first=True))
 
     @pl.loop(3, blocks)
     def _(i):
@@ -1138,7 +1145,7 @@
     return finishing(tokens.shape, o, deep, hidden, tall)
 
 
-PIECES = 2
+PIECES = 1
 
 
 def finishing(shape, o, deep, hidden, tall):

time: 90.8 us -> 89.7 us (0.988)
  Pallas kernels: 89.8 us -> 88.7 us
where the time goes in v6:
time: 89.7 us; the launch traced here: 89.5 us
  Pallas kernels  88.7 us (99%)
    pallas_call x1, Pallas kernels, body_in_one(): pl.pallas_call(kernel, out_shape=[jax.ShapeDtypeStruct(*spec) for spec in...  82.5 us
    pallas_call x1, Pallas kernels, finishing(): pl.pallas_call(kernel, out_shape=[jax.ShapeDtypeStruct(*spec) for spec in...  6.2 us

profile of v6, /device:TPU:0, one launch (start us, length us, event | category | flops | bytes accessed | tf_op | source)
XLA Modules:
  0.0 89.5 jit_solution(4480992613055421239)
XLA Ops:
  0.7 82.5 %mega.1 = (bf16[2048,512]{1,0:T(8,128)(2,1)}, f32[2048,512]{1,0:T(8,128)}, bf16[4,64,1024]{2,1,0:T(8,128)(2,1)}, f32[128,128]{1,0:T(8,128)}, f32[8,128]{1,0:T(8,128)}) custom-call(s32[8]{0:T(128)} %refs_0_.1, bf16[2048,512]{1,0:T(8,128)(2,1)} %bitcast.21, bf16[2048,512]{1,0:T(8,128)(2,1)} %bitcast.22, bf16[512,256]{1,0:T(8,128)(2,1)} %constant.2.clone.refs_3_, ...), custom_call_target="tpu_custom_call" | custom-call | tf_op jit(solution)/shard_map/mega/pallas_call | solution.py:1133
  83.1 6.2 %finishing.1 = (bf16[2048,512]{1,0:T(8,128)(2,1)}, f32[2048,512]{1,0:T(8,128)}, f32[1,64]{1,0:T(1,128)}, f32[1,64]{1,0:T(1,128)}, f32[64,128]{1,0:T(8,128)}, /*i...) custom-call(bf16[2048,512]{1,0:T(8,128)(2,1)} %get-tuple-element.35., ...), custom_call_target="tpu_custom_call" | custom-call | tf_op jit(solution)/shard_map/finishing/pallas_call | solution.py:1213

commit v7 on v6

--- a/solution.py
+++ b/solution.py
@@ -1047,7 +1047,7 @@
         run(*two(block_result, i), *two(mixer_backward_second, i))
         store(0, i)
 
-        @pl.when(i == 1)
+        @pl.when(i == 2)
         def _():
             sums.to_all(last)
 

time: 89.7 us -> 88.4 us (0.986)
  Pallas kernels: 88.7 us -> 87.4 us
    pallas_call x1, Pallas kernels: 82.5 us -> 81.2 us  [body_in_one(): pl.pallas_call(kernel, out_shape=[jax.ShapeDtypeStruct(*spec) for spec in...]
where the time goes in v7:
time: 88.4 us; the launch traced here: 88.2 us
  Pallas kernels  87.4 us (99%)
    pallas_call x1, Pallas kernels, body_in_one(): pl.pallas_call(kernel, out_shape=[jax.ShapeDtypeStruct(*spec) for spec in...  81.2 us
    pallas_call x1, Pallas kernels, finishing(): pl.pallas_call(kernel, out_shape=[jax.ShapeDtypeStruct(*spec) for spec in...  6.2 us

profile of v7, /device:TPU:0, one launch (start us, length us, event | category | flops | bytes accessed | tf_op | source)
XLA Modules:
  0.0 88.2 jit_solution(16144734442126202513)
XLA Ops:
  0.7 81.2 %mega.1 = (bf16[2048,512]{1,0:T(8,128)(2,1)}, f32[2048,512]{1,0:T(8,128)}, bf16[4,64,1024]{2,1,0:T(8,128)(2,1)}, f32[128,128]{1,0:T(8,128)}, f32[8,128]{1,0:T(8,128)}) custom-call(s32[8]{0:T(128)} %refs_0_.1, bf16[2048,512]{1,0:T(8,128)(2,1)} %bitcast.21, bf16[2048,512]{1,0:T(8,128)(2,1)} %bitcast.22, bf16[512,256]{1,0:T(8,128)(2,1)} %constant.2.clone.refs_3_, ...), custom_call_target="tpu_custom_call" | custom-call | tf_op jit(solution)/shard_map/mega/pallas_call | solution.py:1133
  81.9 6.2 %finishing.1 = (bf16[2048,512]{1,0:T(8,128)(2,1)}, f32[2048,512]{1,0:T(8,128)}, f32[1,64]{1,0:T(1,128)}, f32[1,64]{1,0:T(1,128)}, f32[64,128]{1,0:T(8,128)}, /*i...) custom-call(bf16[2048,512]{1,0:T(8,128)(2,1)} %get-tuple-element.35., ...), custom_call_target="tpu_custom_call" | custom-call | tf_op jit(solution)/shard_map/finishing/pallas_call | solution.py:1213
